TPU v7x, 128 devices: a whole 4x4x4 slice. The times are simulated.
128 devices in a mesh: section: 4 (over z), group: 2 (over core), row: 16 (over x, y).
Axes of the slice: x: 4, y: 4, z: 4, core: 2. Of those that a mesh axis runs over, the one named last changes fastest.
Arguments:
- token_ids: int32 [4, 32, 128], P(None, ('group', 'row')), may hold values from 0 to 31999
- segment_ids: int32 [4, 32, 128], P(None, ('group', 'row')), may hold values from 0 to 7, never falling along the last dimension, each value on 1 to 64 neighbouring positions
- noise_input: bfloat16 [4, 32, 128, 256], P(None, ('group', 'row'), None, 'section'), may hold values from -6 to 6
- embed_table: bfloat16 [32000, 256], P(None, 'section'), may hold values from -6 to 6
- input_proj: bfloat16 [256, 1024], P('section'), may hold values from -0.375 to 0.375
- norm_gain: bfloat16 [4, 1024], P('section'), may hold values from 0.5 to 1.5
- lead_weight: bfloat16 [4, 1024, 4096], P('section'), may hold values from -3 to 3
- down_weight: bfloat16 [4, 2048, 1024], P('section'), may hold values from -0.125 to 0.125
- final_gain: bfloat16 [1024], replicated, may hold values from 0.5 to 1.5
- readout_proj: bfloat16 [1024, 256], P(None, 'section'), may hold values from -0.1875 to 0.1875
- head_table: bfloat16 [32000, 256], P('section'), may hold values from -0.75 to 0.75
Outputs:
- noise_grad: float32 [4, 32, 128, 256], P(None, ('group', 'row'), None, 'section')
- embed_grad: float32 [32000, 256], P('row', 'section')
- input_proj_grad: float32 [256, 1024], P(('section', 'row'))
- norm_gain_grad: float32 [4, 1024], P('section', 'row')
- lead_grad: float32 [4, 1024, 4096], P('section', 'row')
- down_grad: float32 [4, 2048, 1024], P('section', 'row')
- final_gain_grad: float32 [1024], P(('section', 'row'))
- readout_grad: float32 [1024, 256], P('row', 'section')
- head_grad: float32 [32000, 256], P(('section', 'row'))
Inputs may be any that keep to these rules, and one draw needn't show every extreme that they name: `segment_ids`: along each packed row the numbers never fall; a segment holds at most 64 positions, and in each row some segment holds exactly that many.
All inputs are finite; a program needn't handle non-finite values.
Results may differ from a plain program's by a relative error of at most 0.04.
Values may be sent and summed in bfloat16 or wider, within the bound.
No kernel may reach another device: no remote copies, remote signals or barrier semaphores. Data moves between devices by JAX's collectives and lax.ppermute only.
A program may use at most 320 MiB of HBM per device.

v0:
```python
import jax
import jax.numpy as jnp
from jax import lax
from jax.sharding import PartitionSpec as P

HEADS = 16
HEAD_SIZE = 64
ROW_LEN = 128


EPSILON = 1e-05
MASKED = -1000000000.0


def shifted(shard, axis, by):
    size = lax.axis_size(axis)
    pairs = [(i, i + by) for i in range(size) if 0 <= i + by < size]
    return lax.ppermute(shard, axis, pairs)


def from_root(shard, axis, root):
    mine = lax.axis_index(axis) == root
    return lax.psum(jnp.where(mine, shard, jnp.zeros_like(shard)), axis)


def merged(value, axis, join):
    pieces = jax.tree.map(lambda part: lax.all_gather(part, axis), value)
    head = jax.tree.map(lambda part: part[0], pieces)
    tail = jax.tree.map(lambda part: part[1:], pieces)
    running, _ = lax.scan(lambda running, share: (join(running, share), None), head, tail)
    return running


def layer_norm(values):
    centre = jnp.mean(values, axis=-1, keepdims=True)
    centred = values - centre
    variance = jnp.mean(centred * centred, axis=-1, keepdims=True)
    factor = lax.rsqrt(variance + EPSILON)
    return (centred * factor, factor)


def norm_back(grad_normed, normed, factor):
    first_mean = jnp.mean(grad_normed, axis=-1, keepdims=True)
    second_mean = jnp.mean(grad_normed * normed, axis=-1, keepdims=True)
    return factor * (grad_normed - first_mean - normed * second_mean)


def matmul(former, latter):
    return jnp.dot(former, latter, preferred_element_type=jnp.float32)


def matmul_nt(former, latter):
    return lax.dot_general(
        former, latter, (((1,), (1,)), ((), ())), preferred_element_type=jnp.float32
    )


def matmul_tn(former, latter):
    return lax.dot_general(
        former, latter, (((0,), (0,)), ((), ())), preferred_element_type=jnp.float32
    )


def split_heads(packed, row_count):
    pieces_qkv = packed.reshape(row_count, ROW_LEN, 3, HEADS, HEAD_SIZE)
    return (pieces_qkv[:, :, 0], pieces_qkv[:, :, 1], pieces_qkv[:, :, 2])


def masked_scores(query_heads, key_heads, segments):
    raw_scores = jnp.einsum(
        "rqhd,rkhd->rhqk", query_heads, key_heads, preferred_element_type=jnp.float32
    ) * HEAD_SIZE ** (-0.5)
    same_segment = segments[:, None, :, None] == segments[:, None, None, :]
    return jnp.where(same_segment, raw_scores, MASKED)


def attend(packed, segments):
    row_count = segments.shape[0]
    query_heads, key_heads, value_heads = split_heads(packed, row_count)
    scores = masked_scores(query_heads, key_heads, segments)
    peak_value = jnp.max(scores, axis=-1, keepdims=True)
    expo_scores = jnp.exp(scores - peak_value)
    exp_total = jnp.sum(expo_scores, axis=-1, keepdims=True)
    attn_probs = (expo_scores / exp_total).astype(jnp.bfloat16)
    mixed_heads = jnp.einsum(
        "rhqk,rkhd->rqhd", attn_probs, value_heads, preferred_element_type=jnp.float32
    )
    logsum = (peak_value + jnp.log(exp_total))[..., 0]
    return (
        mixed_heads.reshape(row_count * ROW_LEN, HEADS * HEAD_SIZE).astype(jnp.bfloat16),
        logsum,
    )


def attend_back(packed, segments, logsum, grad_mixed):
    row_count = segments.shape[0]
    query_heads, key_heads, value_heads = split_heads(packed, row_count)
    attn_probs = jnp.exp(masked_scores(query_heads, key_heads, segments) - logsum[..., None])
    grad_heads = grad_mixed.reshape(row_count, ROW_LEN, HEADS, HEAD_SIZE)
    grad_value = jnp.einsum(
        "rhqk,rqhd->rkhd",
        attn_probs.astype(jnp.bfloat16),
        grad_heads,
        preferred_element_type=jnp.float32,
    )
    grad_probs = jnp.einsum(
        "rqhd,rkhd->rhqk", grad_heads, value_heads, preferred_element_type=jnp.float32
    )
    grad_scores = attn_probs * (
        grad_probs - jnp.sum(attn_probs * grad_probs, axis=-1, keepdims=True)
    )
    grad_low = grad_scores.astype(jnp.bfloat16)
    scale_factor = HEAD_SIZE ** (-0.5)
    grad_query = (
        jnp.einsum("rhqk,rkhd->rqhd", grad_low, key_heads, preferred_element_type=jnp.float32)
        * scale_factor
    )
    grad_key = (
        jnp.einsum("rhqk,rqhd->rkhd", grad_low, query_heads, preferred_element_type=jnp.float32)
        * scale_factor
    )
    joined = jnp.stack((grad_query, grad_key, grad_value), axis=2)
    return joined.reshape(row_count * ROW_LEN, 3 * HEADS * HEAD_SIZE).astype(jnp.bfloat16)


def attention_forward(entry_rows, segments, gain_half, lead):
    width = entry_rows.shape[1]
    residual = entry_rows.astype(jnp.float32)
    normed, factor = layer_norm(residual)
    packed = matmul((normed * gain_half).astype(jnp.bfloat16), lead[:, : 3 * width]).astype(
        jnp.bfloat16
    )
    mixed_heads, logsum = attend(packed, segments)
    result = residual + matmul(mixed_heads, lead[:, 3 * width :])
    return (result.astype(jnp.bfloat16), packed, mixed_heads, logsum)


def forward_mlp(entry_rows, gain_half, lead, full_down):
    residual = entry_rows.astype(jnp.float32)
    normed, factor = layer_norm(residual)
    inner_act = matmul((normed * gain_half).astype(jnp.bfloat16), lead)
    result = residual + matmul(jax.nn.gelu(inner_act).astype(jnp.bfloat16), full_down)
    return (result.astype(jnp.bfloat16), inner_act)


def attention_backward(entry_rows, packed, logsum, segments, gain_half, lead, grad_next):
    width = entry_rows.shape[1]
    normed, factor = layer_norm(entry_rows.astype(jnp.float32))
    grad_mixed = matmul_nt(grad_next, lead[:, 3 * width :]).astype(jnp.bfloat16)
    grad_packed = attend_back(packed, segments, logsum, grad_mixed)
    grad_normed = matmul_nt(grad_packed, lead[:, : 3 * width])
    grad_entry = grad_next.astype(jnp.float32) + norm_back(grad_normed * gain_half, normed, factor)
    gain_term = jnp.sum(grad_normed * normed, axis=0)
    return (
        grad_entry.astype(jnp.bfloat16),
        gain_term,
        (normed * gain_half).astype(jnp.bfloat16),
        grad_packed,
    )


def backward_mlp(entry_rows, inner_act, gain_half, lead, full_down, grad_next):
    normed, factor = layer_norm(entry_rows.astype(jnp.float32))
    active, gelu_back = jax.vjp(jax.nn.gelu, inner_act)
    grad_inner = gelu_back(matmul_nt(grad_next, full_down))[0].astype(jnp.bfloat16)
    grad_normed = matmul_nt(grad_inner, lead)
    grad_entry = grad_next.astype(jnp.float32) + norm_back(grad_normed * gain_half, normed, factor)
    gain_term = jnp.sum(grad_normed * normed, axis=0)
    return (
        grad_entry.astype(jnp.bfloat16),
        gain_term,
        (normed * gain_half).astype(jnp.bfloat16),
        active.astype(jnp.bfloat16),
        grad_inner,
    )


def merge_softmax(former, latter):
    peak_value = jnp.maximum(former[0], latter[0])
    return (
        peak_value,
        former[1] * jnp.exp(former[0] - peak_value) + latter[1] * jnp.exp(latter[0] - peak_value),
    )


def place_slot(buffer, fresh_rows, slot_at):
    return lax.dynamic_update_index_in_dim(buffer, fresh_rows, slot_at, 0)


def local(
    token_ids,
    segment_ids,
    noise_input,
    embed_table,
    input_proj,
    norm_gain,
    lead_weight,
    down_weight,
    final_gain,
    readout_proj,
    head_table,
):
    section_index = lax.axis_index("section")
    section_count = lax.axis_size("section")
    micro_count, rows_dev, row_length = token_ids.shape
    tokens = rows_dev * row_length
    width = input_proj.shape[1]
    hidden_units = lead_weight.shape[2]
    half_rows = down_weight.shape[1]
    emb_part = input_proj.shape[0]
    vocab_part = head_table.shape[0]
    is_attention = section_index % 2 == 0
    gain_half = norm_gain[0].astype(jnp.float32)
    lead = lead_weight[0]
    upper_rows = shifted(down_weight[0], "section", 1)
    full_down = jnp.concatenate((upper_rows, down_weight[0]), axis=0)
    flat_ids = token_ids.reshape(-1)
    embedded = embed_table[flat_ids].astype(jnp.float32) + noise_input.reshape(-1, emb_part).astype(
        jnp.float32
    )
    embedded_low = embedded.astype(jnp.bfloat16)
    lifted = lax.psum(matmul(embedded_low, input_proj).astype(jnp.bfloat16), "section")
    first_layer = lifted.reshape(micro_count, tokens, width)
    stored = (
        jnp.zeros((micro_count, tokens, width), jnp.bfloat16),
        jnp.zeros((micro_count, tokens, 3 * width), jnp.bfloat16),
        jnp.zeros((micro_count, tokens, width), jnp.bfloat16),
        jnp.zeros((micro_count, rows_dev, HEADS, row_length), jnp.float32),
        jnp.zeros((micro_count, tokens, hidden_units), jnp.float32),
    )
    outbox = jnp.zeros((tokens, width), jnp.bfloat16)
    finals = jnp.zeros((micro_count, tokens, width), jnp.bfloat16)
    for step_now in range(micro_count + section_count - 1):
        if step_now > 0:
            inbound = shifted(outbox, "section", 1)
        else:
            inbound = outbox
        position = step_now - section_index
        is_live = jnp.logical_and(position >= 0, position < micro_count)
        slot_at = jnp.clip(position, 0, micro_count - 1)
        entry_rows = jnp.where(section_index == 0, first_layer[slot_at], inbound)
        row_segments = segment_ids[slot_at]

        def forward_run(buffers):

            def forward_attention_case(buffers):
                result, packed, mixed_heads, logsum = attention_forward(
                    entry_rows, row_segments, gain_half, lead
                )
                entries, packs, mixes, logsums, inners = buffers
                return (
                    result,
                    (
                        place_slot(entries, entry_rows, slot_at),
                        place_slot(packs, packed, slot_at),
                        place_slot(mixes, mixed_heads, slot_at),
                        place_slot(logsums, logsum, slot_at),
                        inners,
                    ),
                )

            def forward_mlp_case(buffers):
                result, inner_act = forward_mlp(entry_rows, gain_half, lead, full_down)
                entries, packs, mixes, logsums, inners = buffers
                return (
                    result,
                    (
                        place_slot(entries, entry_rows, slot_at),
                        packs,
                        mixes,
                        logsums,
                        place_slot(inners, inner_act, slot_at),
                    ),
                )

            return lax.cond(is_attention, forward_attention_case, forward_mlp_case, buffers)

        def forward_skip(buffers):
            return (jnp.zeros((tokens, width), jnp.bfloat16), buffers)

        outbox, stored = lax.cond(is_live, forward_run, forward_skip, stored)
        last_live = jnp.logical_and(is_live, section_index == section_count - 1)
        finals = lax.dynamic_update_index_in_dim(
            finals, jnp.where(last_live, outbox, finals[slot_at]), slot_at, 0
        )
    gathered = from_root(finals, "section", section_count - 1)
    last_rows = gathered.reshape(-1, width).astype(jnp.float32)
    normed_f, factor_f = layer_norm(last_rows)
    gain_f = final_gain.astype(jnp.float32)
    final_low = (normed_f * gain_f).astype(jnp.bfloat16)
    readout_part = matmul(final_low, readout_proj).astype(jnp.bfloat16)
    readout = lax.all_gather(readout_part, "section", axis=1, tiled=True)
    logits = matmul_nt(readout, head_table)
    peak_value = jnp.max(logits, axis=1)
    exp_total = jnp.sum(jnp.exp(logits - peak_value[:, None]), axis=1)
    peak_value, exp_total = merged((peak_value, exp_total), "section", merge_softmax)
    logsum = peak_value + jnp.log(exp_total)
    columns = lax.broadcasted_iota(jnp.int32, (1, vocab_part), 1) + section_index * vocab_part
    target_hits = (columns == flat_ids[:, None]).astype(jnp.float32)
    grad_logits = (jnp.exp(logits - logsum[:, None]) - target_hits).astype(jnp.bfloat16)
    head_grad = matmul_tn(grad_logits, readout)
    grad_readout = lax.psum_scatter(
        matmul(grad_logits, head_table).astype(jnp.bfloat16),
        "section",
        scatter_dimension=1,
        tiled=True,
    )
    readout_grad = matmul_tn(final_low, grad_readout)
    grad_final = lax.psum(
        matmul_nt(grad_readout, readout_proj).astype(jnp.bfloat16), "section"
    ).astype(jnp.float32)
    final_gain_full = jnp.sum(grad_final * normed_f, axis=0)
    last_grads = (
        norm_back(grad_final * gain_f, normed_f, factor_f)
        .astype(jnp.bfloat16)
        .reshape(micro_count, tokens, width)
    )
    zero_gain = jnp.zeros((width,), jnp.float32)
    running = (
        zero_gain,
        jnp.zeros((width, hidden_units), jnp.float32),
        jnp.zeros((hidden_units, width), jnp.float32),
    )
    sendbox = jnp.zeros((tokens, width), jnp.bfloat16)
    first_grads = jnp.zeros((micro_count, tokens, width), jnp.bfloat16)
    for step_now in range(micro_count + section_count - 1):
        if step_now > 0:
            inbound = shifted(sendbox, "section", -1)
        else:
            inbound = sendbox
        position = step_now - (section_count - 1 - section_index)
        is_live = jnp.logical_and(position >= 0, position < micro_count)
        slot_at = jnp.clip(position, 0, micro_count - 1)
        grad_next = jnp.where(section_index == section_count - 1, last_grads[slot_at], inbound)
        row_segments = segment_ids[slot_at]

        def backward_run(totals):
            entries, packs, mixes, logsums, inners = stored
            entry_rows = entries[slot_at]

            def backward_attention_case(totals):
                mixed_now = mixes[slot_at]
                grad_entry, gain_term, normed_low, grad_packed = attention_backward(
                    entry_rows,
                    packs[slot_at],
                    logsums[slot_at],
                    row_segments,
                    gain_half,
                    lead,
                    grad_next,
                )
                lead_term = jnp.concatenate(
                    (matmul_tn(normed_low, grad_packed), matmul_tn(mixed_now, grad_next)), axis=1
                )
                updated = (totals[0] + gain_term, totals[1] + lead_term, totals[2])
                return (grad_entry, updated)

            def backward_mlp_case(totals):
                grad_entry, gain_term, normed_low, active_low, grad_inner = backward_mlp(
                    entry_rows, inners[slot_at], gain_half, lead, full_down, grad_next
                )
                updated = (
                    totals[0] + gain_term,
                    totals[1] + matmul_tn(normed_low, grad_inner),
                    totals[2] + matmul_tn(active_low, grad_next),
                )
                return (grad_entry, updated)

            return lax.cond(is_attention, backward_attention_case, backward_mlp_case, totals)

        def backward_skip(totals):
            return (jnp.zeros((tokens, width), jnp.bfloat16), totals)

        sendbox, running = lax.cond(is_live, backward_run, backward_skip, running)
        top_live = jnp.logical_and(is_live, section_index == 0)
        first_grads = lax.dynamic_update_index_in_dim(
            first_grads, jnp.where(top_live, sendbox, first_grads[slot_at]), slot_at, 0
        )
    gain_acc = running[0]
    lead_acc, down_acc = (running[1], running[2])
    spread_grads = from_root(first_grads, "section", 0).reshape(-1, width)
    input_grad = matmul_tn(embedded_low, spread_grads)
    noise_grad = matmul_nt(spread_grads, input_proj)
    embed_grad = jax.ops.segment_sum(noise_grad, flat_ids, num_segments=embed_table.shape[0])
    quarter_width = width // section_count
    final_part = lax.dynamic_slice_in_dim(
        final_gain_full, section_index * quarter_width, quarter_width
    )
    pieces = (
        lead_acc,
        down_acc[:half_rows],
        down_acc[half_rows:],
        gain_acc,
        final_part,
        head_grad,
        embed_grad,
        input_grad,
        readout_grad,
    )
    shards = (
        lax.psum_scatter(
            pieces[0].astype(jnp.bfloat16), "row", scatter_dimension=0, tiled=True
        ).astype(jnp.float32),
        lax.psum_scatter(
            pieces[1].astype(jnp.bfloat16), "row", scatter_dimension=0, tiled=True
        ).astype(jnp.float32),
        lax.psum_scatter(
            pieces[2].astype(jnp.bfloat16), "row", scatter_dimension=0, tiled=True
        ).astype(jnp.float32),
        lax.psum_scatter(
            pieces[3].astype(jnp.bfloat16), "row", scatter_dimension=0, tiled=True
        ).astype(jnp.float32),
        lax.psum_scatter(
            pieces[4].astype(jnp.bfloat16), "row", scatter_dimension=0, tiled=True
        ).astype(jnp.float32),
        lax.psum_scatter(
            pieces[5].astype(jnp.bfloat16), "row", scatter_dimension=0, tiled=True
        ).astype(jnp.float32),
        lax.psum_scatter(
            pieces[6].astype(jnp.bfloat16), "row", scatter_dimension=0, tiled=True
        ).astype(jnp.float32),
        lax.psum_scatter(
            pieces[7].astype(jnp.bfloat16), "row", scatter_dimension=0, tiled=True
        ).astype(jnp.float32),
        lax.psum_scatter(
            pieces[8].astype(jnp.bfloat16), "row", scatter_dimension=0, tiled=True
        ).astype(jnp.float32),
    )
    shards = (
        lax.psum(shards[0].astype(jnp.bfloat16), "group").astype(jnp.float32),
        lax.psum(shards[1].astype(jnp.bfloat16), "group").astype(jnp.float32),
        lax.psum(shards[2].astype(jnp.bfloat16), "group").astype(jnp.float32),
        lax.psum(shards[3].astype(jnp.bfloat16), "group").astype(jnp.float32),
        lax.psum(shards[4].astype(jnp.bfloat16), "group").astype(jnp.float32),
        lax.psum(shards[5].astype(jnp.bfloat16), "group").astype(jnp.float32),
        lax.psum(shards[6].astype(jnp.bfloat16), "group").astype(jnp.float32),
        lax.psum(shards[7].astype(jnp.bfloat16), "group").astype(jnp.float32),
        lax.psum(shards[8].astype(jnp.bfloat16), "group").astype(jnp.float32),
    )
    (
        lead_shard,
        upper_shard,
        lower_shard,
        gain_shard,
        final_shard,
        head_shard,
        embed_shard,
        input_shard,
        readout_shard,
    ) = shards
    upper_from_next = shifted(upper_shard.astype(jnp.bfloat16), "section", -1).astype(
        upper_shard.dtype
    )
    down_shard = jnp.where(is_attention, upper_from_next, lower_shard)
    return (
        noise_grad.reshape(noise_input.shape),
        embed_shard,
        input_shard,
        gain_shard[None],
        lead_shard[None],
        down_shard[None],
        final_shard,
        readout_shard,
        head_shard,
    )


def solution(mesh):
    in_specs = (
        P(None, ("group", "row"), None),
        P(None, ("group", "row"), None),
        P(None, ("group", "row"), None, "section"),
        P(None, "section"),
        P("section", None),
        P("section", None),
        P("section", None, None),
        P("section", None, None),
        P(),
        P(None, "section"),
        P("section", None),
    )
    out_specs = (
        P(None, ("group", "row"), None, "section"),
        P("row", "section"),
        P(("section", "row"), None),
        P("section", "row"),
        P("section", "row", None),
        P("section", "row", None),
        P(("section", "row")),
        P("row", "section"),
        P(("section", "row"), None),
    )
    return jax.shard_map(local, mesh=mesh, in_specs=in_specs, out_specs=out_specs, check_vma=False)
```

profile of v0, /device:TPU:103, one launch (start us, length us, event | category | flops | bytes accessed | tf_op | source)
XLA Modules:
  0.0 1439.6 jit_solution(16257098018389726740)
XLA Ops:
  24.9 92.8 %collective-permute-done = bf16[2048,1024]{1,0:T(8,128)(2,1)} collective-permute-done((bf16[2048,1024]{1,0:T(8,128)(2,1)}, bf16[2048,1024]{1,0:T(8,128)(2,1)}, u32[]{:S(2)}, u32[]{:S(2)}) %collective-permute-start) | collective-permute-done | bytes 4194336 | tf_op jit(solution)/shard_map/ppermute | solution.py:18
  126.2 17.3 %conditional.166 = (bf16[128,1024]{1,0:T(8,128)(2,1)}, bf16[4,128,1024]{2,1,0:T(8,128)(2,1)}, bf16[4,128,3072]{2,1,0:T(8,128)(2,1)}, bf16[4,128,1024]{2,1,0:T(8,...) conditional(s32[]{:T(128)} %convert_element_type.1372, () %tuple.543, (pred[]{:T(512)}, ...), branch_computations={%region_1.2_spmd, %region_2.11_spmd} | conditional | flops 2154168320 | bytes 98214712 | solution.py:281
  173.1 19.3 %collective-permute-done.3 = bf16[128,1024]{1,0:T(8,128)(2,1)S(1)} collective-permute-done((bf16[128,1024]{1,0:T(8,128)(2,1)}, bf16[128,1024]{1,0:T(8,128)(2,1)S(1)}, u32[]{:S(2)}, u32[]{:S(2)}) %collective-permute-start.3) | collective-permute-done | bytes 262176 | tf_op jit(solution)/shard_map/ppermute | solution.py:18
  205.4 12.2 collective-permute-done.4
  257.1 11.1 conditional.179
  270.5 51.6 %all-reduce.18.cloned.1.call-done = bf16[4,128,1024]{2,1,0:T(8,128)(2,1)} async-done(((bf16[4,128,1024]{2,1,0:T(8,128)(2,1)}), bf16[4,128,1024]{2,1,0:T(8,128)(2,1)}) %all-reduce.18.cloned.1.call-update) | async-done | bytes 1048592 | tf_op jit(solution)/shard_map/psum | solution.py:23
  383.1 28.6 %reduce-scatter.11.cloned.1.call-done = bf16[512,64]{0,1:T(8,128)(2,1)} async-done(((bf16[512,256]{0,1:T(8,128)(2,1)}), bf16[512,64]{0,1:T(8,128)(2,1)}) %reduce-scatter.11.cloned.1.call-update) | async-done | bytes 65552 | tf_op jit(solution)/shard_map/reduce_scatter | solution.py:302
  414.1 47.4 %all-reduce.20.cloned.1.call-done = bf16[512,1024]{1,0:T(8,128)(2,1)} async-done(((bf16[512,1024]{1,0:T(8,128)(2,1)}), bf16[512,1024]{1,0:T(8,128)(2,1)}) %all-reduce.20.cloned.1.call-update) | async-done | bytes 1048592 | tf_op jit(solution)/shard_map/psum | solution.py:309
  466.4 32.1 %conditional.180 = (bf16[128,1024]{1,0:T(8,128)(2,1)}, f32[1024]{0:T(1024)}, f32[1024,4096]{1,0:T(8,128)}, f32[4096,1024]{1,0:T(8,128)}) conditional(s32[]{:T(128)} %convert_element_type.1365, () %tuple.542, (pred[]{:T(512)}, s32[]{:T(128)}, bf16[4,128,1024]{2,1,0:T(8,128)(2,1)}, bf16[4,128,1024]{2,1,0:T(8,128)(2,1)S(1)}, ...), branch_computations={%region_82.83_spmd, %region_83.97_spmd} | conditional | flops 4314364928 | bytes 105091360 | solution.py:374
  467.6 30.5 %conditional.195 = (f32[1024]{0:T(1024)}, f32[1024,4096]{1,0:T(8,128)}, f32[4096,1024]{1,0:T(8,128)}, bf16[128,1024]{1,0:T(8,128)(2,1)}) conditional(s32[]{:T(128)} %convert_element_type.1222, (bf16[128,1024]{1,0:T(8,128)(2,1)S(1)}, bf16[4096,1024]{1,0:T(8,128)(2,1)}, s32[]{:T(128)}, f32[4,128,4096]{2,1,0:T(8,128)}, bf16[1024,4096]{1,0:T(8,128)(2,1)}, ...), branch_computations={%region_84.89_spmd, %region_90.96_spmd} | conditional | flops 4314233856 | bytes 103649360
  504.3 50.8 %conditional.181 = (bf16[128,1024]{1,0:T(8,128)(2,1)}, f32[1024]{0:T(1024)}, f32[1024,4096]{1,0:T(8,128)}, f32[4096,1024]{1,0:T(8,128)}) conditional(s32[]{:T(128)} %convert_element_type.1392, (f32[1024]{0:T(1024)}, f32[1024,4096]{1,0:T(8,128)}, f32[4096,1024]{1,0:T(8,128)}) %tuple.559, (pred[]{:T(512)}, s32[]{:T(128)}, ...), branch_computations={%region_97.98_spmd, %region_98.112_spmd} | conditional | flops 4322754560 | bytes 121948584 | solution.py:374
  505.3 42.2 %conditional.196 = (f32[1024]{0:T(1024)}, f32[1024,4096]{1,0:T(8,128)}, f32[4096,1024]{1,0:T(8,128)}, bf16[128,1024]{1,0:T(8,128)(2,1)}) conditional(s32[]{:T(128)} %convert_element_type.1237, (bf16[128,1024]{1,0:T(8,128)(2,1)S(1)}, bf16[4096,1024]{1,0:T(8,128)(2,1)}, s32[]{:T(128)}, f32[4,128,4096]{2,1,0:T(8,128)}, ...), branch_computations={%region_99.104_spmd, %region_105.111_spmd} | conditional | flops 4322623488 | bytes 120506536
  513.4 14.7 %convolution_add_fusion.7 = f32[4096,1024]{1,0:T(8,128)} fusion(f32[4096,1024]{1,0:T(8,128)} %get-tuple-element.3987, bf16[128,1024]{1,0:T(8,128)(2,1)S(1)} %get-tuple-element.3979, f32[4,128,4096]{2,1,0:T(8,128)} %get-tuple-element.3981, s32[]{:T(128)S(6)} %select_n.529), kind=kOutput, calls=%fused_computation.588 | convolution fusion | flops 1082654720 | bytes 35913732 | tf_op jit(solution)/shard_map/cond/branch_1_fun/cond/branch_0_fun/dot_general | solution.py:59
  528.1 14.0 convolution_add_fusion.8
  560.2 50.9 %conditional.182 = (bf16[128,1024]{1,0:T(8,128)(2,1)}, f32[1024]{0:T(1024)}, f32[1024,4096]{1,0:T(8,128)}, f32[4096,1024]{1,0:T(8,128)}) conditional(s32[]{:T(128)} %convert_element_type.1393, (f32[1024]{0:T(1024)}, f32[1024,4096]{1,0:T(8,128)}, f32[4096,1024]{1,0:T(8,128)}) %tuple.561, (pred[]{:T(512)}, s32[]{:T(128)}, ...), branch_computations={%region_112.113_spmd, %region_113.127_spmd} | conditional | flops 4322754560 | bytes 121948584 | solution.py:374
  561.2 42.4 %conditional.197 = (f32[1024]{0:T(1024)}, f32[1024,4096]{1,0:T(8,128)}, f32[4096,1024]{1,0:T(8,128)}, bf16[128,1024]{1,0:T(8,128)(2,1)}) conditional(s32[]{:T(128)} %convert_element_type.1252, (bf16[128,1024]{1,0:T(8,128)(2,1)S(1)}, bf16[4096,1024]{1,0:T(8,128)(2,1)}, s32[]{:T(128)}, f32[4,128,4096]{2,1,0:T(8,128)}, ...), branch_computations={%region_114.119_spmd, %region_120.126_spmd} | conditional | flops 4322623488 | bytes 120506536
  569.3 14.7 %convolution_add_fusion.9 = f32[4096,1024]{1,0:T(8,128)} fusion(f32[4096,1024]{1,0:T(8,128)} %get-tuple-element.4033, bf16[128,1024]{1,0:T(8,128)(2,1)S(1)} %get-tuple-element.4025, f32[4,128,4096]{2,1,0:T(8,128)} %get-tuple-element.4027, s32[]{:T(128)S(6)} %select_n.534), kind=kOutput, calls=%fused_computation.699 | convolution fusion | flops 1082654720 | bytes 35913732 | tf_op jit(solution)/shard_map/cond/branch_1_fun/cond/branch_0_fun/dot_general | solution.py:59
  584.0 14.0 convolution_add_fusion.10
  616.0 43.2 %conditional.183 = (bf16[128,1024]{1,0:T(8,128)(2,1)}, f32[1024]{0:T(1024)}, f32[1024,4096]{1,0:T(8,128)}, f32[4096,1024]{1,0:T(8,128)}) conditional(s32[]{:T(128)} %convert_element_type.1394, (f32[1024]{0:T(1024)}, f32[1024,4096]{1,0:T(8,128)}, f32[4096,1024]{1,0:T(8,128)}) %tuple.563, (pred[]{:T(512)}, s32[]{:T(128)}, ...), branch_computations={%region_127.128_spmd, %region_128.142_spmd} | conditional | flops 4322754560 | bytes 121948584 | solution.py:374
  617.0 42.2 %conditional.198 = (f32[1024]{0:T(1024)}, f32[1024,4096]{1,0:T(8,128)}, f32[4096,1024]{1,0:T(8,128)}, bf16[128,1024]{1,0:T(8,128)(2,1)}) conditional(s32[]{:T(128)} %convert_element_type.1267, (bf16[128,1024]{1,0:T(8,128)(2,1)S(1)}, bf16[4096,1024]{1,0:T(8,128)(2,1)}, s32[]{:T(128)}, f32[4,128,4096]{2,1,0:T(8,128)}, ...), branch_computations={%region_129.134_spmd, %region_135.141_spmd} | conditional | flops 4322623488 | bytes 120506536
  625.1 14.7 %convolution_add_fusion.11 = f32[4096,1024]{1,0:T(8,128)} fusion(f32[4096,1024]{1,0:T(8,128)} %get-tuple-element.4079, bf16[128,1024]{1,0:T(8,128)(2,1)S(1)} %get-tuple-element.4071, f32[4,128,4096]{2,1,0:T(8,128)} %get-tuple-element.4073, s32[]{:T(128)S(6)} %select_n.539), kind=kOutput, calls=%fused_computation.810 | convolution fusion | flops 1082654720 | bytes 35913732 | tf_op jit(solution)/shard_map/cond/branch_1_fun/cond/branch_0_fun/dot_general | solution.py:59
  639.8 14.0 convolution_add_fusion.12
  674.6 44.2 %collective-permute-start.11 = (bf16[128,1024]{1,0:T(8,128)(2,1)}, bf16[128,1024]{1,0:T(8,128)(2,1)S(1)}, u32[]{:S(2)}, u32[]{:S(2)}) collective-permute-start(bf16[128,1024]{1,0:T(8,128)(2,1)} %get-tuple-element.4392), channel_id=1, source_target_pairs={{32,0},{64,32},{96,64},{33,1},{65,33},{97,65},{34,2},{66,34},{98,6... | collective-permute-start | bytes 786440 | tf_op jit(solution)/shard_map/ppermute | solution.py:18
  760.2 116.3 %all-reduce.22.cloned.1.call-done = bf16[512,1024]{1,0:T(8,128)(2,1)} async-done(((bf16[512,1024]{1,0:T(8,128)(2,1)}), bf16[512,1024]{1,0:T(8,128)(2,1)}) %all-reduce.22.cloned.1.call-update) | async-done | bytes 1048592 | tf_op jit(solution)/shard_map/psum | solution.py:23
  914.1 65.6 %fusion = bf16[512,256]{1,0:T(8,128)(2,1)S(1)} fusion(bf16[8000,256]{1,0:T(8,128)(2,1)} %convolution_convert_fusion.14), kind=kCustom, calls=%all-reduce-scatter | all-reduce-scatter fusion | flops 2097153 | bytes 4358656
  989.5 51.0 %reduce-scatter.17.cloned.1.call-done = bf16[128,1024]{1,0:T(8,128)(2,1)} async-done(((bf16[2048,1024]{1,0:T(8,128)(2,1)}), bf16[128,1024]{1,0:T(8,128)(2,1)}) %reduce-scatter.17.cloned.1.call-update) | async-done | bytes 262160 | tf_op jit(solution)/shard_map/reduce_scatter | solution.py:407
  1040.5 98.2 %reduce-scatter.21.cloned.1.call-done = bf16[2000,64]{1,0:T(8,128)(2,1)} async-done(((bf16[32000,64]{1,0:T(8,128)(2,1)}), bf16[2000,64]{1,0:T(8,128)(2,1)}) %reduce-scatter.21.cloned.1.call-update) | async-done | bytes 256016
  1138.7 87.2 %reduce-scatter.13.cloned.1.call-done = bf16[64,4096]{1,0:T(8,128)(2,1)} async-done(((bf16[1024,4096]{1,0:T(8,128)(2,1)}), bf16[64,4096]{1,0:T(8,128)(2,1)}) %reduce-scatter.13.cloned.1.call-update) | async-done | bytes 524304 | tf_op jit(solution)/shard_map/reduce_scatter | solution.py:401
  1228.5 28.9 %all-reduce.26.cloned.1.call-done = (bf16[2000,64]{1,0:T(8,128)(2,1)}, bf16[1,64,4096]{2,1,0:T(8,128)(2,1)}, bf16[128,1024]{1,0:T(8,128)(2,1)}, bf16[128,1024]{1,0:T(8,128)(2,1)}, bf16[500,256]{1,0:T(8,128)(2,1)}) async-done(((bf16[2000,64]{1,0:T(8,128)(2,1)}, bf16[1,64,4096]{2,1,0:T(8,128)(2,1)}, bf16[128,1024]{1,0:T(8,128)(2,1)}, bf16[128,1024]{1,0:T(8,128)(2,1)}, bf16[500,256]{1,0:T(8,128)(2,1)}), ...) | async-done | bytes 1560592 | tf_op jit(solution)/shard_map/psum | solution.py:436
  1263.3 26.6 %all-reduce.6 = (bf16[1024]{0:T(1024)(128)(2,1)S(1)}, bf16[256]{0:T(256)(128)(2,1)S(1)}) all-reduce(bf16[1024]{0:T(1024)(128)(2,1)S(1)} %convert_element_type.1407, bf16[256]{0:T(256)(128)(2,1)S(1)} %dynamic_slice.702), channel_id=7, replica_groups=mesh['section'=4,'group'=2,'row'=16] {'row'}, use_global_device_ids=true, to_apply=%region_193.194.clone | all-reduce | flops 1280 | bytes 5120
  1290.7 51.5 %all-reduce.24.cloned.1.call-done = bf16[64,1024]{1,0:T(8,128)(2,1)} async-done(((bf16[64,1024]{1,0:T(8,128)(2,1)}), bf16[64,1024]{1,0:T(8,128)(2,1)}) %all-reduce.24.cloned.1.call-update) | async-done | bytes 131088
  1343.0 73.9 %reduce-scatter.19.cloned.1.call-done = bf16[64,64]{1,0:T(8,128)(2,1)} async-done(((bf16[1024,64]{1,0:T(8,128)(2,1)}), bf16[64,64]{1,0:T(8,128)(2,1)}) %reduce-scatter.19.cloned.1.call-update) | async-done | bytes 8208 | tf_op jit(solution)/shard_map/reduce_scatter | solution.py:425
  (350 shorter events, 489.9 us)
Async XLA Ops:
  7.2 320.8 %copy-start = (bf16[1024,64]{0,1:T(8,128)(2,1)S(1)}, bf16[1024,64]{0,1:T(8,128)(2,1)}, u32[]{:S(2)}) copy-start(bf16[1024,64]{0,1:T(8,128)(2,1)} %param.78) | copy-start | bytes 393220
  7.2 118.2 %all-reduce.16.cloned.1.call-start = ((), (), s32[]{:S(2)}) async-start(), calls=%async_computation.6 | async-start | bytes 2097152 | tf_op jit(solution)/shard_map/psum | solution.py:222
  7.2 110.5 %collective-permute-start = (bf16[2048,1024]{1,0:T(8,128)(2,1)}, bf16[2048,1024]{1,0:T(8,128)(2,1)}, u32[]{:S(2)}, u32[]{:S(2)}) collective-permute-start(bf16[2048,1024]{1,0:T(8,128)(2,1)} %bitcast.1056), channel_id=1, source_target_pairs={{0,32},{32,64},{64,96},{1,33},{33,65},{65,97},{2,34},{34,66},{66,9... | collective-permute-start | bytes 12582920 | tf_op jit(solution)/shard_map/ppermute | solution.py:18
  24.7 297.4 %all-reduce.18.cloned.1.call-start = ((), (), s32[]{:S(2)}) async-start(), calls=%async_computation.7 | async-start | bytes 2097152 | tf_op jit(solution)/shard_map/psum | solution.py:23
  143.5 8.4 collective-permute-start.1
  154.8 7.3 collective-permute-start.2
  171.6 20.7 %collective-permute-start.3 = (bf16[128,1024]{1,0:T(8,128)(2,1)}, bf16[128,1024]{1,0:T(8,128)(2,1)S(1)}, u32[]{:S(2)}, u32[]{:S(2)}) collective-permute-start(bf16[128,1024]{1,0:T(8,128)(2,1)} %get-tuple-element.4349), channel_id=1, source_target_pairs={{0,32},{32,64},{64,96},{1,33},{33,65},{65,97},{2,34},{34,66},{66,9... | collective-permute-start | bytes 786440 | tf_op jit(solution)/shard_map/ppermute | solution.py:18
  203.1 14.6 %collective-permute-start.4 = (bf16[128,1024]{1,0:T(8,128)(2,1)}, bf16[128,1024]{1,0:T(8,128)(2,1)S(1)}, u32[]{:S(2)}, u32[]{:S(2)}) collective-permute-start(bf16[128,1024]{1,0:T(8,128)(2,1)} %get-tuple-element.4355), channel_id=1, source_target_pairs={{0,32},{32,64},{64,96},{1,33},{33,65},{65,97},{2,34},{34,66},{66,9... | collective-permute-start | bytes 786440 | tf_op jit(solution)/shard_map/ppermute | solution.py:18
  228.3 9.2 collective-permute-start.5
  248.2 8.9 collective-permute-start.6
  270.4 141.3 %reduce-scatter.11.cloned.1.call-start = ((), (), s32[]{:S(2)}) async-start(), calls=%async_computation.8 | async-start | bytes 327680 | tf_op jit(solution)/shard_map/reduce_scatter | solution.py:302
  383.1 78.5 %all-reduce.20.cloned.1.call-start = ((), (), s32[]{:S(2)}) async-start(), calls=%async_computation.9 | async-start | bytes 2097152 | tf_op jit(solution)/shard_map/psum | solution.py:309
  414.0 462.4 %all-reduce.22.cloned.1.call-start = ((), (), s32[]{:S(2)}) async-start(), calls=%async_computation.10 | async-start | bytes 2097152 | tf_op jit(solution)/shard_map/psum | solution.py:23
  498.5 5.8 collective-permute-start.7
  555.0 5.1 collective-permute-start.8
  611.1 4.9 collective-permute-start.9
  659.3 6.8 collective-permute-start.10
  674.6 47.8 %collective-permute-start.11 = (bf16[128,1024]{1,0:T(8,128)(2,1)}, bf16[128,1024]{1,0:T(8,128)(2,1)S(1)}, u32[]{:S(2)}, u32[]{:S(2)}) collective-permute-start(bf16[128,1024]{1,0:T(8,128)(2,1)} %get-tuple-element.4392), channel_id=1, source_target_pairs={{32,0},{64,32},{96,64},{33,1},{65,33},{97,65},{34,2},{66,34},{98,6... | collective-permute-start | bytes 786440 | tf_op jit(solution)/shard_map/ppermute | solution.py:18
  730.9 7.7 collective-permute-start.12
  749.0 240.5 %reduce-scatter.15.cloned.1.call-start = ((), (), s32[]{:S(2)}) async-start(), calls=%async_computation.12 | async-start | bytes 4456448 | tf_op jit(solution)/shard_map/reduce_scatter | solution.py:404
  759.4 281.1 %reduce-scatter.17.cloned.1.call-start = ((), (), s32[]{:S(2)}) async-start(), calls=%async_computation.13 | async-start | bytes 4456448 | tf_op jit(solution)/shard_map/reduce_scatter | solution.py:407
  760.1 378.6 %reduce-scatter.21.cloned.1.call-start = ((), (), s32[]{:S(2)}) async-start(), calls=%async_computation.16 | async-start | bytes 8704000
  896.1 329.8 %reduce-scatter.13.cloned.1.call-start = ((), (), s32[]{:S(2)}) async-start(), calls=%async_computation.11 | async-start | bytes 8912896 | tf_op jit(solution)/shard_map/reduce_scatter | solution.py:401
  905.5 351.9 %all-reduce.26.cloned.1.call-start = ((), (), s32[]{:S(2)}) async-start(), calls=%async_computation.17 | async-start | bytes 3637248 | tf_op jit(solution)/shard_map/psum | solution.py:436
  914.1 311.9 %copy-start.20 = (bf16[512,64]{1,0:T(8,128)(2,1)S(1)}, bf16[512,64]{1,0:T(8,128)(2,1)}, u32[]{:S(2)}) copy-start(bf16[512,64]{1,0:T(8,128)(2,1)} %copy-done.19) | copy-start | bytes 196612
  914.1 312.0 %copy-start.25 = (bf16[4,1,128,64]{2,3,1,0:T(8,128)(2,1)S(1)}, bf16[4,1,128,64]{2,3,1,0:T(8,128)(2,1)}, u32[]{:S(2)}) copy-start(bf16[4,1,128,64]{2,3,1,0:T(8,128)(2,1)} %param.71) | copy-start | bytes 196612
  914.1 312.1 %copy-start.16 = (bf16[512,1024]{1,0:T(8,128)(2,1)S(1)}, bf16[512,1024]{1,0:T(8,128)(2,1)}, u32[]{:S(2)}) copy-start(bf16[512,1024]{1,0:T(8,128)(2,1)} %all-reduce.22.cloned.1.call-done) | copy-start | bytes 3145732
  979.7 247.5 %copy-start.12 = (bf16[512,1024]{1,0:T(8,128)(2,1)S(1)}, bf16[512,1024]{1,0:T(8,128)(2,1)}, u32[]{:S(2)}) copy-start(bf16[512,1024]{1,0:T(8,128)(2,1)} %copy-done.11) | copy-start | bytes 3145732
  979.8 8.4 collective-permute-start.14
  1225.9 116.3 %all-reduce.24.cloned.1.call-start = ((), (), s32[]{:S(2)}) async-start(), calls=%async_computation.15 | async-start | bytes 262144
  1227.2 189.6 %reduce-scatter.19.cloned.1.call-start = ((), (), s32[]{:S(2)}) async-start(), calls=%async_computation.14 | async-start | bytes 278528 | tf_op jit(solution)/shard_map/reduce_scatter | solution.py:425
  1257.4 174.3 %collective-permute-start.13 = (bf16[128,1024]{1,0:T(8,128)(2,1)}, bf16[128,1024]{1,0:T(8,128)(2,1)S(1)}, u32[]{:S(2)}, u32[]{:S(2)}) collective-permute-start(bf16[128,1024]{1,0:T(8,128)(2,1)} %get-tuple-element.5024), channel_id=1, source_target_pairs={{32,0},{64,32},{96,64},{33,1},{65,33},{97,65},{34,2},{66,34},{98,6... | collective-permute-start | bytes 786440 | tf_op jit(solution)/shard_map/ppermute | solution.py:18
  (36 other events, 1495.1 us)
Sparse Core Ops, SparseCore 0:
  24.9 59.6 all-reduce.15
  270.5 51.5 all-reduce.17
  383.2 28.4 reduce-scatter.10
  414.2 47.3 all-reduce.19
  749.2 127.2 all-reduce.21
  880.0 81.0 reduce-scatter.14
  964.5 75.9 reduce-scatter.16
  1044.5 94.1 reduce-scatter.20
  1142.5 83.3 reduce-scatter.12
  1229.4 27.9 all-reduce.25
  1261.5 80.6 all-reduce.23
  1345.8 70.9 reduce-scatter.18
where the time goes:
time: 1450 us; the launch traced here: 1440 us
  waiting for transfers between devices  812 us (56%)
  matrix products  208 us (14%)
  blocking collectives  123 us (8%)
  other arithmetic  96.9 us (7%)
  starting transfers between devices  70 us (5%)
  loops' own time  57.5 us (4%)
  local copies, waits for them, and re-layouts  54 us (4%)
  between operations  18 us (1%)
    ppermute x14, waiting for transfers between devices, shifted(): return lax.ppermute(shard, axis, pairs)  172 us
    psum x2, waiting for transfers between devices, from_root(): return lax.psum(jnp.where(mine, shard, jnp.zeros_like(shard)), axis)  168 us
    unnamed x15, waiting for transfers between devices  155 us
    dot_general x11, matrix products, matmul_tn(): lax.dot_general(former, latter, (((0,), (0,)), ((), ())), preferred_eleme...  114 us
    unnamed x2, blocking collectives  92.1 us
    reduce_scatter x1, waiting for transfers between devices, local(): lax.psum_scatter(pieces[0].astype(jnp.bfloat16), 'row', scatter_dimension...  87.2 us
    reduce_scatter x1, waiting for transfers between devices, local(): lax.psum_scatter(pieces[8].astype(jnp.bfloat16), 'row', scatter_dimension...  73.9 us
    ppermute x14, starting transfers between devices, shifted(): return lax.ppermute(shard, axis, pairs)  67.1 us
  transfers between devices with their start and end apart: 27, of which 24 were waited for; matrix products, arithmetic and copies ran while one was open for 11% of the time, Pallas kernels for 0%

commit v1 on v0

v1 whole, which is shorter than its diff:
```python
import itertools

import jax
import jax.numpy as jnp
from jax import lax
from jax.experimental import pallas as pl
from jax.experimental.pallas import tpu as pltpu
from jax.sharding import PartitionSpec as P

HEADS = 16
HEAD_SIZE = 64
LOW = jnp.bfloat16
WIDE = jnp.float32
EPSILON = 1e-05
MASKED = -1000000000.0
CHUNK = 512


def matmul(former, latter):
    return jnp.dot(former, latter, preferred_element_type=WIDE)


def matmul_nt(former, latter):
    return lax.dot_general(
        former, latter, (((1,), (1,)), ((), ())), preferred_element_type=WIDE
    )


def matmul_tn(former, latter):
    return lax.dot_general(
        former, latter, (((0,), (0,)), ((), ())), preferred_element_type=WIDE
    )


def layer_norm(values):
    centre = jnp.mean(values, axis=-1, keepdims=True)
    centred = values - centre
    variance = jnp.mean(centred * centred, axis=-1, keepdims=True)
    factor = lax.rsqrt(variance + EPSILON)
    return (centred * factor, factor)


def norm_back(grad_normed, normed, factor):
    first_mean = jnp.mean(grad_normed, axis=-1, keepdims=True)
    second_mean = jnp.mean(grad_normed * normed, axis=-1, keepdims=True)
    return factor * (grad_normed - first_mean - normed * second_mean)


GELU_A = 0.7978845608028654
GELU_B = 0.044715


def gelu(v):
    return 0.5 * v * (1.0 + jnp.tanh(GELU_A * (v + GELU_B * (v * v * v))))


def gelu_slope(v):
    square = v * v
    bend = jnp.tanh(GELU_A * (v + GELU_B * (square * v)))
    return 0.5 * (1.0 + bend) + 0.5 * v * (1.0 - bend * bend) * (
        GELU_A * (1.0 + 3.0 * GELU_B * square)
    )


def head_probs(scores, same):
    scores = jnp.where(same, scores * HEAD_SIZE ** (-0.5), MASKED)
    expo = jnp.exp(scores - jnp.max(scores, axis=-1, keepdims=True))
    return expo / jnp.sum(expo, axis=-1, keepdims=True)


def weight_copies(lead_ref, down_ref, lead_buf, down_buf, sems):
    count = lead_buf.shape[0]
    leads = [
        pltpu.make_async_copy(
            lead_ref.at[:, pl.ds(j * CHUNK, CHUNK)], lead_buf.at[j], sems.at[j]
        )
        for j in range(count)
    ]
    downs = [
        pltpu.make_async_copy(
            down_ref.at[pl.ds(j * CHUNK, CHUNK), :], down_buf.at[j], sems.at[count + j]
        )
        for j in range(count)
    ]
    return leads, downs


def forward_kernel(
    role_ref,
    entry_ref,
    seg_col_ref,
    seg_row_ref,
    gain_ref,
    lead_ref,
    down_ref,
    entries_in,
    normeds_in,
    saved_in,
    inner_in,
    out_ref,
    entries_ref,
    normeds_ref,
    saved_ref,
    inner_ref,
    lead_buf,
    down_buf,
    normed_buf,
    saved_buf,
    inner_buf,
    sems,
    out_sems,
):
    role, slot = role_ref[0], role_ref[1]
    width = entry_ref.shape[1]
    leads, downs = weight_copies(lead_ref, down_ref, lead_buf, down_buf, sems)
    count = len(leads)
    keep_normed = pltpu.make_async_copy(normed_buf, normeds_ref.at[slot], out_sems.at[0])
    keep_saved = pltpu.make_async_copy(saved_buf, saved_ref.at[slot], out_sems.at[1])
    keep_inner = pltpu.make_async_copy(inner_buf, inner_ref.at[slot], out_sems.at[2])
    keep_entry = pltpu.make_async_copy(entry_ref, entries_ref.at[slot], out_sems.at[3])

    @pl.when(role == 0)
    def _():
        out_ref[...] = jnp.zeros_like(out_ref)

    @pl.when(role == 1)
    def _():
        for j in range(count):
            leads[j].start()
        keep_entry.start()
        residual = entry_ref[...].astype(WIDE)
        normed, _ = layer_norm(residual)
        normed_buf[...] = (normed * gain_ref[...]).astype(LOW)
        keep_normed.start()
        qkv = 3 * width // CHUNK
        for j in range(qkv):
            leads[j].wait()
            saved_buf[:, j * CHUNK : (j + 1) * CHUNK] = matmul(
                normed_buf[...], lead_buf[j]
            ).astype(LOW)
        same = seg_col_ref[slot] == seg_row_ref[slot]
        left = lax.broadcasted_iota(jnp.int32, (entry_ref.shape[0], 128), 1) < HEAD_SIZE
        zero = jnp.zeros((entry_ref.shape[0], 128), LOW)
        for pair in range(HEADS // 2):
            at = pair * 128
            query = saved_buf[:, at : at + 128]
            key = saved_buf[:, width + at : width + at + 128]
            value = saved_buf[:, 2 * width + at : 2 * width + at + 128]
            probs_a = head_probs(matmul_nt(jnp.where(left, query, zero), key), same)
            probs_b = head_probs(matmul_nt(jnp.where(left, zero, query), key), same)
            mixed = jnp.where(
                left, matmul(probs_a.astype(LOW), value), matmul(probs_b.astype(LOW), value)
            )
            saved_buf[:, 3 * width + at : 3 * width + at + 128] = mixed.astype(LOW)
        keep_saved.start()
        mixed = saved_buf[:, 3 * width :]
        for j in range(qkv, count):
            leads[j].wait()
            at = (j - qkv) * CHUNK
            out_ref[:, at : at + CHUNK] = (
                entry_ref[:, at : at + CHUNK].astype(WIDE) + matmul(mixed, lead_buf[j])
            ).astype(LOW)
        keep_entry.wait()
        keep_normed.wait()
        keep_saved.wait()

    @pl.when(role == 2)
    def _():
        for j in range(count):
            leads[j].start()
            downs[j].start()
        keep_entry.start()
        residual = entry_ref[...].astype(WIDE)
        normed, _ = layer_norm(residual)
        normed_buf[...] = (normed * gain_ref[...]).astype(LOW)
        keep_normed.start()
        result = residual
        for j in range(count):
            leads[j].wait()
            inner = matmul(normed_buf[...], lead_buf[j])
            inner_buf[:, j * CHUNK : (j + 1) * CHUNK] = inner
            active = gelu(inner).astype(LOW)
            saved_buf[:, j * CHUNK : (j + 1) * CHUNK] = active
            downs[j].wait()
            result = result + matmul(active, down_buf[j])
        keep_saved.start()
        keep_inner.start()
        out_ref[...] = result.astype(LOW)
        keep_entry.wait()
        keep_normed.wait()
        keep_saved.wait()
        keep_inner.wait()


VMEM_SPEC = pl.BlockSpec(memory_space=pltpu.VMEM)
ANY_SPEC = pl.BlockSpec(memory_space=pl.ANY)


def weight_scratch(width, hidden):
    count = hidden // CHUNK
    return [
        pltpu.VMEM((count, width, CHUNK), LOW),
        pltpu.VMEM((count, CHUNK, width), LOW),
    ]


def forward_stage(role, entry, seg_col, seg_row, gain, lead, down, kept):
    tokens, width = entry.shape
    hidden = lead.shape[1]
    return pl.pallas_call(
        forward_kernel,
        out_shape=[jax.ShapeDtypeStruct(entry.shape, LOW)]
        + [jax.ShapeDtypeStruct(k.shape, k.dtype) for k in kept],
        in_specs=[pl.BlockSpec(memory_space=pltpu.SMEM)]
        + [VMEM_SPEC] * 4
        + [ANY_SPEC] * 6,
        out_specs=[VMEM_SPEC] + [ANY_SPEC] * 4,
        scratch_shapes=weight_scratch(width, hidden)
        + [
            pltpu.VMEM((tokens, width), LOW),
            pltpu.VMEM((tokens, hidden), LOW),
            pltpu.VMEM((tokens, hidden), WIDE),
            pltpu.SemaphoreType.DMA((2 * hidden // CHUNK,)),
            pltpu.SemaphoreType.DMA((4,)),
        ],
        input_output_aliases={7: 1, 8: 2, 9: 3, 10: 4},
        compiler_params=pltpu.CompilerParams(vmem_limit_bytes=30 << 20),
        cost_estimate=pl.CostEstimate(
            flops=4 * tokens * width * hidden, bytes_accessed=20 << 20, transcendentals=0
        ),
        name="forward_stage",
    )(role, entry, seg_col, seg_row, gain, lead, down, *kept)


def backward_kernel(
    role_ref,
    grad_ref,
    seg_col_ref,
    seg_row_ref,
    gain_ref,
    lead_ref,
    down_ref,
    entries_ref,
    saved_ref,
    inner_ref,
    nexts_in,
    grads_in,
    gains_in,
    out_ref,
    nexts_ref,
    grads_ref,
    gains_ref,
    lead_buf,
    down_buf,
    saved_buf,
    inner_buf,
    grads_buf,
    mixed_buf,
    gain_buf,
    entry_buf,
    sems,
    in_sems,
    out_sems,
):
    role, slot = role_ref[0], role_ref[1]
    tokens, width = grad_ref.shape
    leads, downs = weight_copies(lead_ref, down_ref, lead_buf, down_buf, sems)
    count = len(leads)
    bring_saved = pltpu.make_async_copy(saved_ref.at[slot], saved_buf, in_sems.at[0])
    bring_inner = pltpu.make_async_copy(inner_ref.at[slot], inner_buf, in_sems.at[1])
    bring_entry = pltpu.make_async_copy(entries_ref.at[slot], entry_buf, in_sems.at[2])
    keep_next = pltpu.make_async_copy(grad_ref, nexts_ref.at[slot], out_sems.at[0])
    keep_grads = pltpu.make_async_copy(grads_buf, grads_ref.at[slot], out_sems.at[1])
    keep_gain = pltpu.make_async_copy(gain_buf, gains_ref.at[slot], out_sems.at[2])
    qkv = 3 * width // CHUNK

    def finish(grad_normed):
        keep_grads.start()
        bring_entry.wait()
        normed, factor = layer_norm(entry_buf[...].astype(WIDE))
        gain_buf[...] = jnp.broadcast_to(
            jnp.sum(grad_normed * normed, axis=0, keepdims=True), gain_buf.shape
        )
        keep_gain.start()
        out_ref[...] = (
            grad_ref[...].astype(WIDE) + norm_back(grad_normed * gain_ref[...], normed, factor)
        ).astype(LOW)
        keep_next.wait()
        keep_grads.wait()
        keep_gain.wait()

    @pl.when(role == 0)
    def _():
        out_ref[...] = jnp.zeros_like(out_ref)

    @pl.when(role == 1)
    def _():
        bring_saved.start()
        for j in list(range(qkv, count)) + list(range(qkv)):
            leads[j].start()
        keep_next.start()
        bring_entry.start()
        grads_buf[:, 3 * width :] = grad_ref[...]
        grad_mixed = jnp.zeros((tokens, width), WIDE)
        for j in range(qkv, count):
            leads[j].wait()
            at = (j - qkv) * CHUNK
            grad_mixed = grad_mixed + matmul_nt(grad_ref[:, at : at + CHUNK], lead_buf[j])
        mixed_buf[...] = grad_mixed.astype(LOW)
        bring_saved.wait()
        same = seg_col_ref[slot] == seg_row_ref[slot]
        left = lax.broadcasted_iota(jnp.int32, (tokens, 128), 1) < HEAD_SIZE
        zero = jnp.zeros((tokens, 128), LOW)
        scale = HEAD_SIZE ** (-0.5)
        for pair in range(HEADS // 2):
            at = pair * 128
            query = saved_buf[:, at : at + 128]
            key = saved_buf[:, width + at : width + at + 128]
            value = saved_buf[:, 2 * width + at : 2 * width + at + 128]
            grad = mixed_buf[:, at : at + 128]
            parts = []
            for own in (0, 1):
                mine = lambda v: jnp.where(left, v, zero) if own == 0 else jnp.where(left, zero, v)
                probs = head_probs(matmul_nt(mine(query), key), same)
                grad_probs = matmul_nt(mine(grad), value)
                grad_scores = probs * (
                    grad_probs - jnp.sum(probs * grad_probs, axis=-1, keepdims=True)
                )
                grad_low = grad_scores.astype(LOW)
                parts.append(
                    (
                        matmul(grad_low, key) * scale,
                        matmul_tn(grad_low, query) * scale,
                        matmul_tn(probs.astype(LOW), grad),
                    )
                )
            for which in range(3):
                spot = which * width + at
                grads_buf[:, spot : spot + 128] = jnp.where(
                    left, parts[0][which], parts[1][which]
                ).astype(LOW)
        grad_normed = jnp.zeros((tokens, width), WIDE)
        for j in range(qkv):
            leads[j].wait()
            grad_normed = grad_normed + matmul_nt(
                grads_buf[:, j * CHUNK : (j + 1) * CHUNK], lead_buf[j]
            )
        finish(grad_normed)

    @pl.when(role == 2)
    def _():
        bring_inner.start()
        for j in range(count):
            downs[j].start()
            leads[j].start()
        keep_next.start()
        bring_entry.start()
        grad_normed = jnp.zeros((tokens, width), WIDE)
        bring_inner.wait()
        for j in range(count):
            at = slice(j * CHUNK, (j + 1) * CHUNK)
            downs[j].wait()
            grad_active = matmul_nt(grad_ref[...], down_buf[j])
            grads_buf[:, at] = (gelu_slope(inner_buf[:, at]) * grad_active).astype(LOW)
            leads[j].wait()
            grad_normed = grad_normed + matmul_nt(grads_buf[:, at], lead_buf[j])
        finish(grad_normed)


def backward_stage(
    role, grad, seg_col, seg_row, gain, lead, down, entries, saved, inner, totals
):
    tokens, width = grad.shape
    hidden = lead.shape[1]
    return pl.pallas_call(
        backward_kernel,
        out_shape=[jax.ShapeDtypeStruct(grad.shape, LOW)]
        + [jax.ShapeDtypeStruct(k.shape, k.dtype) for k in totals],
        in_specs=[pl.BlockSpec(memory_space=pltpu.SMEM)]
        + [VMEM_SPEC] * 4
        + [ANY_SPEC] * 8,
        out_specs=[VMEM_SPEC] + [ANY_SPEC] * 3,
        scratch_shapes=weight_scratch(width, hidden)
        + [
            pltpu.VMEM((tokens, hidden), LOW),
            pltpu.VMEM((tokens, hidden), WIDE),
            pltpu.VMEM((tokens, hidden), LOW),
            pltpu.VMEM((tokens, width), LOW),
            pltpu.VMEM((8, width), WIDE),
            pltpu.VMEM((tokens, width), LOW),
            pltpu.SemaphoreType.DMA((2 * hidden // CHUNK,)),
            pltpu.SemaphoreType.DMA((3,)),
            pltpu.SemaphoreType.DMA((3,)),
        ],
        input_output_aliases={10: 1, 11: 2, 12: 3},
        compiler_params=pltpu.CompilerParams(vmem_limit_bytes=32 << 20),
        cost_estimate=pl.CostEstimate(
            flops=4 * tokens * width * hidden, bytes_accessed=20 << 20, transcendentals=0
        ),
        name="backward_stage",
    )(role, grad, seg_col, seg_row, gain, lead, down, entries, saved, inner, *totals)


def stats_kernel(readout_ref, table_ref, peak_ref, total_ref):
    logits = matmul_nt(table_ref[...], readout_ref[...])
    own_peak = jnp.max(logits, axis=0, keepdims=True)
    own_total = lambda peak: jnp.sum(jnp.exp(logits - peak), axis=0, keepdims=True)

    @pl.when(pl.program_id(0) == 0)
    def _():
        peak_ref[...] = own_peak
        total_ref[...] = own_total(own_peak)

    @pl.when(pl.program_id(0) > 0)
    def _():
        peak = jnp.maximum(peak_ref[...], own_peak)
        total_ref[...] = total_ref[...] * jnp.exp(peak_ref[...] - peak) + own_total(peak)
        peak_ref[...] = peak


def head_stats(readout, table, tile):
    tokens, emb = readout.shape
    vocab = table.shape[0]
    whole = pl.BlockSpec((1, tokens), lambda i: (0, 0))
    return pl.pallas_call(
        stats_kernel,
        out_shape=[jax.ShapeDtypeStruct((1, tokens), WIDE)] * 2,
        grid=(vocab // tile,),
        in_specs=[
            pl.BlockSpec((tokens, emb), lambda i: (0, 0)),
            pl.BlockSpec((tile, emb), lambda i: (i, 0)),
        ],
        out_specs=[whole, whole],
        compiler_params=pltpu.CompilerParams(vmem_limit_bytes=40 << 20),
        cost_estimate=pl.CostEstimate(
            flops=2 * tokens * vocab * emb, bytes_accessed=5 << 20, transcendentals=tokens * vocab
        ),
        name="head_stats",
    )(readout, table)


def head_kernel(base_ref, readout_ref, table_ref, logsum_ref, ids_ref, head_ref, grad_ref):
    tile = table_ref.shape[0]
    logits = matmul_nt(table_ref[...], readout_ref[...])
    ids = ids_ref[...] - (base_ref[0] + pl.program_id(0) * tile)
    hits = lax.broadcasted_iota(jnp.int32, logits.shape, 0) == ids
    probs = jnp.exp(logits - logsum_ref[...])
    grads = jnp.where(hits, probs - 1.0, probs).astype(LOW)
    head_ref[...] = matmul(grads, readout_ref[...]).astype(LOW)
    term = matmul_tn(grads, table_ref[...])

    @pl.when(pl.program_id(0) == 0)
    def _():
        grad_ref[...] = term

    @pl.when(pl.program_id(0) > 0)
    def _():
        grad_ref[...] += term


def head_grads(base, readout, table, logsum, ids, tile):
    tokens, emb = readout.shape
    vocab = table.shape[0]
    row = pl.BlockSpec((1, tokens), lambda i: (0, 0))
    whole = pl.BlockSpec((tokens, emb), lambda i: (0, 0))
    part = pl.BlockSpec((tile, emb), lambda i: (i, 0))
    return pl.pallas_call(
        head_kernel,
        out_shape=[
            jax.ShapeDtypeStruct((vocab, emb), LOW),
            jax.ShapeDtypeStruct((tokens, emb), WIDE),
        ],
        grid=(vocab // tile,),
        in_specs=[pl.BlockSpec(memory_space=pltpu.SMEM), whole, part, row, row],
        out_specs=[part, whole],
        compiler_params=pltpu.CompilerParams(vmem_limit_bytes=40 << 20),
        cost_estimate=pl.CostEstimate(
            flops=6 * tokens * vocab * emb, bytes_accessed=9 << 20, transcendentals=tokens * vocab
        ),
        name="head_grads",
    )(base, readout, table, logsum, ids)


ROW_LEN = 128
SEC, GRP, NX, NY = 4, 2, 4, 4
ALL = ("section", "group", "row")
TURNS = (1, 3, 2)


def route(value, target_of):
    number = lambda s, g, x, y: (s * GRP + g) * NX * NY + x * NY + y
    pairs = []
    for at in itertools.product(range(SEC), range(GRP), range(NX), range(NY)):
        target = target_of(*at)
        if target is not None:
            pairs.append((number(*at), number(*target)))
    return lax.ppermute(value, ALL, pairs)


def link(value, source, target):
    return route(value, lambda s, g, x, y: (target, g, x, y) if s == source else None)


def turn(value, by):
    return route(value, lambda s, g, x, y: ((s + by) % SEC, g, x, y))


def swap_cores(value, sections=range(SEC)):
    return route(value, lambda s, g, x, y: (s, 1 - g, x, y) if s in sections else None)


def plane_route(value, by, first, sections=range(SEC)):
    def target_of(s, g, x, y):
        if s not in sections:
            return None
        if (g == 0) == first:
            return (s, g, (x + by) % NX, y)
        return (s, g, x, (y + by) % NY)

    return route(value, target_of)


def after(value, earlier):
    return lax.optimization_barrier((value, earlier))[0]


def block_of(values, block, count):
    size = values.shape[1] // count
    return lax.dynamic_slice_in_dim(values, block * size, size, 1)


def row_block(values, block, count):
    size = values.shape[0] // count
    return lax.dynamic_slice_in_dim(values, block * size, size, 0)


def by_second(values, unit):
    rows, columns = values.shape
    return values.reshape(rows, NX, NY, unit).transpose(0, 2, 1, 3).reshape(rows, columns)


def reduce_plane(block_for, second, sections=range(SEC)):
    pieces = {by: block_for(by) for by in TURNS + (0,)}
    total = pieces[0].astype(WIDE)
    for by in TURNS:
        total = total + plane_route(pieces[by], by, True, sections).astype(WIDE)
    lowered = total.astype(LOW)
    mine = row_block(total, second, 4)
    for by in TURNS:
        piece = row_block(lowered, (second + by) % 4, 4)
        mine = mine + plane_route(piece, by, False, sections).astype(WIDE)
    return mine.astype(LOW)


def gather_plane(values):
    blocks = jnp.stack([values] + [plane_route(values, by, True) for by in TURNS])
    blocks = jnp.concatenate([blocks] + [plane_route(blocks, by, False) for by in TURNS])
    return jnp.concatenate([blocks, swap_cores(blocks)])


def embed_kernel(base_ref, ids_ref, grad_ref, out_ref):
    @pl.when(pl.program_id(0) == 0)
    def _():
        out_ref[...] = jnp.zeros_like(out_ref)

    tokens = grad_ref.shape[2]
    local = ids_ref[...] - base_ref[0]
    for block in range(grad_ref.shape[0]):
        ids = local[block * tokens : (block + 1) * tokens]
        hits = lax.broadcasted_iota(jnp.int32, (tokens, out_ref.shape[1]), 1) == ids
        hits = jnp.where(hits, 1.0, 0.0).astype(LOW)
        out_ref[...] += jnp.dot(grad_ref[block], hits, preferred_element_type=WIDE)


def embed_sum(base, ids, grads, rows):
    count, parts, tokens = grads.shape
    step = 4
    return pl.pallas_call(
        embed_kernel,
        out_shape=jax.ShapeDtypeStruct((parts, rows), WIDE),
        grid=(count // step,),
        in_specs=[
            pl.BlockSpec(memory_space=pltpu.SMEM),
            pl.BlockSpec((step * tokens, 1), lambda i: (i, 0)),
            pl.BlockSpec((step, parts, tokens), lambda i: (i, 0, 0)),
        ],
        out_specs=pl.BlockSpec((parts, rows), lambda i: (0, 0)),
        compiler_params=pltpu.CompilerParams(vmem_limit_bytes=40 << 20),
        cost_estimate=pl.CostEstimate(
            flops=2 * count * tokens * 256 * rows, bytes_accessed=12 << 20, transcendentals=0
        ),
        name="embed_sum",
    )(base, ids.reshape(count * tokens, 1), grads)


def local(
    token_ids,
    segment_ids,
    noise_input,
    embed_table,
    input_proj,
    norm_gain,
    lead_weight,
    down_weight,
    final_gain,
    readout_proj,
    head_table,
):
    section = lax.axis_index("section")
    core = lax.axis_index("group")
    row = lax.axis_index("row")
    x_at, y_at = row // NY, row % NY
    first_at, second_at = jnp.where(core == 0, x_at, y_at), jnp.where(core == 0, y_at, x_at)
    micro, _, tokens = token_ids.shape
    width = input_proj.shape[1]
    hidden = lead_weight.shape[2]
    half_rows = down_weight.shape[1]
    emb_part = input_proj.shape[0]
    vocab_part, emb = head_table.shape
    vocab = embed_table.shape[0]
    all_tokens = micro * tokens
    last = SEC - 1
    is_mlp = section % 2 == 1
    gain_half = norm_gain.astype(WIDE)
    lead = lead_weight[0]
    own_down = down_weight[0]
    seg_row = segment_ids
    seg_col = segment_ids.reshape(micro, tokens, 1)
    flat_ids = token_ids.reshape(-1)

    small_pack = jnp.concatenate((input_proj, readout_proj.T))
    packs = {by: turn(small_pack, by) for by in TURNS}
    packs[0] = small_pack
    pack_of = lambda s: lax.select_n((section - s) % SEC, *[packs[by] for by in range(SEC)])
    packs = [pack_of(s) for s in range(SEC)]
    input_full = jnp.concatenate([p[:emb_part] for p in packs])
    readout_full = jnp.concatenate([p[emb_part:] for p in packs])
    embedded = (
        embed_table[flat_ids].astype(WIDE) + noise_input.reshape(-1, emb_part).astype(WIDE)
    ).astype(LOW)
    parts = {by: turn(after(embedded, packs[0]), by) for by in TURNS}
    embedded = jnp.concatenate(
        [embedded] + [parts[SEC - s] for s in range(1, SEC)], axis=1
    )
    first_in = matmul(embedded, input_full).astype(LOW).reshape(micro, tokens, width)

    eighth = row_block(row_block(own_down, core, 2), first_at, 4)
    eighth = jnp.where(section == 1, link(eighth, 0, 1), link(eighth, 2, 3))
    upper = jnp.zeros((4,) + eighth.shape, LOW)
    upper = lax.dynamic_update_index_in_dim(upper, eighth, first_at, 0)
    for by in TURNS:
        upper = lax.dynamic_update_index_in_dim(
            upper, plane_route(eighth, by, True), (first_at - by) % 4, 0
        )
    upper = upper.reshape(half_rows // 2, width)
    upper_other = swap_cores(upper)
    full_down = jnp.concatenate(
        (
            jnp.where(core == 0, upper, upper_other),
            jnp.where(core == 0, upper_other, upper),
            own_down,
        )
    )
    all_ids = gather_plane(after(flat_ids, upper_other))

    kept = (
        jnp.zeros((micro, tokens, width), LOW),
        jnp.zeros((micro, tokens, width), LOW),
        jnp.zeros((micro, tokens, hidden), LOW),
        jnp.zeros((micro, tokens, hidden), WIDE),
    )

    def role_at(at):
        live = jnp.logical_and(at >= 0, at < micro)
        role = jnp.where(live, jnp.where(is_mlp, 2, 1), 0)
        return jnp.stack((role, jnp.clip(at, 0, micro - 1))).astype(jnp.int32)

    steps = micro + 2 * last
    outs, hops = [], {}

    def arrived(step, by):
        parts = [
            (s + by, hops[step - 2, s])
            for s in range(SEC)
            if (step - 2, s) in hops
        ]
        value = parts[0][1] if parts else None
        for target, part in parts[1:]:
            value = jnp.where(section == target, part, value)
        return value

    for step in range(steps):
        entry = arrived(step, 1)
        if entry is None:
            entry = first_in[step]
        elif step < micro:
            entry = jnp.where(section == 0, first_in[step], entry)
        out, *kept = forward_stage(
            role_at(step - 2 * section), entry, seg_col, seg_row, gain_half, lead, full_down, kept
        )
        outs.append(out)
        for s in range(last):
            if 0 <= step - 2 * s < micro:
                ready = after(out, hops[step - 1, s]) if (step - 1, s) in hops else out
                hops[step, s] = link(ready, s, s + 1)
    entries, normeds, saved, inner = kept

    final_rows = jnp.concatenate(outs[2 * last :]).astype(WIDE)
    normed_f, factor_f = layer_norm(final_rows)
    gain_f = final_gain.astype(WIDE)
    final_low = (normed_f * gain_f).astype(LOW)
    readout = matmul_nt(final_low, readout_full).astype(LOW)
    sent = [link(readout, last, s) for s in range(last)]
    for s in range(last):
        readout = jnp.where(section == s, sent[s], readout)
    peak, total = head_stats(readout, head_table, 1600)
    stats = jnp.concatenate((peak, total))
    all_stats = jnp.stack([stats] + [turn(stats, by) for by in TURNS])
    peak = jnp.max(all_stats[:, 0], axis=0)
    total = jnp.sum(all_stats[:, 1] * jnp.exp(all_stats[:, 0] - peak), axis=0)
    logsum = (peak + jnp.log(total))[None]
    head_grad, grad_readout = head_grads(
        (section * vocab_part).reshape(1), readout, head_table, logsum, flat_ids[None], 1600
    )
    grad_low = grad_readout.astype(LOW)
    for s in range(last):
        grad_readout = grad_readout + link(grad_low, s, last).astype(WIDE)
    grad_readout = grad_readout.astype(LOW)
    head_grad = lax.psum_scatter(
        head_grad.reshape(NX * NY, vocab_part // (NX * NY), emb), "row", scatter_dimension=0
    )
    readout_grad = matmul_tn(final_low, grad_readout)
    grad_final = matmul(grad_readout, readout_full)
    final_gain_grad = jnp.sum(grad_final * normed_f, axis=0)
    last_grads = norm_back(grad_final * gain_f, normed_f, factor_f).astype(LOW)
    last_grads = last_grads.reshape(micro, tokens, width)

    totals = (
        jnp.zeros((micro, tokens, width), LOW),
        jnp.zeros((micro, tokens, hidden), LOW),
        jnp.zeros((micro, 8, width), WIDE),
    )
    outs, hops = [], {}
    for step in range(steps):
        grad_next = arrived(step, -1)
        if grad_next is None:
            grad_next = last_grads[step]
        elif step < micro:
            grad_next = jnp.where(section == last, last_grads[step], grad_next)
        out, *totals = backward_stage(
            role_at(step - 2 * (last - section)),
            grad_next,
            seg_col,
            seg_row,
            gain_half,
            lead,
            full_down,
            entries,
            saved,
            inner,
            totals,
        )
        outs.append(out)
        for s in range(1, SEC):
            if 0 <= step - 2 * (last - s) < micro:
                ready = after(out, hops[step - 1, s]) if (step - 1, s) in hops else out
                hops[step, s] = link(ready, s, s - 1)

    first_grads = jnp.concatenate(outs[2 * last :])
    noise_grad = matmul_nt(input_full, first_grads).astype(LOW)
    pieces = noise_grad.reshape(SEC, emb_part, all_tokens)
    noise_grad = pieces[0]
    for s in TURNS:
        noise_grad = jnp.where(section == s, turn(pieces[s], s), noise_grad)
    embed_grad = embed_sum(
        (row * (vocab // 16)).reshape(1), all_ids, gather_plane(noise_grad), vocab // 16
    ).T
    noise_out = noise_grad.reshape(emb_part, micro, tokens).transpose(1, 2, 0).astype(WIDE)

    grad_nexts, grads, gain_grads = totals
    gain_grad = jnp.sum(gain_grads[:, 0], axis=0)
    flat = lambda v: v.reshape(all_tokens, v.shape[-1])
    normed, grad_nexts, grads, saved = flat(normeds), flat(grad_nexts), flat(grads), flat(saved)
    tail = jnp.where(is_mlp, normed, saved[:, 3 * width :])
    order = lambda values, which, unit: jnp.where(which == 0, values, by_second(values, unit))
    odd = (1, 3)

    def lead_block(which, spot, by):
        block = (spot + by) % 4
        former = block_of(order(normed, which, 64), block, 4)
        latter = block_of(order(jnp.where(which == 0, normed, tail), which, 64), block, 4)
        part = lax.dynamic_slice_in_dim(grads, which * 2 * width, 2 * width, 1)
        return jnp.concatenate(
            (matmul_tn(former, part[:, :width]), matmul_tn(latter, part[:, width:])), axis=1
        )

    def down_block(which, spot, by):
        block = (spot + by) % 4
        part = lax.dynamic_slice_in_dim(saved, which * half_rows, half_rows, 1)
        return matmul_tn(block_of(order(part, which, 128), block, 4), grad_nexts)

    input_grad = matmul_tn(embedded, first_grads).reshape(SEC, 16, 4, width)
    input_grad = input_grad.transpose(1, 0, 2, 3).reshape(16, 16, width)
    readout_grad = readout_grad.reshape(16, 16, width)
    vectors = jnp.concatenate(
        (
            gain_grad.reshape(16, 64),
            final_gain_grad.reshape(SEC, 16, 16).transpose(1, 0, 2).reshape(16, 64),
            jnp.zeros((16, width - 128), WIDE),
        ),
        axis=1,
    )
    small = jnp.concatenate(
        (
            jnp.where(section == 0, input_grad, readout_grad),
            vectors[:, None],
            jnp.zeros((16, 15, width), WIDE),
        ),
        axis=1,
    ).reshape(NX, NY, 32, GRP, width // GRP)
    smalls = (small, small.swapaxes(0, 1))

    def small_block(which, spot, by):
        part = jnp.where(which == 0, smalls[0][:, :, :, 0], smalls[1][:, :, :, 1])
        part = lax.dynamic_index_in_dim(part, (spot + by) % 4, 0, False)
        return part.reshape(NY * 32, width // GRP)

    def summed(maker, sections=range(SEC)):
        def block_for(by):
            other = maker(1 - core, second_at, by).astype(LOW)
            got = swap_cores(other, sections).astype(WIDE)
            return (maker(core, first_at, by) + got).astype(LOW)

        return reduce_plane(block_for, second_at, sections)

    both = lambda mine, other: jnp.where(
        core == 0,
        jnp.concatenate((mine, other), axis=1),
        jnp.concatenate((other, mine), axis=1),
    )
    lead_part = summed(lead_block)
    lead_out = both(lead_part, swap_cores(lead_part)).astype(WIDE)

    down_part = summed(down_block, odd)
    down_other = swap_cores(down_part, odd)
    upper_part = jnp.where(core == 0, down_part, down_other)
    lower_part = jnp.where(core == 0, down_other, down_part)
    upper_half = lax.dynamic_slice_in_dim(upper_part, core * (width // 2), width // 2, 1)
    upper_half = jnp.where(section == 0, link(upper_half, 1, 0), link(upper_half, 3, 2))
    down_out = jnp.where(is_mlp, lower_part, both(upper_half, swap_cores(upper_half))).astype(WIDE)

    small_part = summed(small_block)
    small = both(small_part, swap_cores(small_part))
    gain_out = small[16, :64].astype(WIDE)
    input_rows = small[:16].reshape(SEC, 4, width)
    readout_rows = small[:16].reshape(64, SEC, 64)
    final_rows = small[16, 64:128].reshape(SEC, 16)

    def sent_part(by):
        target = (section + by) % SEC
        readouts = lax.dynamic_index_in_dim(readout_rows, target, 1, False).reshape(4, width)
        finals = lax.dynamic_index_in_dim(final_rows, target, 0, False)
        finals = jnp.pad(finals, (0, width - 16))[None]
        inputs = lax.dynamic_index_in_dim(input_rows, target, 0, False)
        return jnp.concatenate((jnp.where(section == 0, inputs, readouts), finals))

    input_out = input_rows[0]
    readout_out = readout_rows[:, last]
    final_out = final_rows[last]
    for by in TURNS:
        part = turn(sent_part(by), by)
        input_out = jnp.where(section == by, part[:4], input_out)
        here = section == (last + by) % SEC
        readout_out = jnp.where(here, part[:4].reshape(64, 64), readout_out)
        final_out = jnp.where(here, part[4, :16], final_out)

    head_out = head_grad.astype(WIDE) + swap_cores(head_grad).astype(WIDE)
    return (
        noise_out[:, None],
        embed_grad,
        input_out.astype(WIDE),
        gain_out[None],
        lead_out[None],
        down_out[None],
        final_out.astype(WIDE),
        readout_out.astype(WIDE),
        head_out,
    )


def solution(mesh):
    in_specs = (
        P(None, ("group", "row"), None),
        P(None, ("group", "row"), None),
        P(None, ("group", "row"), None, "section"),
        P(None, "section"),
        P("section", None),
        P("section", None),
        P("section", None, None),
        P("section", None, None),
        P(),
        P(None, "section"),
        P("section", None),
    )
    out_specs = (
        P(None, ("group", "row"), None, "section"),
        P("row", "section"),
        P(("section", "row"), None),
        P("section", "row"),
        P("section", "row", None),
        P("section", "row", None),
        P(("section", "row")),
        P("row", "section"),
        P(("section", "row"), None),
    )
    return jax.shard_map(local, mesh=mesh, in_specs=in_specs, out_specs=out_specs, check_vma=False)
```

time: 1450 us -> 713 us (0.49)
  waiting for transfers between devices: 812 us -> 95.9 us
  matrix products: 208 us -> 32.5 us
  Pallas kernels: 0 us -> 156 us
  blocking collectives: 123 us -> 0 us
  starting transfers between devices: 70 us -> 179 us
  local copies, waits for them, and re-layouts: 54 us -> 158 us
  loops' own time: 57.5 us -> 0 us
  other arithmetic: 96.9 us -> 64.6 us
    psum x5 -> x0, waiting for transfers between devices: 244 us -> none  [the longest x2 168 us: from_root(): return lax.psum(jnp.where(mine, shard, jnp.zeros_like(shard)), axis)]
    reduce_scatter x5 -> x0, waiting for transfers between devices: 241 us -> none  [the longest x1 87.2 us: local(): lax.psum_scatter(pieces[0].astype(jnp.bfloat16), 'row', scatter_dimension...]
    pallas_call x0 -> x23, Pallas kernels: none -> 156 us  [the longest x10 82.3 us: backward_stage(): pl.pallas_call(backward_kernel, out_shape=[jax.ShapeDtypeStruct(grad.shap...]
    unnamed x15 -> x2, waiting for transfers between devices: 155 us -> 0.02 us
    ppermute x14 -> x102, starting transfers between devices: 67.1 us -> 179 us  [route(): return lax.ppermute(value, ALL, pairs)]
    unnamed x2 -> x0, blocking collectives: 92.1 us -> none
    unnamed x93 -> x277, local copies, waits for them, and re-layouts: 19.7 us -> 107 us
    dot_general x11 -> x26, matrix products: 114 us -> 28.8 us  [matmul_tn(): lax.dot_general(former, latter, (((0,), (0,)), ((), ())), preferred_eleme...]
  transfers between devices with their start and end apart: 27 -> 103, of which waited for: 24 -> 20; matrix products, arithmetic and copies ran while one was open for 11% -> 22% of each run, Pallas kernels for 0% -> 17%
where the time goes in v1:
time: 713 us; the launch traced here: 703 us
  starting transfers between devices  179 us (25%)
  local copies, waits for them, and re-layouts  158 us (22%)
  Pallas kernels  156 us (22%)
  waiting for transfers between devices  95.9 us (13%)
  other arithmetic  64.6 us (9%)
  matrix products  32.5 us (5%)
  between operations  17.1 us (2%)
    ppermute x102, starting transfers between devices, route(): return lax.ppermute(value, ALL, pairs)  179 us
    unnamed x277, local copies, waits for them, and re-layouts  107 us
    ppermute x102, waiting for transfers between devices, route(): return lax.ppermute(value, ALL, pairs)  95.9 us
    pallas_call x10, Pallas kernels, backward_stage(): pl.pallas_call(backward_kernel, out_shape=[jax.ShapeDtypeStruct(grad.shap...  82.3 us
    pallas_call x10, Pallas kernels, forward_stage(): pl.pallas_call(forward_kernel, out_shape=[jax.ShapeDtypeStruct(entry.shap...  43 us
    dot_general x26, matrix products, matmul_tn(): lax.dot_general(former, latter, (((0,), (0,)), ((), ())), preferred_eleme...  28.8 us
    pallas_call x1, Pallas kernels, embed_sum(): pl.pallas_call(embed_kernel, out_shape=jax.ShapeDtypeStruct((parts, rows)...  15.5 us
  transfers between devices with their start and end apart: 103, of which 20 were waited for; matrix products, arithmetic and copies ran while one was open for 22% of the time, Pallas kernels for 17%

profile of v1, /device:TPU:103, one launch (start us, length us, event | category | flops | bytes accessed | tf_op | source)
XLA Modules:
  0.0 702.7 jit_solution(15163657465380739466)
XLA Ops:
  17.9 6.0 collective-permute-done.7
  50.8 8.4 %copy.193 = bf16[32000,64]{1,0:T(8,128)(2,1)} copy(bf16[32000,64]{0,1:T(8,128)(2,1)} %param.14) | data formatting | bytes 8192000 | tf_op args[3]
  59.5 5.4 gather_fusion
  128.2 4.9 collective-permute-start.54
  151.5 15.4 %collective-permute-done.16 = bf16[128,1024]{1,0:T(8,128)(2,1)S(1)} collective-permute-done((bf16[128,1024]{1,0:T(8,128)(2,1)S(1)}, bf16[128,1024]{1,0:T(8,128)(2,1)S(1)}, u32[]{:S(2)}, u32[]{:S(2)}) %collective-permute-start.16) | collective-permute-done | bytes 262176 | tf_op jit(solution)/shard_map/ppermute | solution.py:497
  168.9 7.3 %forward_stage.16 = (bf16[128,1024]{1,0:T(8,128)(2,1)S(1)}, bf16[4,128,1024]{2,1,0:T(8,128)(2,1)S(1)}, bf16[4,128,1024]{2,1,0:T(8,128)(2,1)S(1)}, bf16[4,128,4096]{2,1,0:T(8,128)(2,1)S(1)}, f32[4,128,4096]{2,1,0:T(8,128)S(1)}) custom-call(s32[2]{0:T(128)S(1)} %pad_add_fusion.4.role_ref, ...), custom_call_target="tpu_custom_call", output_to_operand_aliasing={{1}: (7, {}), {2}: (8, {}), {3}: (9, {}), {4}: (10, {})} | custom-call | flops 2147483648 | bytes 20971520 | tf_op jit(solution)/shard_map/forward_stage/pallas_call | solution.py:210
  176.2 14.2 %collective-permute-done.20 = bf16[128,1024]{1,0:T(8,128)(2,1)S(1)} collective-permute-done((bf16[128,1024]{1,0:T(8,128)(2,1)S(1)}, bf16[128,1024]{1,0:T(8,128)(2,1)S(1)}, u32[]{:S(2)}, u32[]{:S(2)}) %collective-permute-start.20) | collective-permute-done | bytes 262176 | tf_op jit(solution)/shard_map/ppermute | solution.py:497
  191.7 7.7 %forward_stage.17 = (bf16[128,1024]{1,0:T(8,128)(2,1)S(1)}, bf16[4,128,1024]{2,1,0:T(8,128)(2,1)S(1)}, bf16[4,128,1024]{2,1,0:T(8,128)(2,1)S(1)}, bf16[4,128,4096]{2,1,0:T(8,128)(2,1)S(1)}, f32[4,128,4096]{2,1,0:T(8,128)S(1)}) custom-call(s32[2]{0:T(128)S(1)} %copy-done.40, ...), custom_call_target="tpu_custom_call", output_to_operand_aliasing={{1}: (7, {}), {2}: (8, {}), {3}: (9, {}), {4}: (10, {})} | custom-call | flops 2147483648 | bytes 20971520 | tf_op jit(solution)/shard_map/forward_stage/pallas_call | solution.py:210
  208.4 4.9 copy.254
  222.3 7.3 %forward_stage.18 = (bf16[128,1024]{1,0:T(8,128)(2,1)S(1)}, bf16[4,128,1024]{2,1,0:T(8,128)(2,1)S(1)}, bf16[4,128,1024]{2,1,0:T(8,128)(2,1)S(1)}, bf16[4,128,4096]{2,1,0:T(8,128)(2,1)S(1)}, f32[4,128,4096]{2,1,0:T(8,128)S(1)}) custom-call(s32[2]{0:T(128)S(1)} %copy-done.38, ...), custom_call_target="tpu_custom_call", output_to_operand_aliasing={{1}: (7, {}), {2}: (8, {}), {3}: (9, {}), {4}: (10, {})} | custom-call | flops 2147483648 | bytes 20971520 | tf_op jit(solution)/shard_map/forward_stage/pallas_call | solution.py:210
  229.5 11.4 %forward_stage.19 = (bf16[128,1024]{1,0:T(8,128)(2,1)S(1)}, bf16[4,128,1024]{2,1,0:T(8,128)(2,1)S(1)}, bf16[4,128,1024]{2,1,0:T(8,128)(2,1)S(1)}, bf16[4,128,4096]{2,1,0:T(8,128)(2,1)S(1)}, f32[4,128,4096]{2,1,0:T(8,128)S(1)}) custom-call(s32[2]{0:T(128)S(1)} %copy-done.39, ...), custom_call_target="tpu_custom_call", output_to_operand_aliasing={{1}: (7, {}), {2}: (8, {}), {3}: (9, {}), {4}: (10, {})} | custom-call | flops 2147483648 | bytes 20971520 | tf_op jit(solution)/shard_map/forward_stage/pallas_call | solution.py:210
  268.6 5.6 head_stats.1
  293.7 9.3 %head_grads.1 = (bf16[8000,256]{1,0:T(8,128)(2,1)S(1)}, f32[512,256]{1,0:T(8,128)S(1)}) custom-call(s32[1]{0:T(128)} %bitcast.39.base_ref, bf16[512,256]{1,0:T(8,128)(2,1)S(1)} %copy-done.33, bf16[8000,256]{1,0:T(8,128)(2,1)S(1)} %copy-done.48, f32[1,512]{1,0:T(1,128)S(1)} %bitcast.294, s32[1,512]{1,0:T(1,128)S(1)} %bitcast.293), custom_call_target="tpu_custom_call" | custom-call | flops 6291456000 | bytes 9437184 | tf_op jit(solution)/shard_map/head_grads/pallas_call | solution.py:467
  308.8 9.5 %collective-permute-done.30 = bf16[512,256]{1,0:T(8,128)(2,1)S(1)} collective-permute-done((bf16[512,256]{1,0:T(8,128)(2,1)S(1)}, bf16[512,256]{1,0:T(8,128)(2,1)S(1)}, u32[]{:S(2)}, u32[]{:S(2)}) %collective-permute-start.30) | collective-permute-done | bytes 262176 | tf_op jit(solution)/shard_map/ppermute | solution.py:497
  324.6 10.7 %backward_stage.10 = (bf16[128,1024]{1,0:T(8,128)(2,1)S(1)}, bf16[4,128,1024]{2,1,0:T(8,128)(2,1)S(1)}, bf16[4,128,4096]{2,1,0:T(8,128)(2,1)S(1)}, f32[4,8,1024]{2,1,0:T(8,128)S(1)}) custom-call(s32[2]{0:T(128)S(1)} %copy-done.37, bf16[128,1024]{1,0:T(8,128)(2,1)S(1)} %get-tuple-element.280.grad_ref, ...), custom_call_target="tpu_custom_call", output_to_operand_aliasing={{1}: (10, {}), {2}: (11, {}), {3}: (12, {})} | custom-call | flops 2147483648 | bytes 20971520 | tf_op jit(solution)/shard_map/backward_stage/pallas_call | solution.py:375
  338.0 11.5 %backward_stage.11 = (bf16[128,1024]{1,0:T(8,128)(2,1)}, bf16[4,128,1024]{2,1,0:T(8,128)(2,1)S(1)}, bf16[4,128,4096]{2,1,0:T(8,128)(2,1)S(1)}, f32[4,8,1024]{2,1,0:T(8,128)S(1)}) custom-call(s32[2]{0:T(128)S(1)} %copy-done.35, bf16[128,1024]{1,0:T(8,128)(2,1)S(1)} %get-tuple-element.279.grad_ref, ...), custom_call_target="tpu_custom_call", output_to_operand_aliasing={{1}: (10, {}), {2}: (11, {}), {3}: (12, {})} | custom-call | flops 2147483648 | bytes 20971520 | tf_op jit(solution)/shard_map/backward_stage/pallas_call | solution.py:375
  369.6 11.6 %backward_stage.12 = (bf16[128,1024]{1,0:T(8,128)(2,1)}, bf16[4,128,1024]{2,1,0:T(8,128)(2,1)S(1)}, bf16[4,128,4096]{2,1,0:T(8,128)(2,1)S(1)}, f32[4,8,1024]{2,1,0:T(8,128)S(1)}) custom-call(s32[2]{0:T(128)S(1)} %copy-done.36, bf16[128,1024]{1,0:T(8,128)(2,1)S(1)} %get-tuple-element.278.grad_ref, ...), custom_call_target="tpu_custom_call", output_to_operand_aliasing={{1}: (10, {}), {2}: (11, {}), {3}: (12, {})} | custom-call | flops 2147483648 | bytes 20971520 | tf_op jit(solution)/shard_map/backward_stage/pallas_call | solution.py:375
  384.7 5.1 collective-permute-start.35
  403.2 10.8 %backward_stage.13 = (bf16[128,1024]{1,0:T(8,128)(2,1)S(1)}, bf16[4,128,1024]{2,1,0:T(8,128)(2,1)S(1)}, bf16[4,128,4096]{2,1,0:T(8,128)(2,1)S(1)}, f32[4,8,1024]{2,1,0:T(8,128)S(1)}) custom-call(s32[2]{0:T(128)S(1)} %get-tuple-element.334.role_ref, bf16[128,1024]{1,0:T(8,128)(2,1)S(1)} %copy-done.30, ...), custom_call_target="tpu_custom_call", output_to_operand_aliasing={{1}: (10, {}), {2}: (11, {}), {3}: (12, {})} | custom-call | flops 2147483648 | bytes 20971520 | tf_op jit(solution)/shard_map/backward_stage/pallas_call | solution.py:375
  421.9 6.9 backward_stage.15
  430.2 6.9 backward_stage.16
  437.9 7.7 %backward_stage.17 = (bf16[128,1024]{1,0:T(8,128)(2,1)S(1)}, bf16[4,128,1024]{2,1,0:T(8,128)(2,1)S(1)}, bf16[4,128,4096]{2,1,0:T(8,128)(2,1)S(1)}, f32[4,8,1024]{2,1,0:T(8,128)S(1)}) custom-call(s32[2]{0:T(128)S(1)} %copy-done.43, ...), custom_call_target="tpu_custom_call", output_to_operand_aliasing={{1}: (10, {}), {2}: (11, {}), {3}: (12, {})} | custom-call | flops 2147483648 | bytes 20971520 | tf_op jit(solution)/shard_map/backward_stage/pallas_call | solution.py:375
  446.3 7.5 %backward_stage.18 = (bf16[128,1024]{1,0:T(8,128)(2,1)S(1)}, bf16[4,128,1024]{2,1,0:T(8,128)(2,1)S(1)}, bf16[4,128,4096]{2,1,0:T(8,128)(2,1)S(1)}, f32[4,8,1024]{2,1,0:T(8,128)S(1)}) custom-call(s32[2]{0:T(128)S(1)} %copy-done.45, ...), custom_call_target="tpu_custom_call", output_to_operand_aliasing={{1}: (10, {}), {2}: (11, {}), {3}: (12, {})} | custom-call | flops 2147483648 | bytes 20971520 | tf_op jit(solution)/shard_map/backward_stage/pallas_call | solution.py:375
  453.9 7.5 %backward_stage.19 = (bf16[128,1024]{1,0:T(8,128)(2,1)S(1)}, bf16[4,128,1024]{2,1,0:T(8,128)(2,1)S(1)}, bf16[4,128,4096]{2,1,0:T(8,128)(2,1)S(1)}, f32[4,8,1024]{2,1,0:T(8,128)S(1)}) custom-call(s32[2]{0:T(128)S(1)} %copy-done.46, ...), custom_call_target="tpu_custom_call", output_to_operand_aliasing={{1}: (10, {}), {2}: (11, {}), {3}: (12, {})} | custom-call | flops 2147483648 | bytes 20971520 | tf_op jit(solution)/shard_map/backward_stage/pallas_call | solution.py:375
  501.4 16.7 %collective-permute-start.45 = (bf16[64,512]{1,0:T(8,128)(2,1)S(1)}, bf16[64,512]{1,0:T(8,128)(2,1)S(1)}, u32[]{:S(2)}, u32[]{:S(2)}) collective-permute-start(bf16[64,512]{1,0:T(8,128)(2,1)S(1)} %get-tuple-element.296), channel_id=1, source_target_pairs={{0,64},{1,65},{2,66},{3,67},{4,68},{5,69},{6,70},{7,71},{8,72},{9,... | collective-permute-start | bytes 196616 | tf_op jit(solution)/shard_map/ppermute | solution.py:497
  518.1 11.0 %collective-permute-start.46 = (bf16[64,512]{1,0:T(8,128)(2,1)S(1)}, bf16[64,512]{1,0:T(8,128)(2,1)S(1)}, u32[]{:S(2)}, u32[]{:S(2)}) collective-permute-start(bf16[64,512]{1,0:T(8,128)(2,1)S(1)} %get-tuple-element.295), channel_id=1, source_target_pairs={{0,96},{1,97},{2,98},{3,99},{4,100},{5,101},{6,102},{7,103},{8,104... | collective-permute-start | bytes 196616 | tf_op jit(solution)/shard_map/ppermute | solution.py:497
  603.4 8.9 %collective-permute-done.59 = bf16[4,64,512]{2,1,0:T(8,128)(2,1)S(1)} collective-permute-done((bf16[4,64,512]{2,1,0:T(8,128)(2,1)}, bf16[4,64,512]{2,1,0:T(8,128)(2,1)S(1)}, u32[]{:S(2)}, u32[]{:S(2)}) %collective-permute-start.59) | collective-permute-done | bytes 262176 | tf_op jit(solution)/shard_map/ppermute | solution.py:497
  614.7 7.7 %collective-permute-done.60 = bf16[4,64,512]{2,1,0:T(8,128)(2,1)S(1)} collective-permute-done((bf16[4,64,512]{2,1,0:T(8,128)(2,1)}, bf16[4,64,512]{2,1,0:T(8,128)(2,1)S(1)}, u32[]{:S(2)}, u32[]{:S(2)}) %collective-permute-start.60) | collective-permute-done | bytes 262176 | tf_op jit(solution)/shard_map/ppermute | solution.py:497
  625.2 5.4 collective-permute-done.91
  644.6 7.3 %collective-permute-done.80 = bf16[256,2048]{1,0:T(8,128)(2,1)S(1)} collective-permute-done((bf16[256,2048]{1,0:T(8,128)(2,1)S(1)}, bf16[256,2048]{1,0:T(8,128)(2,1)S(1)}, u32[]{:S(2)}, u32[]{:S(2)}) %collective-permute-start.80) | collective-permute-done | bytes 1048608 | tf_op jit(solution)/shard_map/ppermute | solution.py:497
  663.5 7.4 %collective-permute-start.97 = (bf16[128,1024]{1,0:T(8,128)(2,1)S(1)}, bf16[128,1024]{1,0:T(8,128)(2,1)S(1)}, u32[]{:S(2)}, u32[]{:S(2)}) collective-permute-start(bf16[128,1024]{1,0:T(8,128)(2,1)S(1)} %add_convert_fusion.4), channel_id=1, source_target_pairs={{32,48},{33,49},{34,50},{35,51},{36,52},{37,53},{38,54},{39,55},{4... | collective-permute-start | bytes 786440 | tf_op jit(solution)/shard_map/ppermute | solution.py:497
  676.6 15.5 %embed_sum.1 = f32[64,2000]{1,0:T(8,128)} custom-call(s32[1]{0:T(128)} %bitcast.63.base_ref, s32[16384,1]{1,0:T(8,128)S(1)} %bitcast.285, bf16[32,64,512]{2,1,0:T(8,128)(2,1)} %constant_dynamic-update-slice_fusion.11.grad_ref), custom_call_target="tpu_custom_call" | custom-call | flops 16777216000 | bytes 12582912 | tf_op jit(solution)/shard_map/embed_sum/pallas_call | solution.py:578
  (686 shorter events, 402.3 us)
Async XLA Ops:
  7.2 685.1 %reduce-scatter.4.cloned.1.call-start = ((), (), s32[]{:S(2)}) async-start(), calls=%async_computation.1 | async-start | bytes 4386816
  12.1 52.8 %collective-permute-start = (bf16[128,1024]{1,0:T(8,128)(2,1)}, bf16[128,1024]{1,0:T(8,128)(2,1)S(1)}, u32[]{:S(2)}, u32[]{:S(2)}) collective-permute-start(bf16[128,1024]{1,0:T(8,128)(2,1)} %pad_maximum_fusion.8), channel_id=1, source_target_pairs={{0,32},{1,33},{2,34},{3,35},{4,36},{5,37},{6,38},{7,39},{8,40},{9,... | collective-permute-start | bytes 786440 | tf_op jit(solution)/shard_map/ppermute | solution.py:497
  14.1 50.8 %collective-permute-start.1 = (bf16[128,1024]{1,0:T(8,128)(2,1)}, bf16[128,1024]{1,0:T(8,128)(2,1)}, u32[]{:S(2)}, u32[]{:S(2)}) collective-permute-start(bf16[128,1024]{1,0:T(8,128)(2,1)} %pad_maximum_fusion.8), channel_id=1, source_target_pairs={{0,64},{1,65},{2,66},{3,67},{4,68},{5,69},{6,70},{7,71},{8,72},{9,... | collective-permute-start | bytes 786440 | tf_op jit(solution)/shard_map/ppermute | solution.py:497
  37.0 28.0 %collective-permute-start.2 = (bf16[128,1024]{1,0:T(8,128)(2,1)}, bf16[128,1024]{1,0:T(8,128)(2,1)}, u32[]{:S(2)}, u32[]{:S(2)}) collective-permute-start(bf16[128,1024]{1,0:T(8,128)(2,1)} %pad_maximum_fusion.8), channel_id=1, source_target_pairs={{0,96},{1,97},{2,98},{3,99},{4,100},{5,101},{6,102},{7,103},{8,104... | collective-permute-start | bytes 786440 | tf_op jit(solution)/shard_map/ppermute | solution.py:497
  44.8 31.6 %collective-permute-start.11 = (bf16[1024,1024]{1,0:T(8,128)(2,1)S(1)}, bf16[1024,1024]{1,0:T(8,128)(2,1)}, u32[]{:S(2)}, u32[]{:S(2)}) collective-permute-start(bf16[1024,1024]{1,0:T(8,128)(2,1)S(1)} %bitcast.299), channel_id=1, source_target_pairs={{0,16},{1,17},{2,18},{3,19},{4,20},{5,21},{6,22},{7,23},{8,24},{9,... | collective-permute-start | bytes 6291464 | tf_op jit(solution)/shard_map/ppermute | solution.py:497
  107.0 21.1 %collective-permute-start.51 = (s32[4,512]{1,0:T(4,128)S(1)}, s32[4,512]{1,0:T(4,128)S(1)}, u32[]{:S(2)}, u32[]{:S(2)}) collective-permute-start(s32[4,512]{1,0:T(4,128)S(1)} %pad_add_fusion), channel_id=1, source_target_pairs={{0,1},{1,2},{2,3},{3,0},{4,5},{5,6},{6,7},{7,4},{8,9},{9,10},{10,1... | collective-permute-start | bytes 24584 | tf_op jit(solution)/shard_map/ppermute | solution.py:497
  107.1 21.1 %collective-permute-start.52 = (s32[4,512]{1,0:T(4,128)S(1)}, s32[4,512]{1,0:T(4,128)S(1)}, u32[]{:S(2)}, u32[]{:S(2)}) collective-permute-start(s32[4,512]{1,0:T(4,128)S(1)} %pad_add_fusion), channel_id=1, source_target_pairs={{0,3},{1,0},{2,1},{3,2},{4,7},{5,4},{6,5},{7,6},{8,11},{9,8},{10,9... | collective-permute-start | bytes 24584 | tf_op jit(solution)/shard_map/ppermute | solution.py:497
  128.2 80.1 %collective-permute-start.54 = (s32[16,512]{1,0:T(8,128)S(1)}, s32[16,512]{1,0:T(8,128)S(1)}, u32[]{:S(2)}, u32[]{:S(2)}) collective-permute-start(s32[16,512]{1,0:T(8,128)S(1)} %concatenate.130), channel_id=1, source_target_pairs={{0,16},{1,17},{2,18},{3,19},{4,20},{5,21},{6,22},{7,23},{8,24},{9,... | collective-permute-start | bytes 98312 | tf_op jit(solution)/shard_map/ppermute | solution.py:497
  146.1 20.7 %collective-permute-start.16 = (bf16[128,1024]{1,0:T(8,128)(2,1)S(1)}, bf16[128,1024]{1,0:T(8,128)(2,1)S(1)}, u32[]{:S(2)}, u32[]{:S(2)}) collective-permute-start(bf16[128,1024]{1,0:T(8,128)(2,1)S(1)} %get-tuple-element.148), channel_id=1, source_target_pairs={{64,96},{65,97},{66,98},{67,99},{68,100},{69,101},{70,102},{71,103... | collective-permute-start | bytes 786440 | tf_op jit(solution)/shard_map/ppermute | solution.py:497
  147.4 20.7 %collective-permute-start.18 = (bf16[128,1024]{1,0:T(8,128)(2,1)S(1)}, bf16[128,1024]{1,0:T(8,128)(2,1)S(1)}, u32[]{:S(2)}, u32[]{:S(2)}) collective-permute-start(bf16[128,1024]{1,0:T(8,128)(2,1)S(1)} %get-tuple-element.148), channel_id=1, source_target_pairs={{32,64},{33,65},{34,66},{35,67},{36,68},{37,69},{38,70},{39,71},{4... | collective-permute-start | bytes 786440 | tf_op jit(solution)/shard_map/ppermute | solution.py:497
  166.9 23.5 %collective-permute-start.20 = (bf16[128,1024]{1,0:T(8,128)(2,1)S(1)}, bf16[128,1024]{1,0:T(8,128)(2,1)S(1)}, u32[]{:S(2)}, u32[]{:S(2)}) collective-permute-start(bf16[128,1024]{1,0:T(8,128)(2,1)S(1)} %get-tuple-element.161), channel_id=1, source_target_pairs={{64,96},{65,97},{66,98},{67,99},{68,100},{69,101},{70,102},{71,103... | collective-permute-start | bytes 786440 | tf_op jit(solution)/shard_map/ppermute | solution.py:497
  168.2 23.5 %collective-permute-start.21 = (bf16[128,1024]{1,0:T(8,128)(2,1)S(1)}, bf16[128,1024]{1,0:T(8,128)(2,1)S(1)}, u32[]{:S(2)}, u32[]{:S(2)}) collective-permute-start(bf16[128,1024]{1,0:T(8,128)(2,1)S(1)} %get-tuple-element.161), channel_id=1, source_target_pairs={{32,64},{33,65},{34,66},{35,67},{36,68},{37,69},{38,70},{39,71},{4... | collective-permute-start | bytes 786440 | tf_op jit(solution)/shard_map/ppermute | solution.py:497
  204.6 25.0 %collective-permute-start.23 = (bf16[128,1024]{1,0:T(8,128)(2,1)S(1)}, bf16[128,1024]{1,0:T(8,128)(2,1)}, u32[]{:S(2)}, u32[]{:S(2)}) collective-permute-start(bf16[128,1024]{1,0:T(8,128)(2,1)S(1)} %get-tuple-element.173), channel_id=1, source_target_pairs={{64,96},{65,97},{66,98},{67,99},{68,100},{69,101},{70,102},{71,103... | collective-permute-start | bytes 786440 | tf_op jit(solution)/shard_map/ppermute | solution.py:497
  244.3 23.2 %collective-permute-start.24 = (bf16[512,256]{1,0:T(8,128)(2,1)}, bf16[512,256]{1,0:T(8,128)(2,1)}, u32[]{:S(2)}, u32[]{:S(2)}) collective-permute-start(bf16[512,256]{1,0:T(8,128)(2,1)} %convolution_convert_fusion.14), channel_id=1, source_target_pairs={{96,64},{97,65},{98,66},{99,67},{100,68},{101,69},{102,70},{103,71... | collective-permute-start | bytes 786440 | tf_op jit(solution)/shard_map/ppermute | solution.py:497
  247.2 20.3 %collective-permute-start.25 = (bf16[512,256]{1,0:T(8,128)(2,1)}, bf16[512,256]{1,0:T(8,128)(2,1)}, u32[]{:S(2)}, u32[]{:S(2)}) collective-permute-start(bf16[512,256]{1,0:T(8,128)(2,1)} %convolution_convert_fusion.14), channel_id=1, source_target_pairs={{96,32},{97,33},{98,34},{99,35},{100,36},{101,37},{102,38},{103,39... | collective-permute-start | bytes 786440 | tf_op jit(solution)/shard_map/ppermute | solution.py:497
  383.3 34.2 %collective-permute-start.36 = (bf16[128,1024]{1,0:T(8,128)(2,1)}, bf16[128,1024]{1,0:T(8,128)(2,1)}, u32[]{:S(2)}, u32[]{:S(2)}) collective-permute-start(bf16[128,1024]{1,0:T(8,128)(2,1)} %get-tuple-element.195), channel_id=1, source_target_pairs={{64,32},{65,33},{66,34},{67,35},{68,36},{69,37},{70,38},{71,39},{7... | collective-permute-start | bytes 786440 | tf_op jit(solution)/shard_map/ppermute | solution.py:497
  384.7 29.3 %collective-permute-start.35 = (bf16[128,1024]{1,0:T(8,128)(2,1)}, bf16[128,1024]{1,0:T(8,128)(2,1)}, u32[]{:S(2)}, u32[]{:S(2)}) collective-permute-start(bf16[128,1024]{1,0:T(8,128)(2,1)} %get-tuple-element.195), channel_id=1, source_target_pairs={{96,64},{97,65},{98,66},{99,67},{100,68},{101,69},{102,70},{103,71... | collective-permute-start | bytes 786440 | tf_op jit(solution)/shard_map/ppermute | solution.py:497
  491.5 48.9 %collective-permute-start.63 = (bf16[128,512]{1,0:T(8,128)(2,1)S(1)}, bf16[128,512]{1,0:T(8,128)(2,1)S(1)}, u32[]{:S(2)}, u32[]{:S(2)}) collective-permute-start(bf16[128,512]{1,0:T(8,128)(2,1)S(1)} %bitcast.316), channel_id=1, source_target_pairs={{0,16},{1,17},{2,18},{3,19},{4,20},{5,21},{6,22},{7,23},{8,24},{9,... | collective-permute-start | bytes 393224 | tf_op jit(solution)/shard_map/ppermute | solution.py:497
  494.5 46.3 %collective-permute-start.65 = (bf16[128,512]{1,0:T(8,128)(2,1)S(1)}, bf16[128,512]{1,0:T(8,128)(2,1)S(1)}, u32[]{:S(2)}, u32[]{:S(2)}) collective-permute-start(bf16[128,512]{1,0:T(8,128)(2,1)S(1)} %bitcast.315), channel_id=1, source_target_pairs={{0,16},{1,17},{2,18},{3,19},{4,20},{5,21},{6,22},{7,23},{8,24},{9,... | collective-permute-start | bytes 393224 | tf_op jit(solution)/shard_map/ppermute | solution.py:497
  501.4 33.4 %collective-permute-start.45 = (bf16[64,512]{1,0:T(8,128)(2,1)S(1)}, bf16[64,512]{1,0:T(8,128)(2,1)S(1)}, u32[]{:S(2)}, u32[]{:S(2)}) collective-permute-start(bf16[64,512]{1,0:T(8,128)(2,1)S(1)} %get-tuple-element.296), channel_id=1, source_target_pairs={{0,64},{1,65},{2,66},{3,67},{4,68},{5,69},{6,70},{7,71},{8,72},{9,... | collective-permute-start | bytes 196616 | tf_op jit(solution)/shard_map/ppermute | solution.py:497
  536.1 86.4 %collective-permute-start.87 = (bf16[512,1024]{1,0:T(8,128)(2,1)}, bf16[512,1024]{1,0:T(8,128)(2,1)}, u32[]{:S(2)}, u32[]{:S(2)}) collective-permute-start(bf16[512,1024]{1,0:T(8,128)(2,1)} %convolution_convert_fusion.4), channel_id=1, source_target_pairs={{32,48},{33,49},{34,50},{35,51},{36,52},{37,53},{38,54},{39,55},{4... | collective-permute-start | bytes 3145736 | tf_op jit(solution)/shard_map/ppermute | solution.py:497
  546.4 41.9 %collective-permute-start.77 = (bf16[256,2048]{1,0:T(8,128)(2,1)}, bf16[256,2048]{1,0:T(8,128)(2,1)}, u32[]{:S(2)}, u32[]{:S(2)}) collective-permute-start(bf16[256,2048]{1,0:T(8,128)(2,1)} %pad_maximum_fusion.3), channel_id=1, source_target_pairs={{0,16},{1,17},{2,18},{3,19},{4,20},{5,21},{6,22},{7,23},{8,24},{9,... | collective-permute-start | bytes 3145736 | tf_op jit(solution)/shard_map/ppermute | solution.py:497
  590.7 21.8 %collective-permute-start.81 = (bf16[256,2048]{1,0:T(8,128)(2,1)S(1)}, bf16[256,2048]{1,0:T(8,128)(2,1)S(1)}, u32[]{:S(2)}, u32[]{:S(2)}) collective-permute-start(bf16[256,2048]{1,0:T(8,128)(2,1)S(1)} %copy-done.72), channel_id=1, source_target_pairs={{0,16},{1,17},{2,18},{3,19},{4,20},{5,21},{6,22},{7,23},{8,24},{9,... | collective-permute-start | bytes 3145736 | tf_op jit(solution)/shard_map/ppermute | solution.py:497
  593.4 29.2 %collective-permute-start.89 = (bf16[512,1024]{1,0:T(8,128)(2,1)S(1)}, bf16[512,1024]{1,0:T(8,128)(2,1)S(1)}, u32[]{:S(2)}, u32[]{:S(2)}) collective-permute-start(bf16[512,1024]{1,0:T(8,128)(2,1)S(1)} %add_convert_fusion.2), channel_id=1, source_target_pairs={{32,36},{33,37},{34,38},{35,39},{36,40},{37,41},{38,42},{39,43},{4... | collective-permute-start | bytes 3145736 | tf_op jit(solution)/shard_map/ppermute | solution.py:497
  597.4 33.2 %collective-permute-start.91 = (bf16[512,1024]{1,0:T(8,128)(2,1)S(1)}, bf16[512,1024]{1,0:T(8,128)(2,1)S(1)}, u32[]{:S(2)}, u32[]{:S(2)}) collective-permute-start(bf16[512,1024]{1,0:T(8,128)(2,1)S(1)} %add_convert_fusion.1), channel_id=1, source_target_pairs={{32,44},{33,45},{34,46},{35,47},{36,32},{37,33},{38,34},{39,35},{4... | collective-permute-start | bytes 3145736 | tf_op jit(solution)/shard_map/ppermute | solution.py:497
  612.5 21.5 %collective-permute-start.93 = (bf16[512,1024]{1,0:T(8,128)(2,1)S(1)}, bf16[512,1024]{1,0:T(8,128)(2,1)S(1)}, u32[]{:S(2)}, u32[]{:S(2)}) collective-permute-start(bf16[512,1024]{1,0:T(8,128)(2,1)S(1)} %add_convert_fusion), channel_id=1, source_target_pairs={{32,40},{33,41},{34,42},{35,43},{36,44},{37,45},{38,46},{39,47},{4... | collective-permute-start | bytes 3145736 | tf_op jit(solution)/shard_map/ppermute | solution.py:497
  622.6 29.4 %collective-permute-start.80 = (bf16[256,2048]{1,0:T(8,128)(2,1)S(1)}, bf16[256,2048]{1,0:T(8,128)(2,1)S(1)}, u32[]{:S(2)}, u32[]{:S(2)}) collective-permute-start(bf16[256,2048]{1,0:T(8,128)(2,1)S(1)} %fusion.15), channel_id=1, source_target_pairs={{0,12},{1,13},{2,14},{3,15},{4,0},{5,1},{6,2},{7,3},{8,4},{9,5},{1... | collective-permute-start | bytes 3145736 | tf_op jit(solution)/shard_map/ppermute | solution.py:497
  630.6 25.6 %collective-permute-start.82 = (bf16[256,2048]{1,0:T(8,128)(2,1)S(1)}, bf16[256,2048]{1,0:T(8,128)(2,1)S(1)}, u32[]{:S(2)}, u32[]{:S(2)}) collective-permute-start(bf16[256,2048]{1,0:T(8,128)(2,1)S(1)} %fusion.16), channel_id=1, source_target_pairs={{0,8},{1,9},{2,10},{3,11},{4,12},{5,13},{6,14},{7,15},{8,0},{9,1},... | collective-permute-start | bytes 3145736 | tf_op jit(solution)/shard_map/ppermute | solution.py:497
  634.0 26.0 %collective-permute-start.61 = (bf16[16,64,512]{2,1,0:T(8,128)(2,1)S(1)}, bf16[16,64,512]{2,1,0:T(8,128)(2,1)S(1)}, u32[]{:S(2)}, u32[]{:S(2)}) collective-permute-start(bf16[16,64,512]{2,1,0:T(8,128)(2,1)S(1)} %get-tuple-element.288), channel_id=1, source_target_pairs={{0,16},{1,17},{2,18},{3,19},{4,20},{5,21},{6,22},{7,23},{8,24},{9,... | collective-permute-start | bytes 3145736 | tf_op jit(solution)/shard_map/ppermute | solution.py:497
  639.2 21.2 %collective-permute-start.94 = (bf16[128,1024]{1,0:T(8,128)(2,1)S(1)}, bf16[128,1024]{1,0:T(8,128)(2,1)S(1)}, u32[]{:S(2)}, u32[]{:S(2)}) collective-permute-start(bf16[128,1024]{1,0:T(8,128)(2,1)S(1)} %get-tuple-element.261), channel_id=1, source_target_pairs={{32,33},{33,34},{34,35},{35,32},{36,37},{37,38},{38,39},{39,36},{4... | collective-permute-start | bytes 786440 | tf_op jit(solution)/shard_map/ppermute | solution.py:497
  642.1 21.2 %collective-permute-start.95 = (bf16[128,1024]{1,0:T(8,128)(2,1)S(1)}, bf16[128,1024]{1,0:T(8,128)(2,1)S(1)}, u32[]{:S(2)}, u32[]{:S(2)}) collective-permute-start(bf16[128,1024]{1,0:T(8,128)(2,1)S(1)} %get-tuple-element.263), channel_id=1, source_target_pairs={{32,35},{33,32},{34,33},{35,34},{36,39},{37,36},{38,37},{39,38},{4... | collective-permute-start | bytes 786440 | tf_op jit(solution)/shard_map/ppermute | solution.py:497
  671.0 21.7 %collective-permute-start.86 = (bf16[64,2048]{1,0:T(8,128)(2,1)S(1)}, bf16[64,2048]{1,0:T(8,128)(2,1)S(1)}, u32[]{:S(2)}, u32[]{:S(2)}) collective-permute-start(bf16[64,2048]{1,0:T(8,128)(2,1)S(1)} %add_convert_fusion.5), channel_id=1, source_target_pairs={{0,16},{1,17},{2,18},{3,19},{4,20},{5,21},{6,22},{7,23},{8,24},{9,... | collective-permute-start | bytes 786440 | tf_op jit(solution)/shard_map/ppermute | solution.py:497
  (202 other events, 1576.2 us)
Sparse Core Ops, SparseCore 0:
  360.2 77.9 reduce-scatter.3

commit v2 on v1

--- a/solution.py
+++ b/solution.py
@@ -14,6 +14,11 @@
 EPSILON = 1e-05
 MASKED = -1000000000.0
 CHUNK = 512
+GELU_A = 0.7978845608028654
+GELU_B = 0.044715
+HBM_SPEC = pl.BlockSpec(memory_space=pltpu.HBM)
+VMEM_SPEC = pl.BlockSpec(memory_space=pltpu.VMEM)
+SMEM_SPEC = pl.BlockSpec(memory_space=pltpu.SMEM)
 
 
 def matmul(former, latter):
@@ -46,10 +51,6 @@
     return factor * (grad_normed - first_mean - normed * second_mean)
 
 
-GELU_A = 0.7978845608028654
-GELU_B = 0.044715
-
-
 def gelu(v):
     return 0.5 * v * (1.0 + jnp.tanh(GELU_A * (v + GELU_B * (v * v * v))))
 
@@ -65,24 +66,34 @@
 def head_probs(scores, same):
     scores = jnp.where(same, scores * HEAD_SIZE ** (-0.5), MASKED)
     expo = jnp.exp(scores - jnp.max(scores, axis=-1, keepdims=True))
-    return expo / jnp.sum(expo, axis=-1, keepdims=True)
-
-
-def weight_copies(lead_ref, down_ref, lead_buf, down_buf, sems):
-    count = lead_buf.shape[0]
-    leads = [
-        pltpu.make_async_copy(
-            lead_ref.at[:, pl.ds(j * CHUNK, CHUNK)], lead_buf.at[j], sems.at[j]
-        )
-        for j in range(count)
+    return expo * (1.0 / jnp.sum(expo, axis=-1, keepdims=True))
+
+
+def lanes(at, size):
+    return pl.ds(pl.multiple_of(at, 128), size)
+
+
+def hold_kernel(lead_in, down_in, lead_ref, down_ref, sem):
+    copies = [
+        pltpu.make_async_copy(lead_in, lead_ref, sem.at[0]),
+        pltpu.make_async_copy(down_in, down_ref, sem.at[1]),
     ]
-    downs = [
-        pltpu.make_async_copy(
-            down_ref.at[pl.ds(j * CHUNK, CHUNK), :], down_buf.at[j], sems.at[count + j]
-        )
-        for j in range(count)
-    ]
-    return leads, downs
+    for copy in copies:
+        copy.start()
+    for copy in copies:
+        copy.wait()
+
+
+def hold(lead, down):
+    return pl.pallas_call(
+        hold_kernel,
+        out_shape=[pltpu.VMEM(lead.shape, LOW), pltpu.VMEM(down.shape, LOW)],
+        in_specs=[HBM_SPEC] * 2,
+        out_specs=[VMEM_SPEC] * 2,
+        scratch_shapes=[pltpu.SemaphoreType.DMA((2,))],
+        compiler_params=pltpu.CompilerParams(vmem_limit_bytes=4 << 20),
+        name="hold",
+    )(lead, down)
 
 
 def forward_kernel(
@@ -102,106 +113,87 @@
     normeds_ref,
     saved_ref,
     inner_ref,
-    lead_buf,
-    down_buf,
     normed_buf,
     saved_buf,
     inner_buf,
-    sems,
+    result_buf,
     out_sems,
 ):
     role, slot = role_ref[0], role_ref[1]
-    width = entry_ref.shape[1]
-    leads, downs = weight_copies(lead_ref, down_ref, lead_buf, down_buf, sems)
-    count = len(leads)
-    keep_normed = pltpu.make_async_copy(normed_buf, normeds_ref.at[slot], out_sems.at[0])
-    keep_saved = pltpu.make_async_copy(saved_buf, saved_ref.at[slot], out_sems.at[1])
-    keep_inner = pltpu.make_async_copy(inner_buf, inner_ref.at[slot], out_sems.at[2])
-    keep_entry = pltpu.make_async_copy(entry_ref, entries_ref.at[slot], out_sems.at[3])
-
-    @pl.when(role == 0)
-    def _():
-        out_ref[...] = jnp.zeros_like(out_ref)
+    tokens, width = entry_ref.shape
+    keeps = [
+        pltpu.make_async_copy(entry_ref, entries_ref.at[slot], out_sems.at[0]),
+        pltpu.make_async_copy(normed_buf, normeds_ref.at[slot], out_sems.at[1]),
+        pltpu.make_async_copy(saved_buf, saved_ref.at[slot], out_sems.at[2]),
+    ]
+    keep_inner = pltpu.make_async_copy(inner_buf, inner_ref.at[slot], out_sems.at[3])
+
+    @pl.when(role > 0)
+    def _():
+        normed, _ = layer_norm(entry_ref[...].astype(WIDE))
+        normed_buf[...] = (normed * gain_ref[...]).astype(LOW)
+        keeps[0].start()
+        keeps[1].start()
 
     @pl.when(role == 1)
     def _():
-        for j in range(count):
-            leads[j].start()
-        keep_entry.start()
-        residual = entry_ref[...].astype(WIDE)
-        normed, _ = layer_norm(residual)
-        normed_buf[...] = (normed * gain_ref[...]).astype(LOW)
-        keep_normed.start()
-        qkv = 3 * width // CHUNK
-        for j in range(qkv):
-            leads[j].wait()
-            saved_buf[:, j * CHUNK : (j + 1) * CHUNK] = matmul(
-                normed_buf[...], lead_buf[j]
-            ).astype(LOW)
+        @pl.loop(0, 3 * width // CHUNK)
+        def _(j):
+            at = lanes(j * CHUNK, CHUNK)
+            saved_buf[:, at] = matmul(normed_buf[...], lead_ref[:, at]).astype(LOW)
+
         same = seg_col_ref[slot] == seg_row_ref[slot]
-        left = lax.broadcasted_iota(jnp.int32, (entry_ref.shape[0], 128), 1) < HEAD_SIZE
-        zero = jnp.zeros((entry_ref.shape[0], 128), LOW)
-        for pair in range(HEADS // 2):
-            at = pair * 128
-            query = saved_buf[:, at : at + 128]
-            key = saved_buf[:, width + at : width + at + 128]
-            value = saved_buf[:, 2 * width + at : 2 * width + at + 128]
-            probs_a = head_probs(matmul_nt(jnp.where(left, query, zero), key), same)
-            probs_b = head_probs(matmul_nt(jnp.where(left, zero, query), key), same)
-            mixed = jnp.where(
-                left, matmul(probs_a.astype(LOW), value), matmul(probs_b.astype(LOW), value)
-            )
-            saved_buf[:, 3 * width + at : 3 * width + at + 128] = mixed.astype(LOW)
-        keep_saved.start()
-        mixed = saved_buf[:, 3 * width :]
-        for j in range(qkv, count):
-            leads[j].wait()
-            at = (j - qkv) * CHUNK
-            out_ref[:, at : at + CHUNK] = (
-                entry_ref[:, at : at + CHUNK].astype(WIDE) + matmul(mixed, lead_buf[j])
-            ).astype(LOW)
-        keep_entry.wait()
-        keep_normed.wait()
-        keep_saved.wait()
+        left = lax.broadcasted_iota(jnp.int32, (tokens, 128), 1) < HEAD_SIZE
+        zero = jnp.zeros((tokens, 128), LOW)
+
+        @pl.loop(0, HEADS // 4)
+        def _(quad):
+            for which in range(2):
+                at = quad * 256 + which * 128
+                query = saved_buf[:, lanes(at, 128)]
+                key = saved_buf[:, lanes(width + at, 128)]
+                value = saved_buf[:, lanes(2 * width + at, 128)]
+                probs_a = head_probs(matmul_nt(jnp.where(left, query, zero), key), same)
+                probs_b = head_probs(matmul_nt(jnp.where(left, zero, query), key), same)
+                mixed = jnp.where(
+                    left, matmul(probs_a.astype(LOW), value), matmul(probs_b.astype(LOW), value)
+                )
+                saved_buf[:, lanes(3 * width + at, 128)] = mixed.astype(LOW)
+
+        keeps[2].start()
+
+        @pl.loop(0, width // CHUNK)
+        def _(j):
+            at = lanes(j * CHUNK, CHUNK)
+            term = matmul(saved_buf[:, 3 * width :], lead_ref[:, lanes(3 * width + j * CHUNK, CHUNK)])
+            out_ref[:, at] = (entry_ref[:, at].astype(WIDE) + term).astype(LOW)
 
     @pl.when(role == 2)
     def _():
-        for j in range(count):
-            leads[j].start()
-            downs[j].start()
-        keep_entry.start()
-        residual = entry_ref[...].astype(WIDE)
-        normed, _ = layer_norm(residual)
-        normed_buf[...] = (normed * gain_ref[...]).astype(LOW)
-        keep_normed.start()
-        result = residual
-        for j in range(count):
-            leads[j].wait()
-            inner = matmul(normed_buf[...], lead_buf[j])
-            inner_buf[:, j * CHUNK : (j + 1) * CHUNK] = inner
+        result_buf[...] = entry_ref[...].astype(WIDE)
+
+        @pl.loop(0, lead_ref.shape[1] // CHUNK)
+        def _(j):
+            at = lanes(j * CHUNK, CHUNK)
+            inner = matmul(normed_buf[...], lead_ref[:, at])
+            inner_buf[:, at] = inner
             active = gelu(inner).astype(LOW)
-            saved_buf[:, j * CHUNK : (j + 1) * CHUNK] = active
-            downs[j].wait()
-            result = result + matmul(active, down_buf[j])
-        keep_saved.start()
+            saved_buf[:, at] = active
+            result_buf[...] += matmul(active, down_ref[pl.ds(j * CHUNK, CHUNK), :])
+
+        keeps[2].start()
         keep_inner.start()
-        out_ref[...] = result.astype(LOW)
-        keep_entry.wait()
-        keep_normed.wait()
-        keep_saved.wait()
+        out_ref[...] = result_buf[...].astype(LOW)
         keep_inner.wait()
 
-
-VMEM_SPEC = pl.BlockSpec(memory_space=pltpu.VMEM)
-ANY_SPEC = pl.BlockSpec(memory_space=pl.ANY)
-
-
-def weight_scratch(width, hidden):
-    count = hidden // CHUNK
-    return [
-        pltpu.VMEM((count, width, CHUNK), LOW),
-        pltpu.VMEM((count, CHUNK, width), LOW),
-    ]
+    @pl.when(role > 0)
+    def _():
+        for keep in keeps:
+            keep.wait()
+
+
+def pinned(value):
+    return pltpu.with_memory_space_constraint(value, pltpu.VMEM)
 
 
 def forward_stage(role, entry, seg_col, seg_row, gain, lead, down, kept):
@@ -211,25 +203,22 @@
         forward_kernel,
         out_shape=[jax.ShapeDtypeStruct(entry.shape, LOW)]
         + [jax.ShapeDtypeStruct(k.shape, k.dtype) for k in kept],
-        in_specs=[pl.BlockSpec(memory_space=pltpu.SMEM)]
-        + [VMEM_SPEC] * 4
-        + [ANY_SPEC] * 6,
-        out_specs=[VMEM_SPEC] + [ANY_SPEC] * 4,
-        scratch_shapes=weight_scratch(width, hidden)
-        + [
+        in_specs=[SMEM_SPEC] + [VMEM_SPEC] * 6 + [HBM_SPEC] * 4,
+        out_specs=[VMEM_SPEC] + [HBM_SPEC] * 4,
+        scratch_shapes=[
             pltpu.VMEM((tokens, width), LOW),
             pltpu.VMEM((tokens, hidden), LOW),
             pltpu.VMEM((tokens, hidden), WIDE),
-            pltpu.SemaphoreType.DMA((2 * hidden // CHUNK,)),
+            pltpu.VMEM((tokens, width), WIDE),
             pltpu.SemaphoreType.DMA((4,)),
         ],
         input_output_aliases={7: 1, 8: 2, 9: 3, 10: 4},
-        compiler_params=pltpu.CompilerParams(vmem_limit_bytes=30 << 20),
+        compiler_params=pltpu.CompilerParams(vmem_limit_bytes=14 << 20),
         cost_estimate=pl.CostEstimate(
             flops=4 * tokens * width * hidden, bytes_accessed=20 << 20, transcendentals=0
         ),
         name="forward_stage",
-    )(role, entry, seg_col, seg_row, gain, lead, down, *kept)
+    )(role, entry, seg_col, seg_row, gain, pinned(lead), pinned(down), *kept)
 
 
 def backward_kernel(
@@ -250,74 +239,49 @@
     nexts_ref,
     grads_ref,
     gains_ref,
-    lead_buf,
-    down_buf,
     saved_buf,
     inner_buf,
     grads_buf,
     mixed_buf,
     gain_buf,
     entry_buf,
-    sems,
+    normed_buf,
     in_sems,
     out_sems,
 ):
     role, slot = role_ref[0], role_ref[1]
     tokens, width = grad_ref.shape
-    leads, downs = weight_copies(lead_ref, down_ref, lead_buf, down_buf, sems)
-    count = len(leads)
     bring_saved = pltpu.make_async_copy(saved_ref.at[slot], saved_buf, in_sems.at[0])
     bring_inner = pltpu.make_async_copy(inner_ref.at[slot], inner_buf, in_sems.at[1])
     bring_entry = pltpu.make_async_copy(entries_ref.at[slot], entry_buf, in_sems.at[2])
     keep_next = pltpu.make_async_copy(grad_ref, nexts_ref.at[slot], out_sems.at[0])
     keep_grads = pltpu.make_async_copy(grads_buf, grads_ref.at[slot], out_sems.at[1])
     keep_gain = pltpu.make_async_copy(gain_buf, gains_ref.at[slot], out_sems.at[2])
-    qkv = 3 * width // CHUNK
-
-    def finish(grad_normed):
-        keep_grads.start()
-        bring_entry.wait()
-        normed, factor = layer_norm(entry_buf[...].astype(WIDE))
-        gain_buf[...] = jnp.broadcast_to(
-            jnp.sum(grad_normed * normed, axis=0, keepdims=True), gain_buf.shape
-        )
-        keep_gain.start()
-        out_ref[...] = (
-            grad_ref[...].astype(WIDE) + norm_back(grad_normed * gain_ref[...], normed, factor)
-        ).astype(LOW)
-        keep_next.wait()
-        keep_grads.wait()
-        keep_gain.wait()
-
-    @pl.when(role == 0)
-    def _():
-        out_ref[...] = jnp.zeros_like(out_ref)
+
+    @pl.when(role > 0)
+    def _():
+        bring_entry.start()
+        keep_next.start()
+        normed_buf[...] = jnp.zeros_like(normed_buf)
 
     @pl.when(role == 1)
     def _():
         bring_saved.start()
-        for j in list(range(qkv, count)) + list(range(qkv)):
-            leads[j].start()
-        keep_next.start()
-        bring_entry.start()
         grads_buf[:, 3 * width :] = grad_ref[...]
-        grad_mixed = jnp.zeros((tokens, width), WIDE)
-        for j in range(qkv, count):
-            leads[j].wait()
-            at = (j - qkv) * CHUNK
-            grad_mixed = grad_mixed + matmul_nt(grad_ref[:, at : at + CHUNK], lead_buf[j])
-        mixed_buf[...] = grad_mixed.astype(LOW)
+        mixed_buf[...] = matmul_nt(grad_ref[...], lead_ref[:, 3 * width :]).astype(LOW)
         bring_saved.wait()
         same = seg_col_ref[slot] == seg_row_ref[slot]
         left = lax.broadcasted_iota(jnp.int32, (tokens, 128), 1) < HEAD_SIZE
         zero = jnp.zeros((tokens, 128), LOW)
         scale = HEAD_SIZE ** (-0.5)
-        for pair in range(HEADS // 2):
+
+        @pl.loop(0, HEADS // 2)
+        def _(pair):
             at = pair * 128
-            query = saved_buf[:, at : at + 128]
-            key = saved_buf[:, width + at : width + at + 128]
-            value = saved_buf[:, 2 * width + at : 2 * width + at + 128]
-            grad = mixed_buf[:, at : at + 128]
+            query = saved_buf[:, lanes(at, 128)]
+            key = saved_buf[:, lanes(width + at, 128)]
+            value = saved_buf[:, lanes(2 * width + at, 128)]
+            grad = mixed_buf[:, lanes(at, 128)]
             parts = []
             for own in (0, 1):
                 mine = lambda v: jnp.where(left, v, zero) if own == 0 else jnp.where(left, zero, v)
@@ -335,36 +299,44 @@
                     )
                 )
             for which in range(3):
-                spot = which * width + at
-                grads_buf[:, spot : spot + 128] = jnp.where(
+                grads_buf[:, lanes(which * width + at, 128)] = jnp.where(
                     left, parts[0][which], parts[1][which]
                 ).astype(LOW)
-        grad_normed = jnp.zeros((tokens, width), WIDE)
-        for j in range(qkv):
-            leads[j].wait()
-            grad_normed = grad_normed + matmul_nt(
-                grads_buf[:, j * CHUNK : (j + 1) * CHUNK], lead_buf[j]
-            )
-        finish(grad_normed)
+
+        @pl.loop(0, 3 * width // CHUNK)
+        def _(j):
+            at = lanes(j * CHUNK, CHUNK)
+            normed_buf[...] += matmul_nt(grads_buf[:, at], lead_ref[:, at])
 
     @pl.when(role == 2)
     def _():
         bring_inner.start()
-        for j in range(count):
-            downs[j].start()
-            leads[j].start()
-        keep_next.start()
-        bring_entry.start()
-        grad_normed = jnp.zeros((tokens, width), WIDE)
         bring_inner.wait()
-        for j in range(count):
-            at = slice(j * CHUNK, (j + 1) * CHUNK)
-            downs[j].wait()
-            grad_active = matmul_nt(grad_ref[...], down_buf[j])
-            grads_buf[:, at] = (gelu_slope(inner_buf[:, at]) * grad_active).astype(LOW)
-            leads[j].wait()
-            grad_normed = grad_normed + matmul_nt(grads_buf[:, at], lead_buf[j])
-        finish(grad_normed)
+
+        @pl.loop(0, lead_ref.shape[1] // CHUNK)
+        def _(j):
+            at = lanes(j * CHUNK, CHUNK)
+            grad_active = matmul_nt(grad_ref[...], down_ref[pl.ds(j * CHUNK, CHUNK), :])
+            grads = (gelu_slope(inner_buf[:, at]) * grad_active).astype(LOW)
+            grads_buf[:, at] = grads
+            normed_buf[...] += matmul_nt(grads, lead_ref[:, at])
+
+    @pl.when(role > 0)
+    def _():
+        keep_grads.start()
+        bring_entry.wait()
+        grad_normed = normed_buf[...]
+        normed, factor = layer_norm(entry_buf[...].astype(WIDE))
+        gain_buf[...] = jnp.broadcast_to(
+            jnp.sum(grad_normed * normed, axis=0, keepdims=True), gain_buf.shape
+        )
+        keep_gain.start()
+        out_ref[...] = (
+            grad_ref[...].astype(WIDE) + norm_back(grad_normed * gain_ref[...], normed, factor)
+        ).astype(LOW)
+        keep_next.wait()
+        keep_grads.wait()
+        keep_gain.wait()
 
 
 def backward_stage(
@@ -376,29 +348,38 @@
         backward_kernel,
         out_shape=[jax.ShapeDtypeStruct(grad.shape, LOW)]
         + [jax.ShapeDtypeStruct(k.shape, k.dtype) for k in totals],
-        in_specs=[pl.BlockSpec(memory_space=pltpu.SMEM)]
-        + [VMEM_SPEC] * 4
-        + [ANY_SPEC] * 8,
-        out_specs=[VMEM_SPEC] + [ANY_SPEC] * 3,
-        scratch_shapes=weight_scratch(width, hidden)
-        + [
+        in_specs=[SMEM_SPEC] + [VMEM_SPEC] * 6 + [HBM_SPEC] * 6,
+        out_specs=[VMEM_SPEC] + [HBM_SPEC] * 3,
+        scratch_shapes=[
             pltpu.VMEM((tokens, hidden), LOW),
             pltpu.VMEM((tokens, hidden), WIDE),
             pltpu.VMEM((tokens, hidden), LOW),
             pltpu.VMEM((tokens, width), LOW),
             pltpu.VMEM((8, width), WIDE),
             pltpu.VMEM((tokens, width), LOW),
-            pltpu.SemaphoreType.DMA((2 * hidden // CHUNK,)),
+            pltpu.VMEM((tokens, width), WIDE),
             pltpu.SemaphoreType.DMA((3,)),
             pltpu.SemaphoreType.DMA((3,)),
         ],
         input_output_aliases={10: 1, 11: 2, 12: 3},
-        compiler_params=pltpu.CompilerParams(vmem_limit_bytes=32 << 20),
+        compiler_params=pltpu.CompilerParams(vmem_limit_bytes=14 << 20),
         cost_estimate=pl.CostEstimate(
             flops=4 * tokens * width * hidden, bytes_accessed=20 << 20, transcendentals=0
         ),
         name="backward_stage",
-    )(role, grad, seg_col, seg_row, gain, lead, down, entries, saved, inner, *totals)
+    )(
+        role,
+        grad,
+        seg_col,
+        seg_row,
+        gain,
+        pinned(lead),
+        pinned(down),
+        entries,
+        saved,
+        inner,
+        *totals,
+    )
 
 
 def stats_kernel(readout_ref, table_ref, peak_ref, total_ref):
@@ -431,7 +412,7 @@
             pl.BlockSpec((tile, emb), lambda i: (i, 0)),
         ],
         out_specs=[whole, whole],
-        compiler_params=pltpu.CompilerParams(vmem_limit_bytes=40 << 20),
+        compiler_params=pltpu.CompilerParams(vmem_limit_bytes=30 << 20),
         cost_estimate=pl.CostEstimate(
             flops=2 * tokens * vocab * emb, bytes_accessed=5 << 20, transcendentals=tokens * vocab
         ),
@@ -471,14 +452,160 @@
             jax.ShapeDtypeStruct((tokens, emb), WIDE),
         ],
         grid=(vocab // tile,),
-        in_specs=[pl.BlockSpec(memory_space=pltpu.SMEM), whole, part, row, row],
+        in_specs=[SMEM_SPEC, whole, part, row, row],
         out_specs=[part, whole],
-        compiler_params=pltpu.CompilerParams(vmem_limit_bytes=40 << 20),
+        compiler_params=pltpu.CompilerParams(vmem_limit_bytes=30 << 20),
         cost_estimate=pl.CostEstimate(
             flops=6 * tokens * vocab * emb, bytes_accessed=9 << 20, transcendentals=tokens * vocab
         ),
         name="head_grads",
     )(base, readout, table, logsum, ids)
+
+
+def lookup_kernel(ids_ref, table_ref, noise_ref, out_ref, total_ref):
+    step = pl.program_id(0)
+    tile = table_ref.shape[1]
+    tokens = ids_ref.shape[1]
+    ids = ids_ref[...] - step * tile
+    hits = lax.broadcasted_iota(jnp.int32, (tile, tokens), 0) == ids
+    hits = jnp.where(hits, 1.0, 0.0).astype(LOW)
+    term = matmul(table_ref[...], hits)
+
+    @pl.when(step == 0)
+    def _():
+        total_ref[...] = term
+
+    @pl.when(step > 0)
+    def _():
+        total_ref[...] += term
+
+    @pl.when(step == pl.num_programs(0) - 1)
+    def _():
+        out_ref[...] = (total_ref[...] + noise_ref[...].astype(WIDE)).astype(LOW)
+
+
+def lookup(ids, table, noise, tile):
+    parts, vocab = table.shape
+    tokens = ids.shape[1]
+    whole = pl.BlockSpec((parts, tokens), lambda i: (0, 0))
+    return pl.pallas_call(
+        lookup_kernel,
+        out_shape=jax.ShapeDtypeStruct((parts, tokens), LOW),
+        grid=(vocab // tile,),
+        in_specs=[
+            pl.BlockSpec((1, tokens), lambda i: (0, 0)),
+            pl.BlockSpec((parts, tile), lambda i: (0, i)),
+            whole,
+        ],
+        out_specs=whole,
+        scratch_shapes=[pltpu.VMEM((parts, tokens), WIDE)],
+        compiler_params=pltpu.CompilerParams(vmem_limit_bytes=30 << 20),
+        cost_estimate=pl.CostEstimate(
+            flops=2 * 128 * vocab * tokens, bytes_accessed=4 << 20, transcendentals=0
+        ),
+        name="lookup",
+    )(ids, table, noise)
+
+
+def lead_grad_kernel(where_ref, normed_ref, mixed_ref, grads_ref, out_ref, turned_ref):
+    role, half, spot = where_ref[0], where_ref[1], where_ref[2]
+    step = pl.program_id(0)
+    width = normed_ref.shape[1]
+    steps = pl.num_programs(0)
+    use_mixed = jnp.logical_and(role == 1, half == 1)
+
+    @pl.when(step == 0)
+    def _():
+        turned_ref[...] = normed_ref[...].T
+
+    @pl.when(jnp.logical_and(step == steps // 2, use_mixed))
+    def _():
+        turned_ref[...] = mixed_ref[...].T
+
+    result = matmul(turned_ref[...], grads_ref[...]).astype(LOW)
+    unit = width // 16
+    for x in range(4):
+        for y in range(4):
+            part = result[(4 * x + y) * unit : (4 * x + y + 1) * unit]
+
+            @pl.when(half == 0)
+            def _():
+                out_ref[(x - spot + 4) % 4, y * unit : (y + 1) * unit, :] = part
+
+            @pl.when(half == 1)
+            def _():
+                out_ref[(y - spot + 4) % 4, x * unit : (x + 1) * unit, :] = part
+
+
+def lead_grad(where, normed, saved, grads):
+    tokens, width = normed.shape
+    tile = 512
+    return pl.pallas_call(
+        lead_grad_kernel,
+        out_shape=jax.ShapeDtypeStruct((4, width // 4, 2 * width), LOW),
+        grid_spec=pltpu.PrefetchScalarGridSpec(
+            num_scalar_prefetch=1,
+            grid=(2 * width // tile,),
+            in_specs=[
+                pl.BlockSpec((tokens, width), lambda i, where: (0, 0)),
+                pl.BlockSpec((tokens, width), lambda i, where: (0, 3)),
+                pl.BlockSpec((tokens, tile), lambda i, where: (0, where[1] * (2 * width // tile) + i)),
+            ],
+            out_specs=pl.BlockSpec((4, width // 4, tile), lambda i, where: (0, 0, i)),
+            scratch_shapes=[pltpu.VMEM((width, tokens), LOW)],
+        ),
+        compiler_params=pltpu.CompilerParams(vmem_limit_bytes=24 << 20),
+        cost_estimate=pl.CostEstimate(
+            flops=4 * tokens * width * width, bytes_accessed=8 << 20, transcendentals=0
+        ),
+        name="lead_grad",
+    )(where, normed, saved, grads)
+
+
+def down_grad_kernel(where_ref, saved_ref, nexts_ref, out_ref):
+    role, half, spot = where_ref[0], where_ref[1], where_ref[2]
+    at = pl.program_id(0)
+    unit = saved_ref.shape[1] // 4
+
+    @pl.when(role == 2)
+    def _():
+        result = matmul_tn(saved_ref[...], nexts_ref[...]).astype(LOW)
+
+        @pl.when(half == 0)
+        def _():
+            out_ref[(at - spot + 4) % 4] = result
+
+        @pl.when(half == 1)
+        def _():
+            for y in range(4):
+                out_ref[
+                    (y - spot + 4) % 4, pl.ds(pl.multiple_of(at * unit, unit), unit), :
+                ] = result[y * unit : (y + 1) * unit]
+
+
+def down_grad(where, saved, nexts):
+    tokens, hidden = saved.shape
+    width = nexts.shape[1]
+    rows = hidden // 8
+    live = lambda where: jnp.where(where[0] == 2, 1, 0)
+    return pl.pallas_call(
+        down_grad_kernel,
+        out_shape=jax.ShapeDtypeStruct((4, rows, width), LOW),
+        grid_spec=pltpu.PrefetchScalarGridSpec(
+            num_scalar_prefetch=1,
+            grid=(4,),
+            in_specs=[
+                pl.BlockSpec((tokens, rows), lambda i, where: (0, (where[1] * 4 + i) * live(where))),
+                pl.BlockSpec((tokens, width), lambda i, where: (0, 0)),
+            ],
+            out_specs=pl.BlockSpec((4, rows, width), lambda i, where: (0, 0, 0)),
+        ),
+        compiler_params=pltpu.CompilerParams(vmem_limit_bytes=24 << 20),
+        cost_estimate=pl.CostEstimate(
+            flops=2 * tokens * width * hidden // 2, bytes_accessed=8 << 20, transcendentals=0
+        ),
+        name="down_grad",
+    )(where, saved, nexts)
 
 
 ROW_LEN = 128
@@ -524,38 +651,37 @@
     return lax.optimization_barrier((value, earlier))[0]
 
 
-def block_of(values, block, count):
-    size = values.shape[1] // count
-    return lax.dynamic_slice_in_dim(values, block * size, size, 1)
-
-
 def row_block(values, block, count):
     size = values.shape[0] // count
     return lax.dynamic_slice_in_dim(values, block * size, size, 0)
 
 
-def by_second(values, unit):
-    rows, columns = values.shape
-    return values.reshape(rows, NX, NY, unit).transpose(0, 2, 1, 3).reshape(rows, columns)
-
-
-def reduce_plane(block_for, second, sections=range(SEC)):
-    pieces = {by: block_for(by) for by in TURNS + (0,)}
-    total = pieces[0].astype(WIDE)
+def reduce_plane(mine, got, second, sections=range(SEC)):
+    piece = lambda by: mine[by] if got is None else (mine[by].astype(WIDE) + got[by].astype(WIDE))
+    total = piece(0).astype(WIDE)
     for by in TURNS:
-        total = total + plane_route(pieces[by], by, True, sections).astype(WIDE)
+        total = total + plane_route(piece(by).astype(LOW), by, True, sections).astype(WIDE)
     lowered = total.astype(LOW)
-    mine = row_block(total, second, 4)
+    result = row_block(total, second, 4)
     for by in TURNS:
-        piece = row_block(lowered, (second + by) % 4, 4)
-        mine = mine + plane_route(piece, by, False, sections).astype(WIDE)
-    return mine.astype(LOW)
+        block = row_block(lowered, (second + by) % 4, 4)
+        result = result + plane_route(block, by, False, sections).astype(WIDE)
+    return result.astype(LOW)
 
 
 def gather_plane(values):
     blocks = jnp.stack([values] + [plane_route(values, by, True) for by in TURNS])
     blocks = jnp.concatenate([blocks] + [plane_route(blocks, by, False) for by in TURNS])
     return jnp.concatenate([blocks, swap_cores(blocks)])
+
+
+def empty(*kinds):
+    return pl.pallas_call(
+        lambda *refs: None,
+        out_shape=[jax.ShapeDtypeStruct(shape, dtype) for shape, dtype in kinds],
+        out_specs=[HBM_SPEC] * len(kinds),
+        name="empty",
+    )()
 
 
 def embed_kernel(base_ref, ids_ref, grad_ref, out_ref):
@@ -628,21 +754,20 @@
     seg_col = segment_ids.reshape(micro, tokens, 1)
     flat_ids = token_ids.reshape(-1)
 
+    noise = noise_input[:, 0].transpose(2, 0, 1).reshape(emb_part, -1)
+    own_embedded = lookup(flat_ids[None], embed_table.T, noise, 3200)
     small_pack = jnp.concatenate((input_proj, readout_proj.T))
     packs = {by: turn(small_pack, by) for by in TURNS}
     packs[0] = small_pack
     pack_of = lambda s: lax.select_n((section - s) % SEC, *[packs[by] for by in range(SEC)])
-    packs = [pack_of(s) for s in range(SEC)]
-    input_full = jnp.concatenate([p[:emb_part] for p in packs])
-    readout_full = jnp.concatenate([p[emb_part:] for p in packs])
-    embedded = (
-        embed_table[flat_ids].astype(WIDE) + noise_input.reshape(-1, emb_part).astype(WIDE)
-    ).astype(LOW)
-    parts = {by: turn(after(embedded, packs[0]), by) for by in TURNS}
+    packed = [pack_of(s) for s in range(SEC)]
+    input_full = jnp.concatenate([p[:emb_part] for p in packed])
+    readout_full = jnp.concatenate([p[emb_part:] for p in packed])
+    parts = {by: turn(after(own_embedded, packs[by]), by) for by in TURNS}
     embedded = jnp.concatenate(
-        [embedded] + [parts[SEC - s] for s in range(1, SEC)], axis=1
-    )
-    first_in = matmul(embedded, input_full).astype(LOW).reshape(micro, tokens, width)
+        [own_embedded] + [parts[SEC - s] for s in range(1, SEC)]
+    )
+    first_in = matmul_tn(embedded, input_full).astype(LOW).reshape(micro, tokens, width)
 
     eighth = row_block(row_block(own_down, core, 2), first_at, 4)
     eighth = jnp.where(section == 1, link(eighth, 0, 1), link(eighth, 2, 3))
@@ -662,12 +787,13 @@
         )
     )
     all_ids = gather_plane(after(flat_ids, upper_other))
-
-    kept = (
-        jnp.zeros((micro, tokens, width), LOW),
-        jnp.zeros((micro, tokens, width), LOW),
-        jnp.zeros((micro, tokens, hidden), LOW),
-        jnp.zeros((micro, tokens, hidden), WIDE),
+    held = hold(lead, full_down)
+
+    kept = empty(
+        ((micro, tokens, width), LOW),
+        ((micro, tokens, width), LOW),
+        ((micro, tokens, hidden), LOW),
+        ((micro, tokens, hidden), WIDE),
     )
 
     def role_at(at):
@@ -696,7 +822,7 @@
         elif step < micro:
             entry = jnp.where(section == 0, first_in[step], entry)
         out, *kept = forward_stage(
-            role_at(step - 2 * section), entry, seg_col, seg_row, gain_half, lead, full_down, kept
+            role_at(step - 2 * section), entry, seg_col, seg_row, gain_half, *held, kept
         )
         outs.append(out)
         for s in range(last):
@@ -735,10 +861,10 @@
     last_grads = norm_back(grad_final * gain_f, normed_f, factor_f).astype(LOW)
     last_grads = last_grads.reshape(micro, tokens, width)
 
-    totals = (
-        jnp.zeros((micro, tokens, width), LOW),
-        jnp.zeros((micro, tokens, hidden), LOW),
-        jnp.zeros((micro, 8, width), WIDE),
+    totals = empty(
+        ((micro, tokens, width), LOW),
+        ((micro, tokens, hidden), LOW),
+        ((micro, 8, width), WIDE),
     )
     outs, hops = [], {}
     for step in range(steps):
@@ -753,8 +879,7 @@
             seg_col,
             seg_row,
             gain_half,
-            lead,
-            full_down,
+            *held,
             entries,
             saved,
             inner,
@@ -781,25 +906,31 @@
     gain_grad = jnp.sum(gain_grads[:, 0], axis=0)
     flat = lambda v: v.reshape(all_tokens, v.shape[-1])
     normed, grad_nexts, grads, saved = flat(normeds), flat(grad_nexts), flat(grads), flat(saved)
-    tail = jnp.where(is_mlp, normed, saved[:, 3 * width :])
-    order = lambda values, which, unit: jnp.where(which == 0, values, by_second(values, unit))
     odd = (1, 3)
-
-    def lead_block(which, spot, by):
-        block = (spot + by) % 4
-        former = block_of(order(normed, which, 64), block, 4)
-        latter = block_of(order(jnp.where(which == 0, normed, tail), which, 64), block, 4)
-        part = lax.dynamic_slice_in_dim(grads, which * 2 * width, 2 * width, 1)
-        return jnp.concatenate(
-            (matmul_tn(former, part[:, :width]), matmul_tn(latter, part[:, width:])), axis=1
-        )
-
-    def down_block(which, spot, by):
-        block = (spot + by) % 4
-        part = lax.dynamic_slice_in_dim(saved, which * half_rows, half_rows, 1)
-        return matmul_tn(block_of(order(part, which, 128), block, 4), grad_nexts)
-
-    input_grad = matmul_tn(embedded, first_grads).reshape(SEC, 16, 4, width)
+    role = jnp.where(is_mlp, 2, 1)
+    where_other = jnp.stack((role, 1 - core, second_at)).astype(jnp.int32)
+    where_mine = jnp.stack((role, core, first_at)).astype(jnp.int32)
+    both = lambda mine, other: jnp.where(
+        core == 0,
+        jnp.concatenate((mine, other), axis=1),
+        jnp.concatenate((other, mine), axis=1),
+    )
+    lead_got = swap_cores(lead_grad(where_other, normed, saved, grads))
+    lead_mine = lead_grad(where_mine, normed, saved, grads)
+    down_got = swap_cores(down_grad(where_other, saved, grad_nexts), odd)
+    down_mine = down_grad(where_mine, saved, grad_nexts)
+    lead_part = reduce_plane(lead_mine, lead_got, second_at)
+    down_part = reduce_plane(down_mine, down_got, second_at, odd)
+    lead_out = both(lead_part, swap_cores(lead_part)).astype(WIDE)
+
+    down_other = swap_cores(down_part, odd)
+    upper_part = jnp.where(core == 0, down_part, down_other)
+    lower_part = jnp.where(core == 0, down_other, down_part)
+    upper_half = lax.dynamic_slice_in_dim(upper_part, core * (width // 2), width // 2, 1)
+    upper_half = jnp.where(section == 0, link(upper_half, 1, 0), link(upper_half, 3, 2))
+    down_out = jnp.where(is_mlp, lower_part, both(upper_half, swap_cores(upper_half))).astype(WIDE)
+
+    input_grad = matmul(embedded, first_grads).reshape(SEC, 16, 4, width)
     input_grad = input_grad.transpose(1, 0, 2, 3).reshape(16, 16, width)
     readout_grad = readout_grad.reshape(16, 16, width)
     vectors = jnp.concatenate(
@@ -817,39 +948,15 @@
             jnp.zeros((16, 15, width), WIDE),
         ),
         axis=1,
-    ).reshape(NX, NY, 32, GRP, width // GRP)
-    smalls = (small, small.swapaxes(0, 1))
-
-    def small_block(which, spot, by):
-        part = jnp.where(which == 0, smalls[0][:, :, :, 0], smalls[1][:, :, :, 1])
-        part = lax.dynamic_index_in_dim(part, (spot + by) % 4, 0, False)
-        return part.reshape(NY * 32, width // GRP)
-
-    def summed(maker, sections=range(SEC)):
-        def block_for(by):
-            other = maker(1 - core, second_at, by).astype(LOW)
-            got = swap_cores(other, sections).astype(WIDE)
-            return (maker(core, first_at, by) + got).astype(LOW)
-
-        return reduce_plane(block_for, second_at, sections)
-
-    both = lambda mine, other: jnp.where(
-        core == 0,
-        jnp.concatenate((mine, other), axis=1),
-        jnp.concatenate((other, mine), axis=1),
-    )
-    lead_part = summed(lead_block)
-    lead_out = both(lead_part, swap_cores(lead_part)).astype(WIDE)
-
-    down_part = summed(down_block, odd)
-    down_other = swap_cores(down_part, odd)
-    upper_part = jnp.where(core == 0, down_part, down_other)
-    lower_part = jnp.where(core == 0, down_other, down_part)
-    upper_half = lax.dynamic_slice_in_dim(upper_part, core * (width // 2), width // 2, 1)
-    upper_half = jnp.where(section == 0, link(upper_half, 1, 0), link(upper_half, 3, 2))
-    down_out = jnp.where(is_mlp, lower_part, both(upper_half, swap_cores(upper_half))).astype(WIDE)
-
-    small_part = summed(small_block)
+    ).astype(LOW)
+    half_of = lambda which: lax.dynamic_slice_in_dim(small, which * (width // 2), width // 2, 2)
+    small = half_of(core).astype(WIDE) + swap_cores(half_of(1 - core)).astype(WIDE)
+    small = small.astype(LOW).reshape(NX, NY, 32, width // 2)
+    small = jnp.where(core == 0, small, small.swapaxes(0, 1))
+    small = jnp.stack(
+        [lax.dynamic_index_in_dim(small, (first_at + by) % 4, 0, False) for by in range(4)]
+    )
+    small_part = reduce_plane(small.reshape(4, NY * 32, width // 2), None, second_at)
     small = both(small_part, swap_cores(small_part))
     gain_out = small[16, :64].astype(WIDE)
     input_rows = small[:16].reshape(SEC, 4, width)

time: 713 us -> 652 us (0.914)
  waiting for transfers between devices: 95.9 us -> 126 us
  Pallas kernels: 156 us -> 127 us
  local copies, waits for them, and re-layouts: 158 us -> 131 us
  matrix products: 32.5 us -> 6.21 us
  other arithmetic: 64.6 us -> 45.1 us
  starting transfers between devices: 179 us -> 189 us
    pallas_call x10, Pallas kernels: 82.3 us -> 40.5 us  [backward_stage(): pl.pallas_call(backward_kernel, out_shape=[jax.ShapeDtypeStruct(grad.shap...]
    ppermute x102 -> x93, waiting for transfers between devices: 95.9 us -> 126 us  [route(): return lax.ppermute(value, ALL, pairs)]
    pallas_call x0 -> x8, Pallas kernels: none -> 28.3 us  [the longest x2 11.3 us: lead_grad(): pl.pallas_call(lead_grad_kernel, out_shape=jax.ShapeDtypeStruct((4, width...]
    dot_general x26 -> x2, matrix products: 28.8 us -> 2.06 us  [matmul_tn(): lax.dot_general(former, latter, (((0,), (0,)), ((), ())), preferred_eleme...]
    pallas_call x10, Pallas kernels: 43 us -> 28.5 us  [forward_stage(): pl.pallas_call(forward_kernel, out_shape=[jax.ShapeDtypeStruct(entry.shap...]
    select_n x9 -> x1, other arithmetic: 11.8 us -> 0.04 us  [local(): small = jnp.where(core == 0, small, small.swapaxes(0, 1))]
    ppermute x102 -> x93, starting transfers between devices: 179 us -> 189 us  [route(): return lax.ppermute(value, ALL, pairs)]
    unnamed x277 -> x267, local copies, waits for them, and re-layouts: 107 us -> 107 us
  transfers between devices with their start and end apart: 103 -> 94, of which waited for: 20 -> 32; matrix products, arithmetic and copies ran while one was open for 22% -> 11% of each run, Pallas kernels for 17% -> 15%
where the time goes in v2:
time: 652 us; the launch traced here: 642 us
  starting transfers between devices  189 us (29%)
  local copies, waits for them, and re-layouts  131 us (20%)
  Pallas kernels  127 us (19%)
  waiting for transfers between devices  126 us (19%)
  other arithmetic  45.1 us (7%)
  between operations  16.9 us (3%)
    ppermute x93, starting transfers between devices, route(): return lax.ppermute(value, ALL, pairs)  189 us
    ppermute x93, waiting for transfers between devices, route(): return lax.ppermute(value, ALL, pairs)  126 us
    unnamed x267, local copies, waits for them, and re-layouts  107 us
    pallas_call x10, Pallas kernels, backward_stage(): pl.pallas_call(backward_kernel, out_shape=[jax.ShapeDtypeStruct(grad.shap...  40.5 us
    pallas_call x10, Pallas kernels, forward_stage(): pl.pallas_call(forward_kernel, out_shape=[jax.ShapeDtypeStruct(entry.shap...  28.5 us
    pallas_call x1, Pallas kernels, embed_sum(): pl.pallas_call(embed_kernel, out_shape=jax.ShapeDtypeStruct((parts, rows)...  14.5 us
  transfers between devices with their start and end apart: 94, of which 32 were waited for; matrix products, arithmetic and copies ran while one was open for 11% of the time, Pallas kernels for 15%

profile of v2, /device:TPU:103, one launch (start us, length us, event | category | flops | bytes accessed | tf_op | source)
XLA Modules:
  0.0 641.6 jit_solution(13127223495633661733)
XLA Ops:
  10.5 13.3 %collective-permute-done.7 = bf16[256,1024]{1,0:T(8,128)(2,1)S(1)} collective-permute-done((bf16[256,1024]{1,0:T(8,128)(2,1)S(1)}, bf16[256,1024]{1,0:T(8,128)(2,1)S(1)}, u32[]{:S(2)}, u32[]{:S(2)}) %collective-permute-start.7) | collective-permute-done | bytes 524320 | tf_op jit(solution)/shard_map/ppermute | solution.py:624
  36.6 5.1 collective-permute-done.10
  47.3 7.5 %lookup.1 = bf16[64,512]{1,0:T(8,128)(2,1)S(1)} custom-call(s32[1,512]{1,0:T(1,128)S(1)} %bitcast.238, bf16[64,32000]{1,0:T(8,128)(2,1)S(1)} %bitcast.247, bf16[64,512]{1,0:T(8,128)(2,1)S(1)} %copy_bitcast_fusion.noise_ref), custom_call_target="tpu_custom_call" | custom-call | flops 4194304000 | bytes 4194304 | tf_op jit(solution)/shard_map/lookup/pallas_call | solution.py:491
  106.9 44.3 %collective-permute-done.16 = bf16[128,1024]{1,0:T(8,128)(2,1)S(1)} collective-permute-done((bf16[128,1024]{1,0:T(8,128)(2,1)S(1)}, bf16[128,1024]{1,0:T(8,128)(2,1)S(1)}, u32[]{:S(2)}, u32[]{:S(2)}) %collective-permute-start.16) | collective-permute-done | bytes 262176 | tf_op jit(solution)/shard_map/ppermute | solution.py:624
  153.2 6.1 forward_stage.16
  162.7 6.1 forward_stage.17
  172.9 6.1 forward_stage.18
  180.3 6.2 forward_stage.19
  205.1 5.6 head_stats.1
  219.1 9.3 %head_grads.1 = (bf16[8000,256]{1,0:T(8,128)(2,1)S(1)}, f32[512,256]{1,0:T(8,128)S(1)}) custom-call(s32[1]{0:T(128)} %bitcast.40.base_ref, bf16[512,256]{1,0:T(8,128)(2,1)S(1)} %select_select_fusion.readout_ref, bf16[8000,256]{1,0:T(8,128)(2,1)S(1)} %copy-done.66, f32[1,512]{1,0:T(1,128)S(1)} %bitcast.246, s32[1,512]{1,0:T(1,128)S(1)} %bitcast.239), custom_call_target="tpu_custom_call" | custom-call | flops 6291456000 | bytes 9437184 | tf_op jit(solution)/shard_map/head_grads/pallas_call | solution.py:448
  236.5 6.4 collective-permute-done.30
  259.7 8.7 %backward_stage.10 = (bf16[128,1024]{1,0:T(8,128)(2,1)S(1)}, bf16[4,128,1024]{2,1,0:T(8,128)(2,1)S(1)}, bf16[4,128,4096]{2,1,0:T(8,128)(2,1)S(1)}, f32[4,8,1024]{2,1,0:T(8,128)S(1)}) custom-call(s32[2]{0:T(128)S(1)} %get-tuple-element.355.role_ref, ...), custom_call_target="tpu_custom_call", output_to_operand_aliasing={{1}: (10, {}), {2}: (11, {}), {3}: (12, {})} | custom-call | flops 2147483648 | bytes 20971520 | tf_op jit(solution)/shard_map/backward_stage/pallas_call | solution.py:347
  274.9 9.4 %backward_stage.11 = (bf16[128,1024]{1,0:T(8,128)(2,1)}, bf16[4,128,1024]{2,1,0:T(8,128)(2,1)S(1)}, bf16[4,128,4096]{2,1,0:T(8,128)(2,1)S(1)}, f32[4,8,1024]{2,1,0:T(8,128)S(1)}) custom-call(s32[2]{0:T(128)S(1)} %get-tuple-element.356.role_ref, ...), custom_call_target="tpu_custom_call", output_to_operand_aliasing={{1}: (10, {}), {2}: (11, {}), {3}: (12, {})} | custom-call | flops 2147483648 | bytes 20971520 | tf_op jit(solution)/shard_map/backward_stage/pallas_call | solution.py:347
  297.3 7.5 %collective-permute-start.54 = (s32[16,512]{1,0:T(8,128)}, s32[16,512]{1,0:T(8,128)}, u32[]{:S(2)}, u32[]{:S(2)}) collective-permute-start(s32[16,512]{1,0:T(8,128)} %concatenate.101), channel_id=1, source_target_pairs={{0,16},{1,17},{2,18},{3,19},{4,20},{5,21},{6,22},{7,23},{8,24},{9,... | collective-permute-start | bytes 98312 | tf_op jit(solution)/shard_map/ppermute | solution.py:624
  312.3 5.5 copy.253
  317.8 4.9 reshape.312
  340.3 9.4 %backward_stage.12 = (bf16[128,1024]{1,0:T(8,128)(2,1)}, bf16[4,128,1024]{2,1,0:T(8,128)(2,1)S(1)}, bf16[4,128,4096]{2,1,0:T(8,128)(2,1)S(1)}, f32[4,8,1024]{2,1,0:T(8,128)S(1)}) custom-call(s32[2]{0:T(128)S(1)} %copy-done.57, bf16[128,1024]{1,0:T(8,128)(2,1)S(1)} %get-tuple-element.290.grad_ref, ...), custom_call_target="tpu_custom_call", output_to_operand_aliasing={{1}: (10, {}), {2}: (11, {}), {3}: (12, {})} | custom-call | flops 2147483648 | bytes 20971520 | tf_op jit(solution)/shard_map/backward_stage/pallas_call | solution.py:347
  377.3 9.1 %backward_stage.13 = (bf16[128,1024]{1,0:T(8,128)(2,1)S(1)}, bf16[4,128,1024]{2,1,0:T(8,128)(2,1)S(1)}, bf16[4,128,4096]{2,1,0:T(8,128)(2,1)S(1)}, f32[4,8,1024]{2,1,0:T(8,128)S(1)}) custom-call(s32[2]{0:T(128)S(1)} %copy-done.56, bf16[128,1024]{1,0:T(8,128)(2,1)S(1)} %copy-done.50, ...), custom_call_target="tpu_custom_call", output_to_operand_aliasing={{1}: (10, {}), {2}: (11, {}), {3}: (12, {})} | custom-call | flops 2147483648 | bytes 20971520 | tf_op jit(solution)/shard_map/backward_stage/pallas_call | solution.py:347
  414.1 5.3 lead_grad.2
  421.4 6.0 lead_grad.3
  432.1 45.8 %collective-permute-start.45 = (bf16[64,512]{1,0:T(8,128)(2,1)S(1)}, bf16[64,512]{1,0:T(8,128)(2,1)S(1)}, u32[]{:S(2)}, u32[]{:S(2)}) collective-permute-start(bf16[64,512]{1,0:T(8,128)(2,1)S(1)} %get-tuple-element.312), channel_id=1, source_target_pairs={{0,64},{1,65},{2,66},{3,67},{4,68},{5,69},{6,70},{7,71},{8,72},{9,... | collective-permute-start | bytes 196616 | tf_op jit(solution)/shard_map/ppermute | solution.py:624
  477.9 6.9 %collective-permute-start.46 = (bf16[64,512]{1,0:T(8,128)(2,1)S(1)}, bf16[64,512]{1,0:T(8,128)(2,1)S(1)}, u32[]{:S(2)}, u32[]{:S(2)}) collective-permute-start(bf16[64,512]{1,0:T(8,128)(2,1)S(1)} %get-tuple-element.311), channel_id=1, source_target_pairs={{0,96},{1,97},{2,98},{3,99},{4,100},{5,101},{6,102},{7,103},{8,104... | collective-permute-start | bytes 196616 | tf_op jit(solution)/shard_map/ppermute | solution.py:624
  506.8 4.5 collective-permute-done.59
  511.3 4.2 collective-permute-done.67
  515.9 6.9 %collective-permute-start.69 = (bf16[32,512]{1,0:T(8,128)(2,1)S(1)}, bf16[32,512]{1,0:T(8,128)(2,1)S(1)}, u32[]{:S(2)}, u32[]{:S(2)}) collective-permute-start(bf16[32,512]{1,0:T(8,128)(2,1)S(1)} %add_convert_fusion.10), channel_id=1, source_target_pairs={{0,16},{1,17},{2,18},{3,19},{4,20},{5,21},{6,22},{7,23},{8,24},{9,... | collective-permute-start | bytes 98312 | tf_op jit(solution)/shard_map/ppermute | solution.py:624
  525.2 5.4 fusion.20
  537.0 4.4 collective-permute-start.83
  543.7 4.4 fusion.17
  551.0 8.0 %collective-permute-done.82 = bf16[512,1024]{1,0:T(8,128)(2,1)S(1)} collective-permute-done((bf16[512,1024]{1,0:T(8,128)(2,1)S(1)}, bf16[512,1024]{1,0:T(8,128)(2,1)S(1)}, u32[]{:S(2)}, u32[]{:S(2)}) %collective-permute-start.82) | collective-permute-done | bytes 1048608 | tf_op jit(solution)/shard_map/ppermute | solution.py:624
  564.7 5.4 collective-permute-start.61
  597.8 14.7 %collective-permute-start.88 = (bf16[128,1024]{1,0:T(8,128)(2,1)S(1)}, bf16[128,1024]{1,0:T(8,128)(2,1)S(1)}, u32[]{:S(2)}, u32[]{:S(2)}) collective-permute-start(bf16[128,1024]{1,0:T(8,128)(2,1)S(1)} %add_convert_fusion.7), channel_id=1, source_target_pairs={{32,48},{33,49},{34,50},{35,51},{36,52},{37,53},{38,54},{39,55},{4... | collective-permute-start | bytes 786440 | tf_op jit(solution)/shard_map/ppermute | solution.py:624
  616.3 14.5 %embed_sum.1 = f32[64,2000]{1,0:T(8,128)} custom-call(s32[1]{0:T(128)} %bitcast.63.base_ref, s32[16384,1]{1,0:T(8,128)S(1)} %bitcast.236, bf16[32,64,512]{2,1,0:T(8,128)(2,1)S(1)} %copy-done.55), custom_call_target="tpu_custom_call" | custom-call | flops 16777216000 | bytes 12582912 | tf_op jit(solution)/shard_map/embed_sum/pallas_call | solution.py:704
  (601 shorter events, 317.8 us)
Async XLA Ops:
  7.2 623.7 %reduce-scatter.4.cloned.1.call-start = ((), (), s32[]{:S(2)}) async-start(), calls=%async_computation.1 | async-start | bytes 4386816
  28.6 28.0 %collective-permute-start = (bf16[128,1024]{1,0:T(8,128)(2,1)}, bf16[128,1024]{1,0:T(8,128)(2,1)S(1)}, u32[]{:S(2)}, u32[]{:S(2)}) collective-permute-start(bf16[128,1024]{1,0:T(8,128)(2,1)} %pad_maximum_fusion.4), channel_id=1, source_target_pairs={{0,32},{1,33},{2,34},{3,35},{4,36},{5,37},{6,38},{7,39},{8,40},{9,... | collective-permute-start | bytes 786440 | tf_op jit(solution)/shard_map/ppermute | solution.py:624
  28.6 26.3 %collective-permute-start.1 = (bf16[128,1024]{1,0:T(8,128)(2,1)}, bf16[128,1024]{1,0:T(8,128)(2,1)S(1)}, u32[]{:S(2)}, u32[]{:S(2)}) collective-permute-start(bf16[128,1024]{1,0:T(8,128)(2,1)} %pad_maximum_fusion.4), channel_id=1, source_target_pairs={{0,64},{1,65},{2,66},{3,67},{4,68},{5,69},{6,70},{7,71},{8,72},{9,... | collective-permute-start | bytes 786440 | tf_op jit(solution)/shard_map/ppermute | solution.py:624
  34.9 19.9 %collective-permute-start.2 = (bf16[128,1024]{1,0:T(8,128)(2,1)}, bf16[128,1024]{1,0:T(8,128)(2,1)S(1)}, u32[]{:S(2)}, u32[]{:S(2)}) collective-permute-start(bf16[128,1024]{1,0:T(8,128)(2,1)} %pad_maximum_fusion.4), channel_id=1, source_target_pairs={{0,96},{1,97},{2,98},{3,99},{4,100},{5,101},{6,102},{7,103},{8,104... | collective-permute-start | bytes 786440 | tf_op jit(solution)/shard_map/ppermute | solution.py:624
  42.6 20.4 %collective-permute-start.11 = (bf16[1024,1024]{1,0:T(8,128)(2,1)}, bf16[1024,1024]{1,0:T(8,128)(2,1)S(1)}, u32[]{:S(2)}, u32[]{:S(2)}) collective-permute-start(bf16[1024,1024]{1,0:T(8,128)(2,1)} %bitcast.248), channel_id=1, source_target_pairs={{0,16},{1,17},{2,18},{3,19},{4,20},{5,21},{6,22},{7,23},{8,24},{9,... | collective-permute-start | bytes 6291464 | tf_op jit(solution)/shard_map/ppermute | solution.py:624
  104.3 46.9 %collective-permute-start.16 = (bf16[128,1024]{1,0:T(8,128)(2,1)S(1)}, bf16[128,1024]{1,0:T(8,128)(2,1)S(1)}, u32[]{:S(2)}, u32[]{:S(2)}) collective-permute-start(bf16[128,1024]{1,0:T(8,128)(2,1)S(1)} %get-tuple-element.167), channel_id=1, source_target_pairs={{64,96},{65,97},{66,98},{67,99},{68,100},{69,101},{70,102},{71,103... | collective-permute-start | bytes 786440 | tf_op jit(solution)/shard_map/ppermute | solution.py:624
  105.6 46.9 %collective-permute-start.18 = (bf16[128,1024]{1,0:T(8,128)(2,1)S(1)}, bf16[128,1024]{1,0:T(8,128)(2,1)S(1)}, u32[]{:S(2)}, u32[]{:S(2)}) collective-permute-start(bf16[128,1024]{1,0:T(8,128)(2,1)S(1)} %get-tuple-element.167), channel_id=1, source_target_pairs={{32,64},{33,65},{34,66},{35,67},{36,68},{37,69},{38,70},{39,71},{4... | collective-permute-start | bytes 786440 | tf_op jit(solution)/shard_map/ppermute | solution.py:624
  268.4 17.8 %collective-permute-start.33 = (bf16[128,1024]{1,0:T(8,128)(2,1)S(1)}, bf16[128,1024]{1,0:T(8,128)(2,1)S(1)}, u32[]{:S(2)}, u32[]{:S(2)}) collective-permute-start(bf16[128,1024]{1,0:T(8,128)(2,1)S(1)} %get-tuple-element.207), channel_id=1, source_target_pairs={{96,64},{97,65},{98,66},{99,67},{100,68},{101,69},{102,70},{103,71... | collective-permute-start | bytes 786440 | tf_op jit(solution)/shard_map/ppermute | solution.py:624
  270.5 17.7 %collective-permute-start.48 = (s32[512]{0:T(512)S(1)}, s32[512]{0:T(512)S(1)}, u32[]{:S(2)}, u32[]{:S(2)}) collective-permute-start(s32[512]{0:T(512)S(1)} %bitcast.240), channel_id=1, source_target_pairs={{0,4},{1,5},{2,6},{3,7},{4,8},{5,9},{6,10},{7,11},{8,12},{9,13},{1... | collective-permute-start | bytes 6152 | tf_op jit(solution)/shard_map/ppermute | solution.py:624
  271.8 16.4 %collective-permute-start.49 = (s32[512]{0:T(512)S(1)}, s32[512]{0:T(512)S(1)}, u32[]{:S(2)}, u32[]{:S(2)}) collective-permute-start(s32[512]{0:T(512)S(1)} %bitcast.241), channel_id=1, source_target_pairs={{0,12},{1,13},{2,14},{3,15},{4,0},{5,1},{6,2},{7,3},{8,4},{9,5},{1... | collective-permute-start | bytes 6152 | tf_op jit(solution)/shard_map/ppermute | solution.py:624
  286.2 36.5 %collective-permute-start.34 = (bf16[128,1024]{1,0:T(8,128)(2,1)}, bf16[128,1024]{1,0:T(8,128)(2,1)}, u32[]{:S(2)}, u32[]{:S(2)}) collective-permute-start(bf16[128,1024]{1,0:T(8,128)(2,1)} %get-tuple-element.216), channel_id=1, source_target_pairs={{96,64},{97,65},{98,66},{99,67},{100,68},{101,69},{102,70},{103,71... | collective-permute-start | bytes 786440 | tf_op jit(solution)/shard_map/ppermute | solution.py:624
  351.7 36.5 %collective-permute-start.36 = (bf16[128,1024]{1,0:T(8,128)(2,1)}, bf16[128,1024]{1,0:T(8,128)(2,1)}, u32[]{:S(2)}, u32[]{:S(2)}) collective-permute-start(bf16[128,1024]{1,0:T(8,128)(2,1)} %get-tuple-element.217), channel_id=1, source_target_pairs={{64,32},{65,33},{66,34},{67,35},{68,36},{69,37},{70,38},{71,39},{7... | collective-permute-start | bytes 786440 | tf_op jit(solution)/shard_map/ppermute | solution.py:624
  353.2 33.3 %collective-permute-start.35 = (bf16[128,1024]{1,0:T(8,128)(2,1)}, bf16[128,1024]{1,0:T(8,128)(2,1)}, u32[]{:S(2)}, u32[]{:S(2)}) collective-permute-start(bf16[128,1024]{1,0:T(8,128)(2,1)} %get-tuple-element.217), channel_id=1, source_target_pairs={{96,64},{97,65},{98,66},{99,67},{100,68},{101,69},{102,70},{103,71... | collective-permute-start | bytes 786440 | tf_op jit(solution)/shard_map/ppermute | solution.py:624
  429.3 95.9 %collective-permute-start.81 = (bf16[4,512,1024]{2,1,0:T(8,128)(2,1)}, bf16[4,512,1024]{2,1,0:T(8,128)(2,1)}, u32[]{:S(2)}, u32[]{:S(2)}) collective-permute-start(bf16[4,512,1024]{2,1,0:T(8,128)(2,1)} %copy-done.41), channel_id=1, source_target_pairs={{32,48},{33,49},{34,50},{35,51},{36,52},{37,53},{38,54},{39,55},{4... | collective-permute-start | bytes 12582920 | tf_op jit(solution)/shard_map/ppermute | solution.py:624
  432.1 55.2 %collective-permute-start.45 = (bf16[64,512]{1,0:T(8,128)(2,1)S(1)}, bf16[64,512]{1,0:T(8,128)(2,1)S(1)}, u32[]{:S(2)}, u32[]{:S(2)}) collective-permute-start(bf16[64,512]{1,0:T(8,128)(2,1)S(1)} %get-tuple-element.312), channel_id=1, source_target_pairs={{0,64},{1,65},{2,66},{3,67},{4,68},{5,69},{6,70},{7,71},{8,72},{9,... | collective-permute-start | bytes 196616 | tf_op jit(solution)/shard_map/ppermute | solution.py:624
  487.3 54.1 %collective-permute-start.73 = (bf16[4,256,2048]{2,1,0:T(8,128)(2,1)}, bf16[4,256,2048]{2,1,0:T(8,128)(2,1)}, u32[]{:S(2)}, u32[]{:S(2)}) collective-permute-start(bf16[4,256,2048]{2,1,0:T(8,128)(2,1)} %lead_grad.3), channel_id=1, source_target_pairs={{0,16},{1,17},{2,18},{3,19},{4,20},{5,21},{6,22},{7,23},{8,24},{9,... | collective-permute-start | bytes 12582920 | tf_op jit(solution)/shard_map/ppermute | solution.py:624
  503.0 19.8 %collective-permute-start.60 = (bf16[4,64,512]{2,1,0:T(8,128)(2,1)S(1)}, bf16[4,64,512]{2,1,0:T(8,128)(2,1)S(1)}, u32[]{:S(2)}, u32[]{:S(2)}) collective-permute-start(bf16[4,64,512]{2,1,0:T(8,128)(2,1)S(1)} %pad_maximum_fusion.6), channel_id=1, source_target_pairs={{0,2},{1,3},{2,0},{3,1},{4,6},{5,7},{6,4},{7,5},{8,10},{9,11},{10,... | collective-permute-start | bytes 786440 | tf_op jit(solution)/shard_map/ppermute | solution.py:624
  530.7 28.4 %collective-permute-start.82 = (bf16[512,1024]{1,0:T(8,128)(2,1)S(1)}, bf16[512,1024]{1,0:T(8,128)(2,1)S(1)}, u32[]{:S(2)}, u32[]{:S(2)}) collective-permute-start(bf16[512,1024]{1,0:T(8,128)(2,1)S(1)} %get-tuple-element.275), channel_id=1, source_target_pairs={{32,36},{33,37},{34,38},{35,39},{36,40},{37,41},{38,42},{39,43},{4... | collective-permute-start | bytes 3145736 | tf_op jit(solution)/shard_map/ppermute | solution.py:624
  537.0 27.7 %collective-permute-start.83 = (bf16[512,1024]{1,0:T(8,128)(2,1)}, bf16[512,1024]{1,0:T(8,128)(2,1)}, u32[]{:S(2)}, u32[]{:S(2)}) collective-permute-start(bf16[512,1024]{1,0:T(8,128)(2,1)} %get-tuple-element.277), channel_id=1, source_target_pairs={{32,44},{33,45},{34,46},{35,47},{36,32},{37,33},{38,34},{39,35},{4... | collective-permute-start | bytes 3145736 | tf_op jit(solution)/shard_map/ppermute | solution.py:624
  541.4 28.6 %collective-permute-start.84 = (bf16[512,1024]{1,0:T(8,128)(2,1)S(1)}, bf16[512,1024]{1,0:T(8,128)(2,1)}, u32[]{:S(2)}, u32[]{:S(2)}) collective-permute-start(bf16[512,1024]{1,0:T(8,128)(2,1)S(1)} %get-tuple-element.276), channel_id=1, source_target_pairs={{32,40},{33,41},{34,42},{35,43},{36,44},{37,45},{38,46},{39,47},{4... | collective-permute-start | bytes 3145736 | tf_op jit(solution)/shard_map/ppermute | solution.py:624
  548.1 31.3 %collective-permute-start.74 = (bf16[256,2048]{1,0:T(8,128)(2,1)}, bf16[256,2048]{1,0:T(8,128)(2,1)}, u32[]{:S(2)}, u32[]{:S(2)}) collective-permute-start(bf16[256,2048]{1,0:T(8,128)(2,1)} %get-tuple-element.278), channel_id=1, source_target_pairs={{0,4},{1,5},{2,6},{3,7},{4,8},{5,9},{6,10},{7,11},{8,12},{9,13},{1... | collective-permute-start | bytes 3145736 | tf_op jit(solution)/shard_map/ppermute | solution.py:624
  548.3 35.7 %collective-permute-start.75 = (bf16[256,2048]{1,0:T(8,128)(2,1)}, bf16[256,2048]{1,0:T(8,128)(2,1)}, u32[]{:S(2)}, u32[]{:S(2)}) collective-permute-start(bf16[256,2048]{1,0:T(8,128)(2,1)} %get-tuple-element.280), channel_id=1, source_target_pairs={{0,12},{1,13},{2,14},{3,15},{4,0},{5,1},{6,2},{7,3},{8,4},{9,5},{1... | collective-permute-start | bytes 3145736 | tf_op jit(solution)/shard_map/ppermute | solution.py:624
  560.0 26.2 %collective-permute-start.76 = (bf16[256,2048]{1,0:T(8,128)(2,1)}, bf16[256,2048]{1,0:T(8,128)(2,1)}, u32[]{:S(2)}, u32[]{:S(2)}) collective-permute-start(bf16[256,2048]{1,0:T(8,128)(2,1)} %get-tuple-element.279), channel_id=1, source_target_pairs={{0,8},{1,9},{2,10},{3,11},{4,12},{5,13},{6,14},{7,15},{8,0},{9,1},... | collective-permute-start | bytes 3145736 | tf_op jit(solution)/shard_map/ppermute | solution.py:624
  564.7 25.3 %collective-permute-start.61 = (bf16[16,64,512]{2,1,0:T(8,128)(2,1)}, bf16[16,64,512]{2,1,0:T(8,128)(2,1)S(1)}, u32[]{:S(2)}, u32[]{:S(2)}) collective-permute-start(bf16[16,64,512]{2,1,0:T(8,128)(2,1)} %copy-done.111), channel_id=1, source_target_pairs={{0,16},{1,17},{2,18},{3,19},{4,20},{5,21},{6,22},{7,23},{8,24},{9,... | collective-permute-start | bytes 3145736 | tf_op jit(solution)/shard_map/ppermute | solution.py:624
  574.0 17.3 %collective-permute-start.85 = (bf16[128,1024]{1,0:T(8,128)(2,1)S(1)}, bf16[128,1024]{1,0:T(8,128)(2,1)S(1)}, u32[]{:S(2)}, u32[]{:S(2)}) collective-permute-start(bf16[128,1024]{1,0:T(8,128)(2,1)S(1)} %get-tuple-element.283), channel_id=1, source_target_pairs={{32,33},{33,34},{34,35},{35,32},{36,37},{37,38},{38,39},{39,36},{4... | collective-permute-start | bytes 786440 | tf_op jit(solution)/shard_map/ppermute | solution.py:624
  579.5 18.2 %collective-permute-start.86 = (bf16[128,1024]{1,0:T(8,128)(2,1)S(1)}, bf16[128,1024]{1,0:T(8,128)(2,1)S(1)}, u32[]{:S(2)}, u32[]{:S(2)}) collective-permute-start(bf16[128,1024]{1,0:T(8,128)(2,1)S(1)} %get-tuple-element.285), channel_id=1, source_target_pairs={{32,35},{33,32},{34,33},{35,34},{36,39},{37,36},{38,37},{39,38},{4... | collective-permute-start | bytes 786440 | tf_op jit(solution)/shard_map/ppermute | solution.py:624
  589.7 22.7 %collective-permute-start.77 = (bf16[64,2048]{1,0:T(8,128)(2,1)S(1)}, bf16[64,2048]{1,0:T(8,128)(2,1)S(1)}, u32[]{:S(2)}, u32[]{:S(2)}) collective-permute-start(bf16[64,2048]{1,0:T(8,128)(2,1)S(1)} %get-tuple-element.286), channel_id=1, source_target_pairs={{0,1},{1,2},{2,3},{3,0},{4,5},{5,6},{6,7},{7,4},{8,9},{9,10},{10,1... | collective-permute-start | bytes 786440 | tf_op jit(solution)/shard_map/ppermute | solution.py:624
  590.0 22.5 %collective-permute-start.78 = (bf16[64,2048]{1,0:T(8,128)(2,1)S(1)}, bf16[64,2048]{1,0:T(8,128)(2,1)S(1)}, u32[]{:S(2)}, u32[]{:S(2)}) collective-permute-start(bf16[64,2048]{1,0:T(8,128)(2,1)S(1)} %get-tuple-element.288), channel_id=1, source_target_pairs={{0,3},{1,0},{2,1},{3,2},{4,7},{5,4},{6,5},{7,6},{8,11},{9,8},{10,9... | collective-permute-start | bytes 786440 | tf_op jit(solution)/shard_map/ppermute | solution.py:624
  591.3 21.2 %collective-permute-start.79 = (bf16[64,2048]{1,0:T(8,128)(2,1)S(1)}, bf16[64,2048]{1,0:T(8,128)(2,1)S(1)}, u32[]{:S(2)}, u32[]{:S(2)}) collective-permute-start(bf16[64,2048]{1,0:T(8,128)(2,1)S(1)} %get-tuple-element.287), channel_id=1, source_target_pairs={{0,2},{1,3},{2,0},{3,1},{4,6},{5,7},{6,4},{7,5},{8,10},{9,11},{10,... | collective-permute-start | bytes 786440 | tf_op jit(solution)/shard_map/ppermute | solution.py:624
  597.8 16.4 %collective-permute-start.88 = (bf16[128,1024]{1,0:T(8,128)(2,1)S(1)}, bf16[128,1024]{1,0:T(8,128)(2,1)S(1)}, u32[]{:S(2)}, u32[]{:S(2)}) collective-permute-start(bf16[128,1024]{1,0:T(8,128)(2,1)S(1)} %add_convert_fusion.7), channel_id=1, source_target_pairs={{32,48},{33,49},{34,50},{35,51},{36,52},{37,53},{38,54},{39,55},{4... | collective-permute-start | bytes 786440 | tf_op jit(solution)/shard_map/ppermute | solution.py:624
  612.6 18.8 %collective-permute-start.80 = (bf16[64,2048]{1,0:T(8,128)(2,1)S(1)}, bf16[64,2048]{1,0:T(8,128)(2,1)S(1)}, u32[]{:S(2)}, u32[]{:S(2)}) collective-permute-start(bf16[64,2048]{1,0:T(8,128)(2,1)S(1)} %add_convert_fusion.8), channel_id=1, source_target_pairs={{0,16},{1,17},{2,18},{3,19},{4,20},{5,21},{6,22},{7,23},{8,24},{9,... | collective-permute-start | bytes 786440 | tf_op jit(solution)/shard_map/ppermute | solution.py:624
  614.2 16.6 %collective-permute-start.89 = (bf16[128,512]{1,0:T(8,128)(2,1)S(1)}, bf16[128,512]{1,0:T(8,128)(2,1)S(1)}, u32[]{:S(2)}, u32[]{:S(2)}) collective-permute-start(bf16[128,512]{1,0:T(8,128)(2,1)S(1)} %dynamic-slice_select_fusion), channel_id=1, source_target_pairs={{32,0},{33,1},{34,2},{35,3},{36,4},{37,5},{38,6},{39,7},{40,8},{41... | collective-permute-start | bytes 393224 | tf_op jit(solution)/shard_map/ppermute | solution.py:624
  (190 other events, 1731.7 us)
Sparse Core Ops, SparseCore 0:
  322.9 77.2 reduce-scatter.3

commit v3 on v2

--- a/solution.py
+++ b/solution.py
@@ -1,3 +1,4 @@
+import functools
 import itertools
 
 import jax
@@ -73,30 +74,31 @@
     return pl.ds(pl.multiple_of(at, 128), size)
 
 
-def hold_kernel(lead_in, down_in, lead_ref, down_ref, sem):
-    copies = [
-        pltpu.make_async_copy(lead_in, lead_ref, sem.at[0]),
-        pltpu.make_async_copy(down_in, down_ref, sem.at[1]),
-    ]
-    for copy in copies:
-        copy.start()
-    for copy in copies:
-        copy.wait()
-
-
-def hold(lead, down):
+def hold_kernel(source_ref, held_ref, sem):
+    copy = pltpu.make_async_copy(source_ref, held_ref, sem)
+    copy.start()
+    copy.wait()
+
+
+def hold(value):
     return pl.pallas_call(
         hold_kernel,
-        out_shape=[pltpu.VMEM(lead.shape, LOW), pltpu.VMEM(down.shape, LOW)],
-        in_specs=[HBM_SPEC] * 2,
-        out_specs=[VMEM_SPEC] * 2,
-        scratch_shapes=[pltpu.SemaphoreType.DMA((2,))],
+        out_shape=pltpu.VMEM(value.shape, value.dtype),
+        in_specs=[HBM_SPEC],
+        out_specs=VMEM_SPEC,
+        scratch_shapes=[pltpu.SemaphoreType.DMA],
         compiler_params=pltpu.CompilerParams(vmem_limit_bytes=4 << 20),
         name="hold",
-    )(lead, down)
-
-
-def forward_kernel(
+    )(far(value))
+
+
+def forward_kernel(with_down, *refs):
+    if not with_down:
+        refs = refs[:6] + (None,) + refs[6:]
+    forward_body(*refs)
+
+
+def forward_body(
     role_ref,
     entry_ref,
     seg_col_ref,
@@ -117,6 +119,8 @@
     saved_buf,
     inner_buf,
     result_buf,
+    scores_buf,
+    probs_buf,
     out_sems,
 ):
     role, slot = role_ref[0], role_ref[1]
@@ -137,26 +141,39 @@
 
     @pl.when(role == 1)
     def _():
-        @pl.loop(0, 3 * width // CHUNK)
+        @pl.loop(0, 3 * width // CHUNK, unroll=2)
         def _(j):
             at = lanes(j * CHUNK, CHUNK)
             saved_buf[:, at] = matmul(normed_buf[...], lead_ref[:, at]).astype(LOW)
 
-        same = seg_col_ref[slot] == seg_row_ref[slot]
         left = lax.broadcasted_iota(jnp.int32, (tokens, 128), 1) < HEAD_SIZE
         zero = jnp.zeros((tokens, 128), LOW)
 
-        @pl.loop(0, HEADS // 4)
-        def _(quad):
-            for which in range(2):
-                at = quad * 256 + which * 128
+        @pl.loop(0, HEADS // 8)
+        def _(group):
+            for pair in range(4):
+                at = group * 512 + pair * 128
                 query = saved_buf[:, lanes(at, 128)]
                 key = saved_buf[:, lanes(width + at, 128)]
+                scores_buf[group * 8 + 2 * pair] = matmul_nt(jnp.where(left, query, zero), key)
+                scores_buf[group * 8 + 2 * pair + 1] = matmul_nt(jnp.where(left, zero, query), key)
+
+        @pl.loop(0, HEADS // 4)
+        def _(group):
+            same = seg_col_ref[slot] == seg_row_ref[slot]
+            for head in range(4):
+                at = group * 4 + head
+                probs_buf[at] = head_probs(scores_buf[at], same).astype(LOW)
+
+        @pl.loop(0, HEADS // 8)
+        def _(group):
+            for pair in range(4):
+                at = group * 512 + pair * 128
                 value = saved_buf[:, lanes(2 * width + at, 128)]
-                probs_a = head_probs(matmul_nt(jnp.where(left, query, zero), key), same)
-                probs_b = head_probs(matmul_nt(jnp.where(left, zero, query), key), same)
                 mixed = jnp.where(
-                    left, matmul(probs_a.astype(LOW), value), matmul(probs_b.astype(LOW), value)
+                    left,
+                    matmul(probs_buf[group * 8 + 2 * pair], value),
+                    matmul(probs_buf[group * 8 + 2 * pair + 1], value),
                 )
                 saved_buf[:, lanes(3 * width + at, 128)] = mixed.astype(LOW)
 
@@ -168,11 +185,10 @@
             term = matmul(saved_buf[:, 3 * width :], lead_ref[:, lanes(3 * width + j * CHUNK, CHUNK)])
             out_ref[:, at] = (entry_ref[:, at].astype(WIDE) + term).astype(LOW)
 
-    @pl.when(role == 2)
-    def _():
+    def feed_forward():
         result_buf[...] = entry_ref[...].astype(WIDE)
 
-        @pl.loop(0, lead_ref.shape[1] // CHUNK)
+        @pl.loop(0, lead_ref.shape[1] // CHUNK, unroll=2)
         def _(j):
             at = lanes(j * CHUNK, CHUNK)
             inner = matmul(normed_buf[...], lead_ref[:, at])
@@ -186,6 +202,9 @@
         out_ref[...] = result_buf[...].astype(LOW)
         keep_inner.wait()
 
+    if down_ref is not None:
+        pl.when(role == 2)(feed_forward)
+
     @pl.when(role > 0)
     def _():
         for keep in keeps:
@@ -194,31 +213,38 @@
 
 def pinned(value):
     return pltpu.with_memory_space_constraint(value, pltpu.VMEM)
+
+
+def far(value):
+    return pltpu.with_memory_space_constraint(value, pltpu.HBM)
 
 
 def forward_stage(role, entry, seg_col, seg_row, gain, lead, down, kept):
     tokens, width = entry.shape
     hidden = lead.shape[1]
+    count = 5 if down is None else 6
     return pl.pallas_call(
-        forward_kernel,
+        functools.partial(forward_kernel, down is not None),
         out_shape=[jax.ShapeDtypeStruct(entry.shape, LOW)]
         + [jax.ShapeDtypeStruct(k.shape, k.dtype) for k in kept],
-        in_specs=[SMEM_SPEC] + [VMEM_SPEC] * 6 + [HBM_SPEC] * 4,
+        in_specs=[SMEM_SPEC] + [VMEM_SPEC] * count + [HBM_SPEC] * 4,
         out_specs=[VMEM_SPEC] + [HBM_SPEC] * 4,
         scratch_shapes=[
             pltpu.VMEM((tokens, width), LOW),
             pltpu.VMEM((tokens, hidden), LOW),
             pltpu.VMEM((tokens, hidden), WIDE),
             pltpu.VMEM((tokens, width), WIDE),
+            pltpu.VMEM((HEADS, tokens, tokens), WIDE),
+            pltpu.VMEM((HEADS, tokens, tokens), LOW),
             pltpu.SemaphoreType.DMA((4,)),
         ],
-        input_output_aliases={7: 1, 8: 2, 9: 3, 10: 4},
-        compiler_params=pltpu.CompilerParams(vmem_limit_bytes=14 << 20),
+        input_output_aliases={count + 1 + i: 1 + i for i in range(4)},
+        compiler_params=pltpu.CompilerParams(vmem_limit_bytes=18 << 20),
         cost_estimate=pl.CostEstimate(
             flops=4 * tokens * width * hidden, bytes_accessed=20 << 20, transcendentals=0
         ),
         name="forward_stage",
-    )(role, entry, seg_col, seg_row, gain, pinned(lead), pinned(down), *kept)
+    )(role, entry, seg_col, seg_row, gain, pinned(lead), *([pinned(down)] if down is not None else []), *map(far, kept))
 
 
 def backward_kernel(
@@ -246,6 +272,10 @@
     gain_buf,
     entry_buf,
     normed_buf,
+    scores_buf,
+    probs_grad_buf,
+    probs_buf,
+    scores_grad_buf,
     in_sems,
     out_sems,
 ):
@@ -258,6 +288,14 @@
     keep_grads = pltpu.make_async_copy(grads_buf, grads_ref.at[slot], out_sems.at[1])
     keep_gain = pltpu.make_async_copy(gain_buf, gains_ref.at[slot], out_sems.at[2])
 
+    @pl.when(role == 2)
+    def _():
+        bring_inner.start()
+
+    @pl.when(role == 1)
+    def _():
+        bring_saved.start()
+
     @pl.when(role > 0)
     def _():
         bring_entry.start()
@@ -266,54 +304,71 @@
 
     @pl.when(role == 1)
     def _():
-        bring_saved.start()
         grads_buf[:, 3 * width :] = grad_ref[...]
         mixed_buf[...] = matmul_nt(grad_ref[...], lead_ref[:, 3 * width :]).astype(LOW)
         bring_saved.wait()
-        same = seg_col_ref[slot] == seg_row_ref[slot]
         left = lax.broadcasted_iota(jnp.int32, (tokens, 128), 1) < HEAD_SIZE
         zero = jnp.zeros((tokens, 128), LOW)
         scale = HEAD_SIZE ** (-0.5)
 
-        @pl.loop(0, HEADS // 2)
-        def _(pair):
-            at = pair * 128
-            query = saved_buf[:, lanes(at, 128)]
-            key = saved_buf[:, lanes(width + at, 128)]
-            value = saved_buf[:, lanes(2 * width + at, 128)]
-            grad = mixed_buf[:, lanes(at, 128)]
-            parts = []
-            for own in (0, 1):
-                mine = lambda v: jnp.where(left, v, zero) if own == 0 else jnp.where(left, zero, v)
-                probs = head_probs(matmul_nt(mine(query), key), same)
-                grad_probs = matmul_nt(mine(grad), value)
-                grad_scores = probs * (
-                    grad_probs - jnp.sum(probs * grad_probs, axis=-1, keepdims=True)
-                )
-                grad_low = grad_scores.astype(LOW)
-                parts.append(
-                    (
-                        matmul(grad_low, key) * scale,
-                        matmul_tn(grad_low, query) * scale,
-                        matmul_tn(probs.astype(LOW), grad),
+        @pl.loop(0, HEADS // 8)
+        def _(group):
+            for pair in range(4):
+                at = group * 512 + pair * 128
+                query = saved_buf[:, lanes(at, 128)]
+                key = saved_buf[:, lanes(width + at, 128)]
+                value = saved_buf[:, lanes(2 * width + at, 128)]
+                grad = mixed_buf[:, lanes(at, 128)]
+                for own in (0, 1):
+                    mine = lambda v: jnp.where(left, v, zero) if own == 0 else jnp.where(left, zero, v)
+                    scores_buf[group * 8 + 2 * pair + own] = matmul_nt(mine(query), key)
+                    probs_grad_buf[group * 8 + 2 * pair + own] = matmul_nt(mine(grad), value)
+
+        @pl.loop(0, HEADS // 4)
+        def _(group):
+            same = seg_col_ref[slot] == seg_row_ref[slot]
+            for head in range(4):
+                at = group * 4 + head
+                probs = head_probs(scores_buf[at], same)
+                probs_buf[at] = probs.astype(LOW)
+                grad_probs = probs_grad_buf[at]
+                scores_grad_buf[at] = (
+                    probs * (grad_probs - jnp.sum(probs * grad_probs, axis=-1, keepdims=True))
+                ).astype(LOW)
+
+        @pl.loop(0, HEADS // 4)
+        def _(group):
+            for pair in range(2):
+                at = group * 256 + pair * 128
+                query = saved_buf[:, lanes(at, 128)]
+                key = saved_buf[:, lanes(width + at, 128)]
+                grad = mixed_buf[:, lanes(at, 128)]
+                parts = []
+                for own in (0, 1):
+                    probs = probs_buf[group * 4 + 2 * pair + own]
+                    grad_low = scores_grad_buf[group * 4 + 2 * pair + own]
+                    parts.append(
+                        (
+                            matmul(grad_low, key) * scale,
+                            matmul_tn(grad_low, query) * scale,
+                            matmul_tn(probs, grad),
+                        )
                     )
-                )
-            for which in range(3):
-                grads_buf[:, lanes(which * width + at, 128)] = jnp.where(
-                    left, parts[0][which], parts[1][which]
-                ).astype(LOW)
-
-        @pl.loop(0, 3 * width // CHUNK)
+                for which in range(3):
+                    grads_buf[:, lanes(which * width + at, 128)] = jnp.where(
+                        left, parts[0][which], parts[1][which]
+                    ).astype(LOW)
+
+        @pl.loop(0, 3 * width // CHUNK, unroll=2)
         def _(j):
             at = lanes(j * CHUNK, CHUNK)
             normed_buf[...] += matmul_nt(grads_buf[:, at], lead_ref[:, at])
 
     @pl.when(role == 2)
     def _():
-        bring_inner.start()
         bring_inner.wait()
 
-        @pl.loop(0, lead_ref.shape[1] // CHUNK)
+        @pl.loop(0, lead_ref.shape[1] // CHUNK, unroll=2)
         def _(j):
             at = lanes(j * CHUNK, CHUNK)
             grad_active = matmul_nt(grad_ref[...], down_ref[pl.ds(j * CHUNK, CHUNK), :])
@@ -358,11 +413,15 @@
             pltpu.VMEM((8, width), WIDE),
             pltpu.VMEM((tokens, width), LOW),
             pltpu.VMEM((tokens, width), WIDE),
+            pltpu.VMEM((HEADS, tokens, tokens), WIDE),
+            pltpu.VMEM((HEADS, tokens, tokens), WIDE),
+            pltpu.VMEM((HEADS, tokens, tokens), LOW),
+            pltpu.VMEM((HEADS, tokens, tokens), LOW),
             pltpu.SemaphoreType.DMA((3,)),
             pltpu.SemaphoreType.DMA((3,)),
         ],
         input_output_aliases={10: 1, 11: 2, 12: 3},
-        compiler_params=pltpu.CompilerParams(vmem_limit_bytes=14 << 20),
+        compiler_params=pltpu.CompilerParams(vmem_limit_bytes=18 << 20),
         cost_estimate=pl.CostEstimate(
             flops=4 * tokens * width * hidden, bytes_accessed=20 << 20, transcendentals=0
         ),
@@ -375,10 +434,10 @@
         gain,
         pinned(lead),
         pinned(down),
-        entries,
-        saved,
-        inner,
-        *totals,
+        far(entries),
+        far(saved),
+        far(inner),
+        *map(far, totals),
     )
 
 
@@ -412,12 +471,12 @@
             pl.BlockSpec((tile, emb), lambda i: (i, 0)),
         ],
         out_specs=[whole, whole],
-        compiler_params=pltpu.CompilerParams(vmem_limit_bytes=30 << 20),
+        compiler_params=pltpu.CompilerParams(vmem_limit_bytes=32 << 20),
         cost_estimate=pl.CostEstimate(
             flops=2 * tokens * vocab * emb, bytes_accessed=5 << 20, transcendentals=tokens * vocab
         ),
         name="head_stats",
-    )(readout, table)
+    )(readout, far(table))
 
 
 def head_kernel(base_ref, readout_ref, table_ref, logsum_ref, ids_ref, head_ref, grad_ref):
@@ -427,7 +486,10 @@
     hits = lax.broadcasted_iota(jnp.int32, logits.shape, 0) == ids
     probs = jnp.exp(logits - logsum_ref[...])
     grads = jnp.where(hits, probs - 1.0, probs).astype(LOW)
-    head_ref[...] = matmul(grads, readout_ref[...]).astype(LOW)
+    head = matmul(grads, readout_ref[...])
+    unit = tile // 4
+    for shard in range(4):
+        head_ref[shard, :unit] = head[shard * unit : (shard + 1) * unit].astype(LOW)
     term = matmul_tn(grads, table_ref[...])
 
     @pl.when(pl.program_id(0) == 0)
@@ -439,49 +501,71 @@
         grad_ref[...] += term
 
 
-def head_grads(base, readout, table, logsum, ids, tile):
+def head_grads(base, readout, table, logsum, ids):
     tokens, emb = readout.shape
     vocab = table.shape[0]
     row = pl.BlockSpec((1, tokens), lambda i: (0, 0))
     whole = pl.BlockSpec((tokens, emb), lambda i: (0, 0))
-    part = pl.BlockSpec((tile, emb), lambda i: (i, 0))
+    part = pl.BlockSpec((vocab // 4, emb), lambda i: (i, 0))
     return pl.pallas_call(
         head_kernel,
         out_shape=[
-            jax.ShapeDtypeStruct((vocab, emb), LOW),
+            jax.ShapeDtypeStruct((16, 512, emb), LOW),
             jax.ShapeDtypeStruct((tokens, emb), WIDE),
         ],
-        grid=(vocab // tile,),
+        grid=(4,),
         in_specs=[SMEM_SPEC, whole, part, row, row],
-        out_specs=[part, whole],
-        compiler_params=pltpu.CompilerParams(vmem_limit_bytes=30 << 20),
+        out_specs=[pl.BlockSpec((4, 512, emb), lambda i: (i, 0, 0)), whole],
+        compiler_params=pltpu.CompilerParams(vmem_limit_bytes=32 << 20),
         cost_estimate=pl.CostEstimate(
             flops=6 * tokens * vocab * emb, bytes_accessed=9 << 20, transcendentals=tokens * vocab
         ),
         name="head_grads",
-    )(base, readout, table, logsum, ids)
-
-
-def lookup_kernel(ids_ref, table_ref, noise_ref, out_ref, total_ref):
+    )(base, readout, far(table), logsum, ids)
+
+
+def pair_kernel(former_ref, latter_ref, out_ref):
+    rows = out_ref.shape[0]
+    out_ref[...] = former_ref[:rows].astype(WIDE) + latter_ref[:rows].astype(WIDE)
+
+
+def pair_sum(former, latter, rows):
+    return pl.pallas_call(
+        pair_kernel,
+        out_shape=jax.ShapeDtypeStruct((rows, former.shape[1]), WIDE),
+        in_specs=[VMEM_SPEC] * 2,
+        out_specs=VMEM_SPEC,
+        compiler_params=pltpu.CompilerParams(vmem_limit_bytes=8 << 20),
+        name="pair_sum",
+    )(former, latter)
+
+
+def lookup_kernel(ids_ref, table_ref, noise_ref, out_ref, total_ref, low_ref):
     step = pl.program_id(0)
-    tile = table_ref.shape[1]
+    parts, tile = table_ref.shape
     tokens = ids_ref.shape[1]
-    ids = ids_ref[...] - step * tile
-    hits = lax.broadcasted_iota(jnp.int32, (tile, tokens), 0) == ids
-    hits = jnp.where(hits, 1.0, 0.0).astype(LOW)
-    term = matmul(table_ref[...], hits)
+    blocks = tile // 128
 
     @pl.when(step == 0)
     def _():
-        total_ref[...] = term
-
-    @pl.when(step > 0)
-    def _():
-        total_ref[...] += term
+        lane = jnp.bitwise_and(ids_ref[...], 127)
+        hits = lax.broadcasted_iota(jnp.int32, (128, tokens), 0) == lane
+        low_ref[...] = jnp.where(hits, 1.0, 0.0).astype(LOW)
+        total_ref[...] = noise_ref[...].astype(WIDE)
+
+    stacked = jnp.concatenate(
+        [table_ref[:, block * 128 : (block + 1) * 128] for block in range(blocks)]
+    )
+    found = matmul(stacked, low_ref[...])
+    own = jnp.right_shift(ids_ref[...], 7) - step * blocks
+    total = jnp.zeros_like(total_ref)
+    for block in range(blocks):
+        total = jnp.where(own == block, found[block * parts : (block + 1) * parts], total)
+    total_ref[...] += total
 
     @pl.when(step == pl.num_programs(0) - 1)
     def _():
-        out_ref[...] = (total_ref[...] + noise_ref[...].astype(WIDE)).astype(LOW)
+        out_ref[...] = total_ref[...].astype(LOW)
 
 
 def lookup(ids, table, noise, tile):
@@ -498,13 +582,13 @@
             whole,
         ],
         out_specs=whole,
-        scratch_shapes=[pltpu.VMEM((parts, tokens), WIDE)],
-        compiler_params=pltpu.CompilerParams(vmem_limit_bytes=30 << 20),
+        scratch_shapes=[pltpu.VMEM((parts, tokens), WIDE), pltpu.VMEM((128, tokens), LOW)],
+        compiler_params=pltpu.CompilerParams(vmem_limit_bytes=32 << 20),
         cost_estimate=pl.CostEstimate(
             flops=2 * 128 * vocab * tokens, bytes_accessed=4 << 20, transcendentals=0
         ),
         name="lookup",
-    )(ids, table, noise)
+    )(ids, far(table), noise)
 
 
 def lead_grad_kernel(where_ref, normed_ref, mixed_ref, grads_ref, out_ref, turned_ref):
@@ -559,7 +643,7 @@
             flops=4 * tokens * width * width, bytes_accessed=8 << 20, transcendentals=0
         ),
         name="lead_grad",
-    )(where, normed, saved, grads)
+    )(where, far(normed), far(saved), far(grads))
 
 
 def down_grad_kernel(where_ref, saved_ref, nexts_ref, out_ref):
@@ -605,7 +689,66 @@
             flops=2 * tokens * width * hidden // 2, bytes_accessed=8 << 20, transcendentals=0
         ),
         name="down_grad",
-    )(where, saved, nexts)
+    )(where, far(saved), far(nexts))
+
+
+def embed_kernel(base_ref, ids_ref, grad_ref, out_ref, total_ref):
+    step = pl.program_id(0)
+    count, parts, tokens = grad_ref.shape
+    blocks = total_ref.shape[0] // parts
+    term = None
+    for at in range(count):
+        ids = ids_ref[at] - base_ref[0]
+        lane = jnp.bitwise_and(ids, 127)
+        hits = lax.broadcasted_iota(jnp.int32, (128, tokens), 0) == lane
+        hits = jnp.where(hits, 1.0, 0.0).astype(LOW)
+        own = jnp.right_shift(ids, 7)
+        grads = grad_ref[at]
+        masked = jnp.concatenate(
+            [grads * jnp.where(own == block, 1.0, 0.0).astype(LOW) for block in range(blocks)]
+        )
+        part = matmul_nt(masked, hits)
+        term = part if term is None else term + part
+
+    @pl.when(step == 0)
+    def _():
+        total_ref[...] = term
+
+    @pl.when(step > 0)
+    def _():
+        total_ref[...] += term
+
+    @pl.when(step == pl.num_programs(0) - 1)
+    def _():
+        rows = out_ref.shape[1]
+        for block in range(blocks):
+            size = min(128, rows - block * 128)
+            out_ref[:, block * 128 : block * 128 + size] = total_ref[
+                block * parts : (block + 1) * parts, :size
+            ]
+
+
+def embed_sum(base, ids, grads, rows):
+    count, parts, tokens = grads.shape
+    step = 4
+    blocks = -(-rows // 128)
+    return pl.pallas_call(
+        embed_kernel,
+        out_shape=jax.ShapeDtypeStruct((parts, rows), WIDE),
+        grid=(count // step,),
+        in_specs=[
+            SMEM_SPEC,
+            pl.BlockSpec((step, 1, tokens), lambda i: (i, 0, 0)),
+            pl.BlockSpec((step, parts, tokens), lambda i: (i, 0, 0)),
+        ],
+        out_specs=pl.BlockSpec((parts, rows), lambda i: (0, 0)),
+        scratch_shapes=[pltpu.VMEM((blocks * parts, 128), WIDE)],
+        compiler_params=pltpu.CompilerParams(vmem_limit_bytes=32 << 20),
+        cost_estimate=pl.CostEstimate(
+            flops=2 * count * tokens * parts * rows, bytes_accessed=3 << 20, transcendentals=0
+        ),
+        name="embed_sum",
+    )(base, ids.reshape(count, 1, tokens), grads)
 
 
 ROW_LEN = 128
@@ -656,22 +799,32 @@
     return lax.dynamic_slice_in_dim(values, block * size, size, 0)
 
 
-def reduce_plane(mine, got, second, sections=range(SEC)):
+def plane_first(mine, got, sections=range(SEC)):
     piece = lambda by: mine[by] if got is None else (mine[by].astype(WIDE) + got[by].astype(WIDE))
-    total = piece(0).astype(WIDE)
+    pieces = [piece(by).astype(LOW) for by in range(4)]
+    return (pieces, [plane_route(pieces[by], by, True, sections) for by in TURNS])
+
+
+def plane_second(first, second, sections=range(SEC)):
+    pieces, arrived = first
+    total = pieces[0].astype(WIDE)
+    for piece in arrived:
+        total = total + piece.astype(WIDE)
+    total = total.astype(LOW)
+    result = row_block(total, second, 4).astype(WIDE)
     for by in TURNS:
-        total = total + plane_route(piece(by).astype(LOW), by, True, sections).astype(WIDE)
-    lowered = total.astype(LOW)
-    result = row_block(total, second, 4)
-    for by in TURNS:
-        block = row_block(lowered, (second + by) % 4, 4)
+        block = row_block(total, (second + by) % 4, 4)
         result = result + plane_route(block, by, False, sections).astype(WIDE)
     return result.astype(LOW)
 
 
+def gather_own(values):
+    blocks = jnp.stack([values] + [plane_route(values, by, True) for by in TURNS])
+    return jnp.concatenate([blocks] + [plane_route(blocks, by, False) for by in TURNS])
+
+
 def gather_plane(values):
-    blocks = jnp.stack([values] + [plane_route(values, by, True) for by in TURNS])
-    blocks = jnp.concatenate([blocks] + [plane_route(blocks, by, False) for by in TURNS])
+    blocks = gather_own(values)
     return jnp.concatenate([blocks, swap_cores(blocks)])
 
 
@@ -682,41 +835,6 @@
         out_specs=[HBM_SPEC] * len(kinds),
         name="empty",
     )()
-
-
-def embed_kernel(base_ref, ids_ref, grad_ref, out_ref):
-    @pl.when(pl.program_id(0) == 0)
-    def _():
-        out_ref[...] = jnp.zeros_like(out_ref)
-
-    tokens = grad_ref.shape[2]
-    local = ids_ref[...] - base_ref[0]
-    for block in range(grad_ref.shape[0]):
-        ids = local[block * tokens : (block + 1) * tokens]
-        hits = lax.broadcasted_iota(jnp.int32, (tokens, out_ref.shape[1]), 1) == ids
-        hits = jnp.where(hits, 1.0, 0.0).astype(LOW)
-        out_ref[...] += jnp.dot(grad_ref[block], hits, preferred_element_type=WIDE)
-
-
-def embed_sum(base, ids, grads, rows):
-    count, parts, tokens = grads.shape
-    step = 4
-    return pl.pallas_call(
-        embed_kernel,
-        out_shape=jax.ShapeDtypeStruct((parts, rows), WIDE),
-        grid=(count // step,),
-        in_specs=[
-            pl.BlockSpec(memory_space=pltpu.SMEM),
-            pl.BlockSpec((step * tokens, 1), lambda i: (i, 0)),
-            pl.BlockSpec((step, parts, tokens), lambda i: (i, 0, 0)),
-        ],
-        out_specs=pl.BlockSpec((parts, rows), lambda i: (0, 0)),
-        compiler_params=pltpu.CompilerParams(vmem_limit_bytes=40 << 20),
-        cost_estimate=pl.CostEstimate(
-            flops=2 * count * tokens * 256 * rows, bytes_accessed=12 << 20, transcendentals=0
-        ),
-        name="embed_sum",
-    )(base, ids.reshape(count * tokens, 1), grads)
 
 
 def local(
@@ -754,23 +872,24 @@
     seg_col = segment_ids.reshape(micro, tokens, 1)
     flat_ids = token_ids.reshape(-1)
 
+    to_first = lambda v: [v] + [link(v, s, 0) for s in range(1, SEC)]
+    eighth = row_block(row_block(own_down, core, 2), first_at, 4)
+    eighth = jnp.where(section == 1, link(eighth, 0, 1), link(eighth, 2, 3))
     noise = noise_input[:, 0].transpose(2, 0, 1).reshape(emb_part, -1)
     own_embedded = lookup(flat_ids[None], embed_table.T, noise, 3200)
-    small_pack = jnp.concatenate((input_proj, readout_proj.T))
-    packs = {by: turn(small_pack, by) for by in TURNS}
-    packs[0] = small_pack
-    pack_of = lambda s: lax.select_n((section - s) % SEC, *[packs[by] for by in range(SEC)])
-    packed = [pack_of(s) for s in range(SEC)]
-    input_full = jnp.concatenate([p[:emb_part] for p in packed])
-    readout_full = jnp.concatenate([p[emb_part:] for p in packed])
-    parts = {by: turn(after(own_embedded, packs[by]), by) for by in TURNS}
+    inputs = to_first(input_proj)
+    input_full = jnp.concatenate(inputs)
     embedded = jnp.concatenate(
-        [own_embedded] + [parts[SEC - s] for s in range(1, SEC)]
+        [own_embedded] + [link(after(own_embedded, inputs[s]), s, 0) for s in range(1, SEC)]
     )
     first_in = matmul_tn(embedded, input_full).astype(LOW).reshape(micro, tokens, width)
-
-    eighth = row_block(row_block(own_down, core, 2), first_at, 4)
-    eighth = jnp.where(section == 1, link(eighth, 0, 1), link(eighth, 2, 3))
+    held_lead = hold(lead)
+    readout_own = after(readout_proj.T, first_in)
+    readout_full = jnp.concatenate(
+        [link(readout_own, s, last) for s in range(last)] + [readout_own]
+    )
+
+    eighth = after(eighth, own_embedded)
     upper = jnp.zeros((4,) + eighth.shape, LOW)
     upper = lax.dynamic_update_index_in_dim(upper, eighth, first_at, 0)
     for by in TURNS:
@@ -779,15 +898,16 @@
         )
     upper = upper.reshape(half_rows // 2, width)
     upper_other = swap_cores(upper)
-    full_down = jnp.concatenate(
-        (
-            jnp.where(core == 0, upper, upper_other),
-            jnp.where(core == 0, upper_other, upper),
-            own_down,
+    held_down = hold(
+        jnp.concatenate(
+            (
+                jnp.where(core == 0, upper, upper_other),
+                jnp.where(core == 0, upper_other, upper),
+                own_down,
+            )
         )
     )
     all_ids = gather_plane(after(flat_ids, upper_other))
-    held = hold(lead, full_down)
 
     kept = empty(
         ((micro, tokens, width), LOW),
@@ -821,8 +941,17 @@
             entry = first_in[step]
         elif step < micro:
             entry = jnp.where(section == 0, first_in[step], entry)
+        if step == 5:
+            entry = after(entry, all_ids)
         out, *kept = forward_stage(
-            role_at(step - 2 * section), entry, seg_col, seg_row, gain_half, *held, kept
+            role_at(step - 2 * section),
+            entry,
+            seg_col,
+            seg_row,
+            gain_half,
+            held_lead,
+            held_down if step > 1 else None,
+            kept,
         )
         outs.append(out)
         for s in range(last):
@@ -839,22 +968,20 @@
     sent = [link(readout, last, s) for s in range(last)]
     for s in range(last):
         readout = jnp.where(section == s, sent[s], readout)
-    peak, total = head_stats(readout, head_table, 1600)
+    peak, total = head_stats(readout, head_table, 2000)
     stats = jnp.concatenate((peak, total))
     all_stats = jnp.stack([stats] + [turn(stats, by) for by in TURNS])
     peak = jnp.max(all_stats[:, 0], axis=0)
     total = jnp.sum(all_stats[:, 1] * jnp.exp(all_stats[:, 0] - peak), axis=0)
     logsum = (peak + jnp.log(total))[None]
     head_grad, grad_readout = head_grads(
-        (section * vocab_part).reshape(1), readout, head_table, logsum, flat_ids[None], 1600
+        (section * vocab_part).reshape(1), readout, head_table, logsum, flat_ids[None]
     )
     grad_low = grad_readout.astype(LOW)
     for s in range(last):
         grad_readout = grad_readout + link(grad_low, s, last).astype(WIDE)
     grad_readout = grad_readout.astype(LOW)
-    head_grad = lax.psum_scatter(
-        head_grad.reshape(NX * NY, vocab_part // (NX * NY), emb), "row", scatter_dimension=0
-    )
+    head_grad = lax.psum_scatter(head_grad, "row", scatter_dimension=0)
     readout_grad = matmul_tn(final_low, grad_readout)
     grad_final = matmul(grad_readout, readout_full)
     final_gain_grad = jnp.sum(grad_final * normed_f, axis=0)
@@ -873,13 +1000,16 @@
             grad_next = last_grads[step]
         elif step < micro:
             grad_next = jnp.where(section == last, last_grads[step], grad_next)
+        if step == steps - 1:
+            grad_next = after(grad_next, head_grad)
         out, *totals = backward_stage(
             role_at(step - 2 * (last - section)),
             grad_next,
             seg_col,
             seg_row,
             gain_half,
-            *held,
+            held_lead,
+            held_down,
             entries,
             saved,
             inner,
@@ -894,13 +1024,7 @@
     first_grads = jnp.concatenate(outs[2 * last :])
     noise_grad = matmul_nt(input_full, first_grads).astype(LOW)
     pieces = noise_grad.reshape(SEC, emb_part, all_tokens)
-    noise_grad = pieces[0]
-    for s in TURNS:
-        noise_grad = jnp.where(section == s, turn(pieces[s], s), noise_grad)
-    embed_grad = embed_sum(
-        (row * (vocab // 16)).reshape(1), all_ids, gather_plane(noise_grad), vocab // 16
-    ).T
-    noise_out = noise_grad.reshape(emb_part, micro, tokens).transpose(1, 2, 0).astype(WIDE)
+    sent = [link(pieces[s], 0, s) for s in range(1, SEC)]
 
     grad_nexts, grads, gain_grads = totals
     gain_grad = jnp.sum(gain_grads[:, 0], axis=0)
@@ -919,9 +1043,18 @@
     lead_mine = lead_grad(where_mine, normed, saved, grads)
     down_got = swap_cores(down_grad(where_other, saved, grad_nexts), odd)
     down_mine = down_grad(where_mine, saved, grad_nexts)
-    lead_part = reduce_plane(lead_mine, lead_got, second_at)
-    down_part = reduce_plane(down_mine, down_got, second_at, odd)
+    lead_first = plane_first(lead_mine, lead_got)
+    down_first = plane_first(down_mine, down_got, odd)
+    noise_grad = pieces[0]
+    for s in range(1, SEC):
+        noise_grad = jnp.where(section == s, sent[s - 1], noise_grad)
+    blocks = gather_own(after(noise_grad, (lead_first[0], down_first[0])))
+    lead_part = plane_second(lead_first, second_at)
+    down_part = plane_second(down_first, second_at, odd)
     lead_out = both(lead_part, swap_cores(lead_part)).astype(WIDE)
+    blocks = jnp.concatenate([blocks, swap_cores(blocks)])
+    embed_grad = embed_sum((row * (vocab // 16)).reshape(1), all_ids, blocks, vocab // 16).T
+    noise_out = noise_grad.reshape(emb_part, micro, tokens).transpose(1, 2, 0).astype(WIDE)
 
     down_other = swap_cores(down_part, odd)
     upper_part = jnp.where(core == 0, down_part, down_other)
@@ -956,7 +1089,8 @@
     small = jnp.stack(
         [lax.dynamic_index_in_dim(small, (first_at + by) % 4, 0, False) for by in range(4)]
     )
-    small_part = reduce_plane(small.reshape(4, NY * 32, width // 2), None, second_at)
+    small = after(small, (lead_part, down_part)).reshape(4, NY * 32, width // 2)
+    small_part = plane_second(plane_first(small, None), second_at)
     small = both(small_part, swap_cores(small_part))
     gain_out = small[16, :64].astype(WIDE)
     input_rows = small[:16].reshape(SEC, 4, width)
@@ -981,7 +1115,7 @@
         readout_out = jnp.where(here, part[:4].reshape(64, 64), readout_out)
         final_out = jnp.where(here, part[4, :16], final_out)
 
-    head_out = head_grad.astype(WIDE) + swap_cores(head_grad).astype(WIDE)
+    head_out = pair_sum(head_grad, swap_cores(head_grad), vocab_part // (NX * NY))
     return (
         noise_out[:, None],
         embed_grad,

time: 652 us -> 575 us (0.88)
  the two profiles are of different devices: /device:TPU:103 before, /device:TPU:1 now
where the time goes in v3:
time: 575 us; the launch traced here: 564 us
  starting transfers between devices  162 us (28%)
  waiting for transfers between devices  152 us (26%)
  Pallas kernels  137 us (24%)
  local copies, waits for them, and re-layouts  53.4 us (9%)
  other arithmetic  39.1 us (7%)
  between operations  16.6 us (3%)
    ppermute x96, starting transfers between devices, route(): return lax.ppermute(value, ALL, pairs)  162 us
    ppermute x96, waiting for transfers between devices, route(): return lax.ppermute(value, ALL, pairs)  151 us
    pallas_call x10, Pallas kernels, backward_stage(): pl.pallas_call(backward_kernel, out_shape=[jax.ShapeDtypeStruct(grad.shap...  41.9 us
    unnamed x102, local copies, waits for them, and re-layouts  40.7 us
    pallas_call x10, Pallas kernels, forward_stage(): pl.pallas_call(functools.partial(forward_kernel, down is not None), out_s...  29.1 us
    pallas_call x2, Pallas kernels, lead_grad(): pl.pallas_call(lead_grad_kernel, out_shape=jax.ShapeDtypeStruct((4, width...  15.1 us
  transfers between devices with their start and end apart: 97, of which 24 were waited for; matrix products, arithmetic and copies ran while one was open for 10% of the time, Pallas kernels for 16%

profile of v3, /device:TPU:1, one launch (start us, length us, event | category | flops | bytes accessed | tf_op | source)
XLA Modules:
  0.0 563.7 jit_solution(16753087044803890140)
XLA Ops:
  8.5 4.4 collective-permute-start.7
  14.3 8.7 %lookup.1 = bf16[64,512]{1,0:T(8,128)(2,1)S(1)} custom-call(s32[1,512]{1,0:T(1,128)S(1)} %bitcast.213, bf16[64,32000]{1,0:T(8,128)(2,1)} %bitcast.257, bf16[64,512]{1,0:T(8,128)(2,1)S(1)} %copy_bitcast_fusion.noise_ref), custom_call_target="tpu_custom_call" | custom-call | flops 4194304000 | bytes 4194304 | tf_op jit(solution)/shard_map/lookup/pallas_call | solution.py:575
  40.0 4.6 collective-permute-start.12
  60.9 6.2 %forward_stage.10 = (bf16[128,1024]{1,0:T(8,128)(2,1)S(1)}, bf16[4,128,1024]{2,1,0:T(8,128)(2,1)}, bf16[4,128,1024]{2,1,0:T(8,128)(2,1)}, bf16[4,128,4096]{2,1,0:T(8,128)(2,1)}, f32[4,128,4096]{2,1,0:T(8,128)}) custom-call(s32[2]{0:T(128)S(1)} %get-tuple-element.350.refs_0_, ...), custom_call_target="tpu_custom_call", output_to_operand_aliasing={{1}: (6, {}), {2}: (7, {}), {3}: (8, {}), {4}: (9, {})} | custom-call | flops 2147483648 | bytes 20971520 | tf_op jit(solution)/shard_map/forward_stage/pallas_call | solution.py:226
  68.5 6.3 %forward_stage.11 = (bf16[128,1024]{1,0:T(8,128)(2,1)S(1)}, bf16[4,128,1024]{2,1,0:T(8,128)(2,1)}, bf16[4,128,1024]{2,1,0:T(8,128)(2,1)}, bf16[4,128,4096]{2,1,0:T(8,128)(2,1)}, f32[4,128,4096]{2,1,0:T(8,128)}) custom-call(s32[2]{0:T(128)S(1)} %get-tuple-element.351.refs_0_, ...), custom_call_target="tpu_custom_call", output_to_operand_aliasing={{1}: (6, {}), {2}: (7, {}), {3}: (8, {}), {4}: (9, {})} | custom-call | flops 2147483648 | bytes 20971520 | tf_op jit(solution)/shard_map/forward_stage/pallas_call | solution.py:226
  78.1 4.2 collective-permute-done.14
  90.7 4.1 pad_maximum_fusion.source_ref
  99.5 6.3 %forward_stage.12 = (bf16[128,1024]{1,0:T(8,128)(2,1)S(1)}, bf16[4,128,1024]{2,1,0:T(8,128)(2,1)}, bf16[4,128,1024]{2,1,0:T(8,128)(2,1)}, bf16[4,128,4096]{2,1,0:T(8,128)(2,1)}, f32[4,128,4096]{2,1,0:T(8,128)}) custom-call(s32[2]{0:T(128)S(1)} %get-tuple-element.348.refs_0_, ...), custom_call_target="tpu_custom_call", output_to_operand_aliasing={{1}: (7, {}), {2}: (8, {}), {3}: (9, {}), {4}: (10, {})} | custom-call | flops 2147483648 | bytes 20971520 | tf_op jit(solution)/shard_map/forward_stage/pallas_call | solution.py:226
  106.5 5.0 collective-permute-start.15
  119.4 4.1 collective-permute-start.26
  130.3 6.3 %forward_stage.13 = (bf16[128,1024]{1,0:T(8,128)(2,1)S(1)}, bf16[4,128,1024]{2,1,0:T(8,128)(2,1)}, bf16[4,128,1024]{2,1,0:T(8,128)(2,1)}, bf16[4,128,4096]{2,1,0:T(8,128)(2,1)}, f32[4,128,4096]{2,1,0:T(8,128)}) custom-call(s32[2]{0:T(128)S(1)} %get-tuple-element.349.refs_0_, ...), custom_call_target="tpu_custom_call", output_to_operand_aliasing={{1}: (7, {}), {2}: (8, {}), {3}: (9, {}), {4}: (10, {})} | custom-call | flops 2147483648 | bytes 20971520 | tf_op jit(solution)/shard_map/forward_stage/pallas_call | solution.py:226
  161.0 43.9 %collective-permute-done.36 = bf16[512,256]{1,0:T(8,128)(2,1)S(1)} collective-permute-done((bf16[512,256]{1,0:T(8,128)(2,1)S(1)}, bf16[512,256]{1,0:T(8,128)(2,1)S(1)}, u32[]{:S(2)}, u32[]{:S(2)}) %collective-permute-start.36) | collective-permute-done | bytes 262176 | tf_op jit(solution)/shard_map/ppermute | solution.py:767
  205.0 6.6 %head_stats.1 = (f32[1,512]{1,0:T(1,128)S(1)}, f32[1,512]{1,0:T(1,128)S(1)}) custom-call(bf16[512,256]{1,0:T(8,128)(2,1)S(1)} %select_select_fusion.readout_ref, bf16[8000,256]{1,0:T(8,128)(2,1)} %table_ref.3), custom_call_target="tpu_custom_call" | custom-call | flops 2097152000 | bytes 5242880 | tf_op jit(solution)/shard_map/head_stats/pallas_call | solution.py:465
  211.7 6.0 %collective-permute-start.38 = (f32[2,512]{1,0:T(2,128)S(1)}, f32[2,512]{1,0:T(2,128)S(1)}, u32[]{:S(2)}, u32[]{:S(2)}) collective-permute-start(f32[2,512]{1,0:T(2,128)S(1)} %get-tuple-element.341), channel_id=1, source_target_pairs={{0,96},{1,97},{2,98},{3,99},{4,100},{5,101},{6,102},{7,103},{8,104... | collective-permute-start | bytes 12296 | tf_op jit(solution)/shard_map/ppermute | solution.py:767
  221.4 10.3 %head_grads.1 = (bf16[16,512,256]{2,1,0:T(8,128)(2,1)S(1)}, f32[512,256]{1,0:T(8,128)S(1)}) custom-call(s32[1]{0:T(128)} %bitcast.44.base_ref, bf16[512,256]{1,0:T(8,128)(2,1)S(1)} %select_select_fusion.readout_ref, bf16[8000,256]{1,0:T(8,128)(2,1)} %table_ref.3, f32[1,512]{1,0:T(1,128)S(1)} %bitcast.221, s32[1,512]{1,0:T(1,128)S(1)} %bitcast.220), custom_call_target="tpu_custom_call" | custom-call | flops 6291456000 | bytes 9437184 | tf_op jit(solution)/shard_map/head_grads/pallas_call | solution.py:510
  235.2 3.6 collective-permute-start.40
  239.1 8.7 %collective-permute-done.40 = bf16[512,256]{1,0:T(8,128)(2,1)S(1)} collective-permute-done((bf16[512,256]{1,0:T(8,128)(2,1)S(1)}, bf16[512,256]{1,0:T(8,128)(2,1)S(1)}, u32[]{:S(2)}, u32[]{:S(2)}) %collective-permute-start.40) | collective-permute-done | bytes 262176 | tf_op jit(solution)/shard_map/ppermute | solution.py:767
  274.0 51.5 %collective-permute-done.49 = bf16[128,1024]{1,0:T(8,128)(2,1)S(1)} collective-permute-done((bf16[128,1024]{1,0:T(8,128)(2,1)S(1)}, bf16[128,1024]{1,0:T(8,128)(2,1)S(1)}, u32[]{:S(2)}, u32[]{:S(2)}) %collective-permute-start.49) | collective-permute-done | bytes 262176 | tf_op jit(solution)/shard_map/ppermute | solution.py:767
  327.6 9.1 %backward_stage.16 = (bf16[128,1024]{1,0:T(8,128)(2,1)S(1)}, bf16[4,128,1024]{2,1,0:T(8,128)(2,1)}, bf16[4,128,4096]{2,1,0:T(8,128)(2,1)}, f32[4,8,1024]{2,1,0:T(8,128)}) custom-call(s32[2]{0:T(128)S(1)} %pad_add_fusion.1.role_ref, ...), custom_call_target="tpu_custom_call", output_to_operand_aliasing={{1}: (10, {}), {2}: (11, {}), {3}: (12, {})} | custom-call | flops 2147483648 | bytes 20971520 | tf_op jit(solution)/shard_map/backward_stage/pallas_call | solution.py:402
  340.0 9.2 %backward_stage.17 = (bf16[128,1024]{1,0:T(8,128)(2,1)S(1)}, bf16[4,128,1024]{2,1,0:T(8,128)(2,1)}, bf16[4,128,4096]{2,1,0:T(8,128)(2,1)}, f32[4,8,1024]{2,1,0:T(8,128)}) custom-call(s32[2]{0:T(128)S(1)} %pad_add_fusion.18.role_ref, ...), custom_call_target="tpu_custom_call", output_to_operand_aliasing={{1}: (10, {}), {2}: (11, {}), {3}: (12, {})} | custom-call | flops 2147483648 | bytes 20971520 | tf_op jit(solution)/shard_map/backward_stage/pallas_call | solution.py:402
  352.7 9.1 %backward_stage.18 = (bf16[128,1024]{1,0:T(8,128)(2,1)S(1)}, bf16[4,128,1024]{2,1,0:T(8,128)(2,1)}, bf16[4,128,4096]{2,1,0:T(8,128)(2,1)}, f32[4,8,1024]{2,1,0:T(8,128)}) custom-call(s32[2]{0:T(128)S(1)} %get-tuple-element.354.role_ref, ...), custom_call_target="tpu_custom_call", output_to_operand_aliasing={{1}: (10, {}), {2}: (11, {}), {3}: (12, {})} | custom-call | flops 2147483648 | bytes 20971520 | tf_op jit(solution)/shard_map/backward_stage/pallas_call | solution.py:402
  369.4 9.1 %backward_stage.19 = (bf16[128,1024]{1,0:T(8,128)(2,1)S(1)}, bf16[4,128,1024]{2,1,0:T(8,128)(2,1)}, bf16[4,128,4096]{2,1,0:T(8,128)(2,1)}, f32[4,8,1024]{2,1,0:T(8,128)}) custom-call(s32[2]{0:T(128)S(1)} %get-tuple-element.355.role_ref, ...), custom_call_target="tpu_custom_call", output_to_operand_aliasing={{1}: (10, {}), {2}: (11, {}), {3}: (12, {})} | custom-call | flops 2147483648 | bytes 20971520 | tf_op jit(solution)/shard_map/backward_stage/pallas_call | solution.py:402
  378.5 7.9 %lead_grad.3 = bf16[4,256,2048]{2,1,0:T(8,128)(2,1)} custom-call(s32[3]{0:T(128)S(1)} %pad_add_fusion.22.where_ref, bf16[512,1024]{1,0:T(8,128)(2,1)} %bitcast.228, bf16[512,4096]{1,0:T(8,128)(2,1)} %bitcast.222, bf16[512,4096]{1,0:T(8,128)(2,1)} %bitcast.226), custom_call_target="tpu_custom_call" | custom-call | flops 2147483648 | bytes 8388608 | tf_op jit(solution)/shard_map/lead_grad/pallas_call | solution.py:627
  386.5 4.3 collective-permute-start.58
  390.7 4.0 down_grad.3
  408.2 7.1 %lead_grad.2 = bf16[4,256,2048]{2,1,0:T(8,128)(2,1)S(1)} custom-call(s32[3]{0:T(128)S(1)} %pad_add_fusion.21.where_ref, bf16[512,1024]{1,0:T(8,128)(2,1)} %bitcast.229, bf16[512,4096]{1,0:T(8,128)(2,1)} %bitcast.224, bf16[512,4096]{1,0:T(8,128)(2,1)} %bitcast.227), custom_call_target="tpu_custom_call" | custom-call | flops 2147483648 | bytes 8388608 | tf_op jit(solution)/shard_map/lead_grad/pallas_call | solution.py:627
  415.3 5.7 %fusion.14 = (bf16[256,2048]{1,0:T(8,128)(2,1)S(1)}, bf16[256,2048]{1,0:T(8,128)(2,1)S(1)}, bf16[256,2048]{1,0:T(8,128)(2,1)}) fusion(bf16[4,256,2048]{2,1,0:T(8,128)(2,1)} %collective-permute-done.58, bf16[4,256,2048]{2,1,0:T(8,128)(2,1)S(1)} %lead_grad.2), kind=kLoop, calls=%fused_computation.33 | loop fusion | flops 6291456 | bytes 9437184 | tf_op jit(solution)/shard_map/convert_element_type | solution.py:804
  438.9 8.1 %collective-permute-done.69 = bf16[256,2048]{1,0:T(8,128)(2,1)S(1)} collective-permute-done((bf16[256,2048]{1,0:T(8,128)(2,1)S(1)}, bf16[256,2048]{1,0:T(8,128)(2,1)S(1)}, u32[]{:S(2)}, u32[]{:S(2)}) %collective-permute-start.69) | collective-permute-done | bytes 1048608 | tf_op jit(solution)/shard_map/ppermute | solution.py:767
  473.0 3.7 collective-permute-done.82
  484.4 6.2 %collective-permute-start.90 = (bf16[64,2048]{1,0:T(8,128)(2,1)}, bf16[64,2048]{1,0:T(8,128)(2,1)}, u32[]{:S(2)}, u32[]{:S(2)}) collective-permute-start(bf16[64,2048]{1,0:T(8,128)(2,1)} %add_convert_fusion.12), channel_id=1, source_target_pairs={{0,16},{1,17},{2,18},{3,19},{4,20},{5,21},{6,22},{7,23},{8,24},{9,... | collective-permute-start | bytes 786440 | tf_op jit(solution)/shard_map/ppermute | solution.py:767
  495.8 28.9 %collective-permute-start.89 = (bf16[5,1024]{1,0:T(8,128)(2,1)S(1)}, bf16[5,1024]{1,0:T(8,128)(2,1)S(1)}, u32[]{:S(2)}, u32[]{:S(2)}) collective-permute-start(bf16[5,1024]{1,0:T(8,128)(2,1)S(1)} %pad_maximum_fusion.13), channel_id=1, source_target_pairs={{0,32},{1,33},{2,34},{3,35},{4,36},{5,37},{6,38},{7,39},{8,40},{9,... | collective-permute-start | bytes 30728 | tf_op jit(solution)/shard_map/ppermute | solution.py:767
  545.1 11.3 %embed_sum.1 = f32[64,2000]{1,0:T(8,128)} custom-call(s32[1]{0:T(128)} %bitcast.69.base_ref, s32[32,1,512]{2,1,0:T(1,128)S(1)} %reshape.291.ids_ref, bf16[32,64,512]{2,1,0:T(8,128)(2,1)S(1)} %constant_dynamic-update-slice_fusion.15.grad_ref), custom_call_target="tpu_custom_call" | custom-call | flops 4194304000 | bytes 3145728 | tf_op jit(solution)/shard_map/embed_sum/pallas_call | solution.py:735
  (439 shorter events, 232.6 us)
Async XLA Ops:
  7.2 355.4 %reduce-scatter.4.cloned.1.call-start = ((), (), s32[]{:S(2)}) async-start(), calls=%async_computation.1 | async-start | bytes 4456448
  24.9 27.1 %collective-permute-start = (bf16[64,1024]{1,0:T(8,128)(2,1)}, bf16[64,1024]{1,0:T(8,128)(2,1)}, u32[]{:S(2)}, u32[]{:S(2)}) collective-permute-start(bf16[64,1024]{1,0:T(8,128)(2,1)} %param.15), channel_id=1, source_target_pairs={{32,0},{33,1},{34,2},{35,3},{36,4},{37,5},{38,6},{39,7},{40,8},{41... | collective-permute-start | bytes 393224 | tf_op jit(solution)/shard_map/ppermute | solution.py:767
  26.1 24.5 %collective-permute-start.1 = (bf16[64,1024]{1,0:T(8,128)(2,1)}, bf16[64,1024]{1,0:T(8,128)(2,1)}, u32[]{:S(2)}, u32[]{:S(2)}) collective-permute-start(bf16[64,1024]{1,0:T(8,128)(2,1)} %param.15), channel_id=1, source_target_pairs={{64,0},{65,1},{66,2},{67,3},{68,4},{69,5},{70,6},{71,7},{72,8},{73... | collective-permute-start | bytes 393224 | tf_op jit(solution)/shard_map/ppermute | solution.py:767
  33.1 16.2 %collective-permute-start.2 = (bf16[64,1024]{1,0:T(8,128)(2,1)}, bf16[64,1024]{1,0:T(8,128)(2,1)}, u32[]{:S(2)}, u32[]{:S(2)}) collective-permute-start(bf16[64,1024]{1,0:T(8,128)(2,1)} %param.15), channel_id=1, source_target_pairs={{96,0},{97,1},{98,2},{99,3},{100,4},{101,5},{102,6},{103,7},{104,8... | collective-permute-start | bytes 393224 | tf_op jit(solution)/shard_map/ppermute | solution.py:767
  40.0 43.4 %collective-permute-start.12 = (bf16[1024,1024]{1,0:T(8,128)(2,1)S(1)}, bf16[1024,1024]{1,0:T(8,128)(2,1)}, u32[]{:S(2)}, u32[]{:S(2)}) collective-permute-start(bf16[1024,1024]{1,0:T(8,128)(2,1)S(1)} %bitcast.233), channel_id=1, source_target_pairs={{0,16},{1,17},{2,18},{3,19},{4,20},{5,21},{6,22},{7,23},{8,24},{9,... | collective-permute-start | bytes 6291464 | tf_op jit(solution)/shard_map/ppermute | solution.py:767
  83.4 28.1 %collective-permute-start.20 = (s32[512]{0:T(512)S(1)}, s32[512]{0:T(512)S(1)}, u32[]{:S(2)}, u32[]{:S(2)}) collective-permute-start(s32[512]{0:T(512)S(1)} %bitcast.214), channel_id=1, source_target_pairs={{0,4},{1,5},{2,6},{3,7},{4,8},{5,9},{6,10},{7,11},{8,12},{9,13},{1... | collective-permute-start | bytes 6152 | tf_op jit(solution)/shard_map/ppermute | solution.py:767
  84.8 26.7 %collective-permute-start.21 = (s32[512]{0:T(512)S(1)}, s32[512]{0:T(512)S(1)}, u32[]{:S(2)}, u32[]{:S(2)}) collective-permute-start(s32[512]{0:T(512)S(1)} %bitcast.215), channel_id=1, source_target_pairs={{0,12},{1,13},{2,14},{3,15},{4,0},{5,1},{6,2},{7,3},{8,4},{9,5},{1... | collective-permute-start | bytes 6152 | tf_op jit(solution)/shard_map/ppermute | solution.py:767
  86.3 25.2 %collective-permute-start.22 = (s32[512]{0:T(512)S(1)}, s32[512]{0:T(512)S(1)}, u32[]{:S(2)}, u32[]{:S(2)}) collective-permute-start(s32[512]{0:T(512)S(1)} %bitcast.216), channel_id=1, source_target_pairs={{0,8},{1,9},{2,10},{3,11},{4,12},{5,13},{6,14},{7,15},{8,0},{9,1},... | collective-permute-start | bytes 6152 | tf_op jit(solution)/shard_map/ppermute | solution.py:767
  105.8 33.9 %collective-permute-start.13 = (bf16[128,1024]{1,0:T(8,128)(2,1)S(1)}, bf16[128,1024]{1,0:T(8,128)(2,1)S(1)}, u32[]{:S(2)}, u32[]{:S(2)}) collective-permute-start(bf16[128,1024]{1,0:T(8,128)(2,1)S(1)} %get-tuple-element.157), channel_id=1, source_target_pairs={{32,64},{33,65},{34,66},{35,67},{36,68},{37,69},{38,70},{39,71},{4... | collective-permute-start | bytes 786440 | tf_op jit(solution)/shard_map/ppermute | solution.py:767
  106.5 33.9 %collective-permute-start.15 = (bf16[128,1024]{1,0:T(8,128)(2,1)S(1)}, bf16[128,1024]{1,0:T(8,128)(2,1)S(1)}, u32[]{:S(2)}, u32[]{:S(2)}) collective-permute-start(bf16[128,1024]{1,0:T(8,128)(2,1)S(1)} %get-tuple-element.157), channel_id=1, source_target_pairs={{0,32},{1,33},{2,34},{3,35},{4,36},{5,37},{6,38},{7,39},{8,40},{9,... | collective-permute-start | bytes 786440 | tf_op jit(solution)/shard_map/ppermute | solution.py:767
  116.6 41.1 %collective-permute-start.33 = (bf16[64,1024]{1,0:T(8,128)(2,1)S(1)}, bf16[64,1024]{1,0:T(8,128)(2,1)S(1)}, u32[]{:S(2)}, u32[]{:S(2)}) collective-permute-start(bf16[64,1024]{1,0:T(8,128)(2,1)S(1)} %bitcast.258), channel_id=1, source_target_pairs={{64,96},{65,97},{66,98},{67,99},{68,100},{69,101},{70,102},{71,103... | collective-permute-start | bytes 393224 | tf_op jit(solution)/shard_map/ppermute | solution.py:767
  117.2 40.4 %collective-permute-start.32 = (bf16[64,1024]{1,0:T(8,128)(2,1)S(1)}, bf16[64,1024]{1,0:T(8,128)(2,1)S(1)}, u32[]{:S(2)}, u32[]{:S(2)}) collective-permute-start(bf16[64,1024]{1,0:T(8,128)(2,1)S(1)} %bitcast.259), channel_id=1, source_target_pairs={{32,96},{33,97},{34,98},{35,99},{36,100},{37,101},{38,102},{39,103... | collective-permute-start | bytes 393224 | tf_op jit(solution)/shard_map/ppermute | solution.py:767
  119.4 17.2 %collective-permute-start.26 = (s32[16,512]{1,0:T(8,128)S(1)}, s32[16,512]{1,0:T(8,128)S(1)}, u32[]{:S(2)}, u32[]{:S(2)}) collective-permute-start(s32[16,512]{1,0:T(8,128)S(1)} %concatenate.93), channel_id=1, source_target_pairs={{0,16},{1,17},{2,18},{3,19},{4,20},{5,21},{6,22},{7,23},{8,24},{9,... | collective-permute-start | bytes 98312 | tf_op jit(solution)/shard_map/ppermute | solution.py:767
  136.6 21.1 %collective-permute-start.31 = (bf16[64,1024]{1,0:T(8,128)(2,1)S(1)}, bf16[64,1024]{1,0:T(8,128)(2,1)S(1)}, u32[]{:S(2)}, u32[]{:S(2)}) collective-permute-start(bf16[64,1024]{1,0:T(8,128)(2,1)S(1)} %bitcast.260), channel_id=1, source_target_pairs={{0,96},{1,97},{2,98},{3,99},{4,100},{5,101},{6,102},{7,103},{8,104... | collective-permute-start | bytes 393224 | tf_op jit(solution)/shard_map/ppermute | solution.py:767
  159.7 45.2 %collective-permute-start.36 = (bf16[512,256]{1,0:T(8,128)(2,1)S(1)}, bf16[512,256]{1,0:T(8,128)(2,1)S(1)}, u32[]{:S(2)}, u32[]{:S(2)}) collective-permute-start(bf16[512,256]{1,0:T(8,128)(2,1)S(1)} %convolution_convert_fusion.2), channel_id=1, source_target_pairs={{96,0},{97,1},{98,2},{99,3},{100,4},{101,5},{102,6},{103,7},{104,8... | collective-permute-start | bytes 786440 | tf_op jit(solution)/shard_map/ppermute | solution.py:767
  269.9 55.6 %collective-permute-start.49 = (bf16[128,1024]{1,0:T(8,128)(2,1)S(1)}, bf16[128,1024]{1,0:T(8,128)(2,1)S(1)}, u32[]{:S(2)}, u32[]{:S(2)}) collective-permute-start(bf16[128,1024]{1,0:T(8,128)(2,1)S(1)} %get-tuple-element.231), channel_id=1, source_target_pairs={{32,0},{33,1},{34,2},{35,3},{36,4},{37,5},{38,6},{39,7},{40,8},{41... | collective-permute-start | bytes 786440 | tf_op jit(solution)/shard_map/ppermute | solution.py:767
  271.2 55.6 %collective-permute-start.48 = (bf16[128,1024]{1,0:T(8,128)(2,1)S(1)}, bf16[128,1024]{1,0:T(8,128)(2,1)S(1)}, u32[]{:S(2)}, u32[]{:S(2)}) collective-permute-start(bf16[128,1024]{1,0:T(8,128)(2,1)S(1)} %get-tuple-element.231), channel_id=1, source_target_pairs={{64,32},{65,33},{66,34},{67,35},{68,36},{69,37},{70,38},{71,39},{7... | collective-permute-start | bytes 786440 | tf_op jit(solution)/shard_map/ppermute | solution.py:767
  386.5 28.8 %collective-permute-start.58 = (bf16[4,256,2048]{2,1,0:T(8,128)(2,1)}, bf16[4,256,2048]{2,1,0:T(8,128)(2,1)}, u32[]{:S(2)}, u32[]{:S(2)}) collective-permute-start(bf16[4,256,2048]{2,1,0:T(8,128)(2,1)} %lead_grad.3), channel_id=1, source_target_pairs={{0,16},{1,17},{2,18},{3,19},{4,20},{5,21},{6,22},{7,23},{8,24},{9,... | collective-permute-start | bytes 12582920 | tf_op jit(solution)/shard_map/ppermute | solution.py:767
  394.7 38.3 %collective-permute-start.59 = (bf16[4,512,1024]{2,1,0:T(8,128)(2,1)}, bf16[4,512,1024]{2,1,0:T(8,128)(2,1)}, u32[]{:S(2)}, u32[]{:S(2)}) collective-permute-start(bf16[4,512,1024]{2,1,0:T(8,128)(2,1)} %down_grad.3), channel_id=1, source_target_pairs={{32,48},{33,49},{34,50},{35,51},{36,52},{37,53},{38,54},{39,55},{4... | collective-permute-start | bytes 12582920 | tf_op jit(solution)/shard_map/ppermute | solution.py:767
  401.1 22.5 %collective-permute-start.55 = (bf16[64,512]{1,0:T(8,128)(2,1)}, bf16[64,512]{1,0:T(8,128)(2,1)}, u32[]{:S(2)}, u32[]{:S(2)}) collective-permute-start(bf16[64,512]{1,0:T(8,128)(2,1)} %get-tuple-element.315), channel_id=1, source_target_pairs={{0,96},{1,97},{2,98},{3,99},{4,100},{5,101},{6,102},{7,103},{8,104... | collective-permute-start | bytes 196616 | tf_op jit(solution)/shard_map/ppermute | solution.py:767
  403.0 21.4 %collective-permute-start.56 = (bf16[64,512]{1,0:T(8,128)(2,1)}, bf16[64,512]{1,0:T(8,128)(2,1)}, u32[]{:S(2)}, u32[]{:S(2)}) collective-permute-start(bf16[64,512]{1,0:T(8,128)(2,1)} %get-tuple-element.314), channel_id=1, source_target_pairs={{0,64},{1,65},{2,66},{3,67},{4,68},{5,69},{6,70},{7,71},{8,72},{9,... | collective-permute-start | bytes 196616 | tf_op jit(solution)/shard_map/ppermute | solution.py:767
  408.2 23.4 %collective-permute-start.67 = (bf16[16,32,512]{2,0,1:T(8,128)(2,1)}, bf16[16,32,512]{2,0,1:T(8,128)(2,1)}, u32[]{:S(2)}, u32[]{:S(2)}) collective-permute-start(bf16[16,32,512]{2,0,1:T(8,128)(2,1)} %constant_dynamic-slice_fusion.19), channel_id=1, source_target_pairs={{0,16},{1,17},{2,18},{3,19},{4,20},{5,21},{6,22},{7,23},{8,24},{9,... | collective-permute-start | bytes 1572872 | tf_op jit(solution)/shard_map/ppermute | solution.py:767
  421.0 17.0 %collective-permute-start.70 = (bf16[256,2048]{1,0:T(8,128)(2,1)}, bf16[256,2048]{1,0:T(8,128)(2,1)}, u32[]{:S(2)}, u32[]{:S(2)}) collective-permute-start(bf16[256,2048]{1,0:T(8,128)(2,1)} %get-tuple-element.282), channel_id=1, source_target_pairs={{0,8},{1,9},{2,10},{3,11},{4,12},{5,13},{6,14},{7,15},{8,0},{9,1},... | collective-permute-start | bytes 3145736 | tf_op jit(solution)/shard_map/ppermute | solution.py:767
  430.0 17.1 %collective-permute-start.69 = (bf16[256,2048]{1,0:T(8,128)(2,1)S(1)}, bf16[256,2048]{1,0:T(8,128)(2,1)S(1)}, u32[]{:S(2)}, u32[]{:S(2)}) collective-permute-start(bf16[256,2048]{1,0:T(8,128)(2,1)S(1)} %get-tuple-element.281), channel_id=1, source_target_pairs={{0,12},{1,13},{2,14},{3,15},{4,0},{5,1},{6,2},{7,3},{8,4},{9,5},{1... | collective-permute-start | bytes 3145736 | tf_op jit(solution)/shard_map/ppermute | solution.py:767
  431.6 16.5 %collective-permute-start.68 = (bf16[256,2048]{1,0:T(8,128)(2,1)S(1)}, bf16[256,2048]{1,0:T(8,128)(2,1)S(1)}, u32[]{:S(2)}, u32[]{:S(2)}) collective-permute-start(bf16[256,2048]{1,0:T(8,128)(2,1)S(1)} %get-tuple-element.280), channel_id=1, source_target_pairs={{0,4},{1,5},{2,6},{3,7},{4,8},{5,9},{6,10},{7,11},{8,12},{9,13},{1... | collective-permute-start | bytes 3145736 | tf_op jit(solution)/shard_map/ppermute | solution.py:767
  466.2 15.3 %collective-permute-start.63 = (bf16[4,64,512]{2,1,0:T(8,128)(2,1)S(1)}, bf16[4,64,512]{2,1,0:T(8,128)(2,1)S(1)}, u32[]{:S(2)}, u32[]{:S(2)}) collective-permute-start(bf16[4,64,512]{2,1,0:T(8,128)(2,1)S(1)} %pad_maximum_fusion.5), channel_id=1, source_target_pairs={{0,1},{1,2},{2,3},{3,0},{4,5},{5,6},{6,7},{7,4},{8,9},{9,10},{10,1... | collective-permute-start | bytes 786440 | tf_op jit(solution)/shard_map/ppermute | solution.py:767
  467.2 25.7 %collective-permute-start.64 = (bf16[4,64,512]{2,1,0:T(8,128)(2,1)S(1)}, bf16[4,64,512]{2,1,0:T(8,128)(2,1)S(1)}, u32[]{:S(2)}, u32[]{:S(2)}) collective-permute-start(bf16[4,64,512]{2,1,0:T(8,128)(2,1)S(1)} %pad_maximum_fusion.5), channel_id=1, source_target_pairs={{0,3},{1,0},{2,1},{3,2},{4,7},{5,4},{6,5},{7,6},{8,11},{9,8},{10,9... | collective-permute-start | bytes 786440 | tf_op jit(solution)/shard_map/ppermute | solution.py:767
  476.7 48.2 %collective-permute-start.65 = (bf16[4,64,512]{2,1,0:T(8,128)(2,1)S(1)}, bf16[4,64,512]{2,1,0:T(8,128)(2,1)S(1)}, u32[]{:S(2)}, u32[]{:S(2)}) collective-permute-start(bf16[4,64,512]{2,1,0:T(8,128)(2,1)S(1)} %pad_maximum_fusion.5), channel_id=1, source_target_pairs={{0,2},{1,3},{2,0},{3,1},{4,6},{5,7},{6,4},{7,5},{8,10},{9,11},{10,... | collective-permute-start | bytes 786440 | tf_op jit(solution)/shard_map/ppermute | solution.py:767
  484.4 57.4 %collective-permute-start.90 = (bf16[64,2048]{1,0:T(8,128)(2,1)}, bf16[64,2048]{1,0:T(8,128)(2,1)}, u32[]{:S(2)}, u32[]{:S(2)}) collective-permute-start(bf16[64,2048]{1,0:T(8,128)(2,1)} %add_convert_fusion.12), channel_id=1, source_target_pairs={{0,16},{1,17},{2,18},{3,19},{4,20},{5,21},{6,22},{7,23},{8,24},{9,... | collective-permute-start | bytes 786440 | tf_op jit(solution)/shard_map/ppermute | solution.py:767
  490.5 41.6 %collective-permute-start.91 = (bf16[128,1024]{1,0:T(8,128)(2,1)S(1)}, bf16[128,1024]{1,0:T(8,128)(2,1)}, u32[]{:S(2)}, u32[]{:S(2)}) collective-permute-start(bf16[128,1024]{1,0:T(8,128)(2,1)S(1)} %add_convert_fusion.11), channel_id=1, source_target_pairs={{32,48},{33,49},{34,50},{35,51},{36,52},{37,53},{38,54},{39,55},{4... | collective-permute-start | bytes 786440 | tf_op jit(solution)/shard_map/ppermute | solution.py:767
  495.8 31.7 %collective-permute-start.89 = (bf16[5,1024]{1,0:T(8,128)(2,1)S(1)}, bf16[5,1024]{1,0:T(8,128)(2,1)S(1)}, u32[]{:S(2)}, u32[]{:S(2)}) collective-permute-start(bf16[5,1024]{1,0:T(8,128)(2,1)S(1)} %pad_maximum_fusion.13), channel_id=1, source_target_pairs={{0,32},{1,33},{2,34},{3,35},{4,36},{5,37},{6,38},{7,39},{8,40},{9,... | collective-permute-start | bytes 30728 | tf_op jit(solution)/shard_map/ppermute | solution.py:767
  527.5 17.5 %collective-permute-start.66 = (bf16[16,64,512]{2,1,0:T(8,128)(2,1)}, bf16[16,64,512]{2,1,0:T(8,128)(2,1)S(1)}, u32[]{:S(2)}, u32[]{:S(2)}) collective-permute-start(bf16[16,64,512]{2,1,0:T(8,128)(2,1)} %get-tuple-element.307), channel_id=1, source_target_pairs={{0,16},{1,17},{2,18},{3,19},{4,20},{5,21},{6,22},{7,23},{8,24},{9,... | collective-permute-start | bytes 3145736 | tf_op jit(solution)/shard_map/ppermute | solution.py:767
  (110 other events, 708.4 us)
Sparse Core Ops, SparseCore 0:
  234.0 76.3 reduce-scatter.3

commit v4 on v3

--- a/solution.py
+++ b/solution.py
@@ -3,6 +3,7 @@
 
 import jax
 import jax.numpy as jnp
+import numpy as np
 from jax import lax
 from jax.experimental import pallas as pl
 from jax.experimental.pallas import tpu as pltpu
@@ -70,6 +71,11 @@
     return expo * (1.0 / jnp.sum(expo, axis=-1, keepdims=True))
 
 
+def same_segment(row):
+    across = jnp.broadcast_to(row.astype(WIDE), (row.shape[1], row.shape[1]))
+    return across.T == across
+
+
 def lanes(at, size):
     return pl.ds(pl.multiple_of(at, 128), size)
 
@@ -92,16 +98,25 @@
     )(far(value))
 
 
-def forward_kernel(with_down, *refs):
+def chosen(choice, candidates, buffer):
+    for at, candidate in enumerate(candidates):
+
+        @pl.when(choice == at)
+        def _():
+            buffer[...] = candidate[...]
+
+
+def forward_kernel(spot, with_down, count, *refs):
+    table_ref, candidates, refs = refs[0], refs[1 : 1 + count], refs[1 + count :]
     if not with_down:
-        refs = refs[:6] + (None,) + refs[6:]
-    forward_body(*refs)
+        refs = refs[:3] + (None,) + refs[3:]
+    forward_body(spot, table_ref, candidates, *refs)
 
 
 def forward_body(
-    role_ref,
-    entry_ref,
-    seg_col_ref,
+    spot,
+    table_ref,
+    candidates,
     seg_row_ref,
     gain_ref,
     lead_ref,
@@ -121,9 +136,10 @@
     result_buf,
     scores_buf,
     probs_buf,
+    entry_ref,
     out_sems,
 ):
-    role, slot = role_ref[0], role_ref[1]
+    role, slot = table_ref[spot], table_ref[spot + 1]
     tokens, width = entry_ref.shape
     keeps = [
         pltpu.make_async_copy(entry_ref, entries_ref.at[slot], out_sems.at[0]),
@@ -134,6 +150,7 @@
 
     @pl.when(role > 0)
     def _():
+        chosen(table_ref[spot + 2], candidates, entry_ref)
         normed, _ = layer_norm(entry_ref[...].astype(WIDE))
         normed_buf[...] = (normed * gain_ref[...]).astype(LOW)
         keeps[0].start()
@@ -160,7 +177,7 @@
 
         @pl.loop(0, HEADS // 4)
         def _(group):
-            same = seg_col_ref[slot] == seg_row_ref[slot]
+            same = same_segment(seg_row_ref[slot])
             for head in range(4):
                 at = group * 4 + head
                 probs_buf[at] = head_probs(scores_buf[at], same).astype(LOW)
@@ -219,13 +236,13 @@
     return pltpu.with_memory_space_constraint(value, pltpu.HBM)
 
 
-def forward_stage(role, entry, seg_col, seg_row, gain, lead, down, kept):
-    tokens, width = entry.shape
+def forward_stage(spot, table, entries, seg_row, gain, lead, down, kept):
+    tokens, width = entries[0].shape
     hidden = lead.shape[1]
-    count = 5 if down is None else 6
-    return pl.pallas_call(
-        functools.partial(forward_kernel, down is not None),
-        out_shape=[jax.ShapeDtypeStruct(entry.shape, LOW)]
+    count = len(entries) + (3 if down is None else 4)
+    return pl.pallas_call(
+        functools.partial(forward_kernel, spot, down is not None, len(entries)),
+        out_shape=[jax.ShapeDtypeStruct((tokens, width), LOW)]
         + [jax.ShapeDtypeStruct(k.shape, k.dtype) for k in kept],
         in_specs=[SMEM_SPEC] + [VMEM_SPEC] * count + [HBM_SPEC] * 4,
         out_specs=[VMEM_SPEC] + [HBM_SPEC] * 4,
@@ -236,6 +253,7 @@
             pltpu.VMEM((tokens, width), WIDE),
             pltpu.VMEM((HEADS, tokens, tokens), WIDE),
             pltpu.VMEM((HEADS, tokens, tokens), LOW),
+            pltpu.VMEM((tokens, width), LOW),
             pltpu.SemaphoreType.DMA((4,)),
         ],
         input_output_aliases={count + 1 + i: 1 + i for i in range(4)},
@@ -244,13 +262,17 @@
             flops=4 * tokens * width * hidden, bytes_accessed=20 << 20, transcendentals=0
         ),
         name="forward_stage",
-    )(role, entry, seg_col, seg_row, gain, pinned(lead), *([pinned(down)] if down is not None else []), *map(far, kept))
-
-
-def backward_kernel(
-    role_ref,
-    grad_ref,
-    seg_col_ref,
+    )(table, *entries, seg_row, gain, pinned(lead), *([pinned(down)] if down is not None else []), *map(far, kept))
+
+
+def backward_kernel(spot, count, *refs):
+    backward_body(spot, refs[0], refs[1 : 1 + count], *refs[1 + count :])
+
+
+def backward_body(
+    spot,
+    table_ref,
+    candidates,
     seg_row_ref,
     gain_ref,
     lead_ref,
@@ -276,10 +298,11 @@
     probs_grad_buf,
     probs_buf,
     scores_grad_buf,
+    grad_ref,
     in_sems,
     out_sems,
 ):
-    role, slot = role_ref[0], role_ref[1]
+    role, slot = table_ref[spot], table_ref[spot + 1]
     tokens, width = grad_ref.shape
     bring_saved = pltpu.make_async_copy(saved_ref.at[slot], saved_buf, in_sems.at[0])
     bring_inner = pltpu.make_async_copy(inner_ref.at[slot], inner_buf, in_sems.at[1])
@@ -299,6 +322,7 @@
     @pl.when(role > 0)
     def _():
         bring_entry.start()
+        chosen(table_ref[spot + 2], candidates, grad_ref)
         keep_next.start()
         normed_buf[...] = jnp.zeros_like(normed_buf)
 
@@ -326,7 +350,7 @@
 
         @pl.loop(0, HEADS // 4)
         def _(group):
-            same = seg_col_ref[slot] == seg_row_ref[slot]
+            same = same_segment(seg_row_ref[slot])
             for head in range(4):
                 at = group * 4 + head
                 probs = head_probs(scores_buf[at], same)
@@ -395,15 +419,16 @@
 
 
 def backward_stage(
-    role, grad, seg_col, seg_row, gain, lead, down, entries, saved, inner, totals
+    spot, table, nexts, seg_row, gain, lead, down, entries, saved, inner, totals
 ):
-    tokens, width = grad.shape
+    tokens, width = nexts[0].shape
+    count = len(nexts)
     hidden = lead.shape[1]
     return pl.pallas_call(
-        backward_kernel,
-        out_shape=[jax.ShapeDtypeStruct(grad.shape, LOW)]
+        functools.partial(backward_kernel, spot, count),
+        out_shape=[jax.ShapeDtypeStruct((tokens, width), LOW)]
         + [jax.ShapeDtypeStruct(k.shape, k.dtype) for k in totals],
-        in_specs=[SMEM_SPEC] + [VMEM_SPEC] * 6 + [HBM_SPEC] * 6,
+        in_specs=[SMEM_SPEC] + [VMEM_SPEC] * (count + 4) + [HBM_SPEC] * 6,
         out_specs=[VMEM_SPEC] + [HBM_SPEC] * 3,
         scratch_shapes=[
             pltpu.VMEM((tokens, hidden), LOW),
@@ -417,19 +442,19 @@
             pltpu.VMEM((HEADS, tokens, tokens), WIDE),
             pltpu.VMEM((HEADS, tokens, tokens), LOW),
             pltpu.VMEM((HEADS, tokens, tokens), LOW),
+            pltpu.VMEM((tokens, width), LOW),
             pltpu.SemaphoreType.DMA((3,)),
             pltpu.SemaphoreType.DMA((3,)),
         ],
-        input_output_aliases={10: 1, 11: 2, 12: 3},
+        input_output_aliases={count + 8 + i: 1 + i for i in range(3)},
         compiler_params=pltpu.CompilerParams(vmem_limit_bytes=18 << 20),
         cost_estimate=pl.CostEstimate(
             flops=4 * tokens * width * hidden, bytes_accessed=20 << 20, transcendentals=0
         ),
         name="backward_stage",
     )(
-        role,
-        grad,
-        seg_col,
+        table,
+        *nexts,
         seg_row,
         gain,
         pinned(lead),
@@ -441,48 +466,56 @@
     )
 
 
-def stats_kernel(readout_ref, table_ref, peak_ref, total_ref):
+def stats_kernel(spot, plan_ref, *refs):
+    candidates, (table_ref, readout_ref, peak_ref, total_ref) = refs[:-4], refs[-4:]
+    step = pl.program_id(0)
+
+    @pl.when(step == 0)
+    def _():
+        chosen(plan_ref[spot], candidates, readout_ref)
+
     logits = matmul_nt(table_ref[...], readout_ref[...])
     own_peak = jnp.max(logits, axis=0, keepdims=True)
     own_total = lambda peak: jnp.sum(jnp.exp(logits - peak), axis=0, keepdims=True)
 
-    @pl.when(pl.program_id(0) == 0)
+    @pl.when(step == 0)
     def _():
         peak_ref[...] = own_peak
         total_ref[...] = own_total(own_peak)
 
-    @pl.when(pl.program_id(0) > 0)
+    @pl.when(step > 0)
     def _():
         peak = jnp.maximum(peak_ref[...], own_peak)
         total_ref[...] = total_ref[...] * jnp.exp(peak_ref[...] - peak) + own_total(peak)
         peak_ref[...] = peak
 
 
-def head_stats(readout, table, tile):
-    tokens, emb = readout.shape
+def head_stats(spot, plan, readouts, table, tile):
+    tokens, emb = readouts[0].shape
     vocab = table.shape[0]
     whole = pl.BlockSpec((1, tokens), lambda i: (0, 0))
-    return pl.pallas_call(
-        stats_kernel,
-        out_shape=[jax.ShapeDtypeStruct((1, tokens), WIDE)] * 2,
+    rows = pl.BlockSpec((tokens, emb), lambda i: (0, 0))
+    return pl.pallas_call(
+        functools.partial(stats_kernel, spot),
+        out_shape=[jax.ShapeDtypeStruct((tokens, emb), LOW)]
+        + [jax.ShapeDtypeStruct((1, tokens), WIDE)] * 2,
         grid=(vocab // tile,),
-        in_specs=[
-            pl.BlockSpec((tokens, emb), lambda i: (0, 0)),
-            pl.BlockSpec((tile, emb), lambda i: (i, 0)),
-        ],
-        out_specs=[whole, whole],
+        in_specs=[SMEM_SPEC]
+        + [rows] * len(readouts)
+        + [pl.BlockSpec((tile, emb), lambda i: (i, 0))],
+        out_specs=[rows, whole, whole],
         compiler_params=pltpu.CompilerParams(vmem_limit_bytes=32 << 20),
         cost_estimate=pl.CostEstimate(
             flops=2 * tokens * vocab * emb, bytes_accessed=5 << 20, transcendentals=tokens * vocab
         ),
         name="head_stats",
-    )(readout, far(table))
-
-
-def head_kernel(base_ref, readout_ref, table_ref, logsum_ref, ids_ref, head_ref, grad_ref):
+    )(plan, *readouts, far(table))
+
+
+def head_kernel(spot, table_base_ref, readout_ref, table_ref, logsum_ref, ids_ref, head_ref, grad_ref):
     tile = table_ref.shape[0]
     logits = matmul_nt(table_ref[...], readout_ref[...])
-    ids = ids_ref[...] - (base_ref[0] + pl.program_id(0) * tile)
+    ids = ids_ref[...] - (table_base_ref[spot] + pl.program_id(0) * tile)
     hits = lax.broadcasted_iota(jnp.int32, logits.shape, 0) == ids
     probs = jnp.exp(logits - logsum_ref[...])
     grads = jnp.where(hits, probs - 1.0, probs).astype(LOW)
@@ -501,16 +534,16 @@
         grad_ref[...] += term
 
 
-def head_grads(base, readout, table, logsum, ids):
+def head_grads(spot, base, readout, table, logsum, ids):
     tokens, emb = readout.shape
     vocab = table.shape[0]
     row = pl.BlockSpec((1, tokens), lambda i: (0, 0))
     whole = pl.BlockSpec((tokens, emb), lambda i: (0, 0))
     part = pl.BlockSpec((vocab // 4, emb), lambda i: (i, 0))
     return pl.pallas_call(
-        head_kernel,
+        functools.partial(head_kernel, spot),
         out_shape=[
-            jax.ShapeDtypeStruct((16, 512, emb), LOW),
+            pltpu.HBM((16, 512, emb), LOW),
             jax.ShapeDtypeStruct((tokens, emb), WIDE),
         ],
         grid=(4,),
@@ -646,7 +679,7 @@
     )(where, far(normed), far(saved), far(grads))
 
 
-def down_grad_kernel(where_ref, saved_ref, nexts_ref, out_ref):
+def down_grad_kernel(where_ref, saved_ref, nexts_ref, out_ref, buf_ref, sem):
     role, half, spot = where_ref[0], where_ref[1], where_ref[2]
     at = pl.program_id(0)
     unit = saved_ref.shape[1] // 4
@@ -657,14 +690,20 @@
 
         @pl.when(half == 0)
         def _():
-            out_ref[(at - spot + 4) % 4] = result
+            buf_ref[(at - spot + 4) % 4] = result
 
         @pl.when(half == 1)
         def _():
             for y in range(4):
-                out_ref[
+                buf_ref[
                     (y - spot + 4) % 4, pl.ds(pl.multiple_of(at * unit, unit), unit), :
                 ] = result[y * unit : (y + 1) * unit]
+
+        @pl.when(at == pl.num_programs(0) - 1)
+        def _():
+            copy = pltpu.make_async_copy(buf_ref, out_ref, sem)
+            copy.start()
+            copy.wait()
 
 
 def down_grad(where, saved, nexts):
@@ -674,7 +713,7 @@
     live = lambda where: jnp.where(where[0] == 2, 1, 0)
     return pl.pallas_call(
         down_grad_kernel,
-        out_shape=jax.ShapeDtypeStruct((4, rows, width), LOW),
+        out_shape=pltpu.HBM((4, rows, width), LOW),
         grid_spec=pltpu.PrefetchScalarGridSpec(
             num_scalar_prefetch=1,
             grid=(4,),
@@ -682,7 +721,8 @@
                 pl.BlockSpec((tokens, rows), lambda i, where: (0, (where[1] * 4 + i) * live(where))),
                 pl.BlockSpec((tokens, width), lambda i, where: (0, 0)),
             ],
-            out_specs=pl.BlockSpec((4, rows, width), lambda i, where: (0, 0, 0)),
+            out_specs=HBM_SPEC,
+            scratch_shapes=[pltpu.VMEM((4, rows, width), LOW), pltpu.SemaphoreType.DMA],
         ),
         compiler_params=pltpu.CompilerParams(vmem_limit_bytes=24 << 20),
         cost_estimate=pl.CostEstimate(
@@ -692,33 +732,128 @@
     )(where, far(saved), far(nexts))
 
 
-def embed_kernel(base_ref, ids_ref, grad_ref, out_ref, total_ref):
+def upper_kernel(where_ref, *refs):
+    out_ref, sems = refs[4], refs[5]
+    rows = refs[0].shape[0]
+    copies = []
+    for at, part in enumerate(refs[:4]):
+        place = (where_ref[0] - at + 4) % 4
+        copies.append(
+            pltpu.make_async_copy(
+                part, out_ref.at[pl.ds(pl.multiple_of(place * rows, rows), rows), :], sems.at[at]
+            )
+        )
+        copies[-1].start()
+    for copy in copies:
+        copy.wait()
+
+
+def upper_half(where, parts):
+    rows, width = parts[0].shape
+    return pl.pallas_call(
+        upper_kernel,
+        out_shape=pltpu.HBM((4 * rows, width), LOW),
+        in_specs=[SMEM_SPEC] + [HBM_SPEC] * 4,
+        out_specs=HBM_SPEC,
+        scratch_shapes=[pltpu.SemaphoreType.DMA((4,))],
+        compiler_params=pltpu.CompilerParams(vmem_limit_bytes=4 << 20),
+        name="upper_half",
+    )(where, *map(far, parts))
+
+
+def hold_down_kernel(where_ref, mine_ref, other_ref, own_ref, out_ref, sems):
+    rows = mine_ref.shape[0]
+    core = where_ref[1]
+    spot = lambda at: out_ref.at[pl.ds(pl.multiple_of(at * rows, rows), rows), :]
+    copies = [
+        pltpu.make_async_copy(mine_ref, spot(core), sems.at[0]),
+        pltpu.make_async_copy(other_ref, spot(1 - core), sems.at[1]),
+        pltpu.make_async_copy(own_ref, out_ref.at[pl.ds(2 * rows, 2 * rows), :], sems.at[2]),
+    ]
+    for copy in copies:
+        copy.start()
+    for copy in copies:
+        copy.wait()
+
+
+def hold_down(where, mine, other, own):
+    rows, width = mine.shape
+    return pl.pallas_call(
+        hold_down_kernel,
+        out_shape=pltpu.VMEM((4 * rows, width), LOW),
+        in_specs=[SMEM_SPEC] + [HBM_SPEC] * 3,
+        out_specs=VMEM_SPEC,
+        scratch_shapes=[pltpu.SemaphoreType.DMA((3,))],
+        compiler_params=pltpu.CompilerParams(vmem_limit_bytes=4 << 20),
+        name="hold_down",
+    )(where, far(mine), far(other), far(own))
+
+
+def noise_kernel(spot, plan_ref, ids_ref, *refs):
+    candidates, (packed_ref, noise_ref, buf_ref) = refs[:-3], refs[-3:]
+    parts = noise_ref.shape[0]
+    chosen(plan_ref[spot], candidates, buf_ref)
+    packed_ref[:parts] = buf_ref[...]
+    noise_ref[...] = buf_ref[...].astype(WIDE)
+    ids = ids_ref[...]
+    high = jnp.right_shift(ids, 8).astype(WIDE)
+    low = jnp.bitwise_and(ids, 255).astype(WIDE)
+    at = lax.broadcasted_iota(jnp.int32, (16, ids.shape[1]), 0)
+    split = jnp.where(at == 0, high, jnp.where(at == 1, low, 0.0))
+    packed_ref[parts:] = split.astype(LOW)
+
+
+def noise_pack(spot, plan, ids, candidates):
+    parts, tokens = candidates[0].shape
+    return pl.pallas_call(
+        functools.partial(noise_kernel, spot),
+        out_shape=[
+            jax.ShapeDtypeStruct((parts + 16, tokens), LOW),
+            jax.ShapeDtypeStruct((parts, tokens), WIDE),
+        ],
+        in_specs=[SMEM_SPEC] + [VMEM_SPEC] * (1 + len(candidates)),
+        out_specs=[VMEM_SPEC] * 2,
+        scratch_shapes=[pltpu.VMEM((parts, tokens), LOW)],
+        compiler_params=pltpu.CompilerParams(vmem_limit_bytes=8 << 20),
+        name="noise_pack",
+    )(plan, ids, *candidates)
+
+
+def embed_kernel(base_ref, mine_ref, other_ref, out_ref, total_ref):
     step = pl.program_id(0)
-    count, parts, tokens = grad_ref.shape
+    steps = pl.num_programs(0)
+    parts = out_ref.shape[0]
     blocks = total_ref.shape[0] // parts
-    term = None
-    for at in range(count):
-        ids = ids_ref[at] - base_ref[0]
-        lane = jnp.bitwise_and(ids, 127)
-        hits = lax.broadcasted_iota(jnp.int32, (128, tokens), 0) == lane
-        hits = jnp.where(hits, 1.0, 0.0).astype(LOW)
-        own = jnp.right_shift(ids, 7)
-        grads = grad_ref[at]
-        masked = jnp.concatenate(
-            [grads * jnp.where(own == block, 1.0, 0.0).astype(LOW) for block in range(blocks)]
-        )
-        part = matmul_nt(masked, hits)
-        term = part if term is None else term + part
-
-    @pl.when(step == 0)
-    def _():
-        total_ref[...] = term
-
-    @pl.when(step > 0)
-    def _():
-        total_ref[...] += term
-
-    @pl.when(step == pl.num_programs(0) - 1)
+
+    def add(gathered_ref):
+        count, _, tokens = gathered_ref.shape
+        term = None
+        for at in range(count):
+            split = gathered_ref[at, parts : parts + 16].astype(WIDE)
+            ids = (split[0:1] * 256.0 + split[1:2]).astype(jnp.int32) - base_ref[0]
+            lane = jnp.bitwise_and(ids, 127)
+            hits = lax.broadcasted_iota(jnp.int32, (128, tokens), 0) == lane
+            hits = jnp.where(hits, 1.0, 0.0).astype(LOW)
+            own = jnp.right_shift(ids, 7)
+            grads = gathered_ref[at, :parts]
+            masked = jnp.concatenate(
+                [grads * jnp.where(own == block, 1.0, 0.0).astype(LOW) for block in range(blocks)]
+            )
+            part = matmul_nt(masked, hits)
+            term = part if term is None else term + part
+
+        @pl.when(step == 0)
+        def _():
+            total_ref[...] = term
+
+        @pl.when(step > 0)
+        def _():
+            total_ref[...] += term
+
+    pl.when(step < steps // 2)(lambda: add(mine_ref))
+    pl.when(step >= steps // 2)(lambda: add(other_ref))
+
+    @pl.when(step == steps - 1)
     def _():
         rows = out_ref.shape[1]
         for block in range(blocks):
@@ -728,27 +863,38 @@
             ]
 
 
-def embed_sum(base, ids, grads, rows):
-    count, parts, tokens = grads.shape
+def embed_sum(base, mine, other, parts, rows):
+    count, deep, tokens = mine.shape
     step = 4
+    half = count // step
     blocks = -(-rows // 128)
     return pl.pallas_call(
         embed_kernel,
         out_shape=jax.ShapeDtypeStruct((parts, rows), WIDE),
-        grid=(count // step,),
+        grid=(2 * half,),
         in_specs=[
             SMEM_SPEC,
-            pl.BlockSpec((step, 1, tokens), lambda i: (i, 0, 0)),
-            pl.BlockSpec((step, parts, tokens), lambda i: (i, 0, 0)),
+            pl.BlockSpec((step, deep, tokens), lambda i: (jnp.minimum(i, half - 1), 0, 0)),
+            pl.BlockSpec((step, deep, tokens), lambda i: (jnp.maximum(i - half, 0), 0, 0)),
         ],
         out_specs=pl.BlockSpec((parts, rows), lambda i: (0, 0)),
         scratch_shapes=[pltpu.VMEM((blocks * parts, 128), WIDE)],
         compiler_params=pltpu.CompilerParams(vmem_limit_bytes=32 << 20),
         cost_estimate=pl.CostEstimate(
-            flops=2 * count * tokens * parts * rows, bytes_accessed=3 << 20, transcendentals=0
+            flops=4 * count * tokens * parts * rows, bytes_accessed=3 << 20, transcendentals=0
         ),
         name="embed_sum",
-    )(base, ids.reshape(count, 1, tokens), grads)
+    )(base, mine, other)
+
+
+def empty(*kinds):
+    return pl.pallas_call(
+        lambda *refs: None,
+        out_shape=[pltpu.HBM(shape, dtype) for shape, dtype in kinds],
+        out_specs=[HBM_SPEC] * len(kinds),
+        compiler_params=pltpu.CompilerParams(vmem_limit_bytes=1 << 20),
+        name="empty",
+    )()
 
 
 ROW_LEN = 128
@@ -805,36 +951,54 @@
     return (pieces, [plane_route(pieces[by], by, True, sections) for by in TURNS])
 
 
-def plane_second(first, second, sections=range(SEC)):
-    pieces, arrived = first
+def plane_sum(pieces):
     total = pieces[0].astype(WIDE)
-    for piece in arrived:
+    for piece in pieces[1:]:
         total = total + piece.astype(WIDE)
-    total = total.astype(LOW)
-    result = row_block(total, second, 4).astype(WIDE)
-    for by in TURNS:
-        block = row_block(total, (second + by) % 4, 4)
-        result = result + plane_route(block, by, False, sections).astype(WIDE)
-    return result.astype(LOW)
-
-
-def gather_own(values):
-    blocks = jnp.stack([values] + [plane_route(values, by, True) for by in TURNS])
-    return jnp.concatenate([blocks] + [plane_route(blocks, by, False) for by in TURNS])
-
-
-def gather_plane(values):
-    blocks = gather_own(values)
-    return jnp.concatenate([blocks, swap_cores(blocks)])
-
-
-def empty(*kinds):
-    return pl.pallas_call(
-        lambda *refs: None,
-        out_shape=[jax.ShapeDtypeStruct(shape, dtype) for shape, dtype in kinds],
-        out_specs=[HBM_SPEC] * len(kinds),
-        name="empty",
-    )()
+    return total.astype(LOW)
+
+
+def plane_second(pieces, arrived, second, sections=range(SEC)):
+    total = plane_sum([pieces[0]] + arrived)
+    return [row_block(total, second, 4)] + [
+        plane_route(row_block(total, (second + by) % 4, 4), by, False, sections) for by in TURNS
+    ]
+
+
+def group_exchange(values, first):
+    number = lambda s, g, x, y: (s * GRP + g) * NX * NY + x * NY + y
+    groups = []
+    for s in range(SEC):
+        for g in range(GRP):
+            along_x = (g == 0) == first
+            for at in range(4):
+                groups.append(
+                    [number(s, g, i, at) if along_x else number(s, g, at, i) for i in range(4)]
+                )
+    return lax.all_to_all(values, ALL, 0, 0, axis_index_groups=groups, tiled=True)
+
+
+def section_exchange(values):
+    return lax.all_to_all(values, "section", 0, 0, tiled=True)
+
+
+def plans(micro, vocab_part):
+    last = SEC - 1
+    steps = micro + 2 * last
+    table = np.zeros((SEC, 6 * steps + 2), np.int32)
+    for s in range(SEC):
+        for way in range(2):
+            depth = s if way == 0 else last - s
+            for step in range(steps):
+                at = step - 2 * depth
+                if 0 <= at < micro:
+                    sources = ([0] if step < micro else []) + [
+                        d + 1 for d in range(last) if 0 <= step - 2 - 2 * d < micro
+                    ]
+                    spot = 3 * (way * steps + step)
+                    table[s, spot : spot + 3] = (1 + s % 2, at, sources.index(depth))
+        table[s, 6 * steps :] = (s * vocab_part, s)
+    return table
 
 
 def local(
@@ -854,7 +1018,7 @@
     core = lax.axis_index("group")
     row = lax.axis_index("row")
     x_at, y_at = row // NY, row % NY
-    first_at, second_at = jnp.where(core == 0, x_at, y_at), jnp.where(core == 0, y_at, x_at)
+    first_at = jnp.where(core == 0, x_at, y_at)
     micro, _, tokens = token_ids.shape
     width = input_proj.shape[1]
     hidden = lead_weight.shape[2]
@@ -864,14 +1028,16 @@
     vocab = embed_table.shape[0]
     all_tokens = micro * tokens
     last = SEC - 1
-    is_mlp = section % 2 == 1
     gain_half = norm_gain.astype(WIDE)
     lead = lead_weight[0]
     own_down = down_weight[0]
     seg_row = segment_ids
-    seg_col = segment_ids.reshape(micro, tokens, 1)
     flat_ids = token_ids.reshape(-1)
 
+    plan = plans(micro, vocab_part)
+    steps = micro + 2 * last
+    table = lax.dynamic_index_in_dim(jnp.asarray(plan), section, 0, False)
+    where_start = jnp.stack((first_at, core)).astype(jnp.int32)
     to_first = lambda v: [v] + [link(v, s, 0) for s in range(1, SEC)]
     eighth = row_block(row_block(own_down, core, 2), first_at, 4)
     eighth = jnp.where(section == 1, link(eighth, 0, 1), link(eighth, 2, 3))
@@ -880,34 +1046,14 @@
     inputs = to_first(input_proj)
     input_full = jnp.concatenate(inputs)
     embedded = jnp.concatenate(
-        [own_embedded] + [link(after(own_embedded, inputs[s]), s, 0) for s in range(1, SEC)]
+        [own_embedded] + [link(own_embedded, s, 0) for s in range(1, SEC)]
     )
     first_in = matmul_tn(embedded, input_full).astype(LOW).reshape(micro, tokens, width)
     held_lead = hold(lead)
-    readout_own = after(readout_proj.T, first_in)
-    readout_full = jnp.concatenate(
-        [link(readout_own, s, last) for s in range(last)] + [readout_own]
-    )
-
     eighth = after(eighth, own_embedded)
-    upper = jnp.zeros((4,) + eighth.shape, LOW)
-    upper = lax.dynamic_update_index_in_dim(upper, eighth, first_at, 0)
-    for by in TURNS:
-        upper = lax.dynamic_update_index_in_dim(
-            upper, plane_route(eighth, by, True), (first_at - by) % 4, 0
-        )
-    upper = upper.reshape(half_rows // 2, width)
-    upper_other = swap_cores(upper)
-    held_down = hold(
-        jnp.concatenate(
-            (
-                jnp.where(core == 0, upper, upper_other),
-                jnp.where(core == 0, upper_other, upper),
-                own_down,
-            )
-        )
-    )
-    all_ids = gather_plane(after(flat_ids, upper_other))
+    eighths = [eighth] + [plane_route(eighth, by, True) for by in (1, 2, 3)]
+    upper = upper_half(where_start, [after(part, first_in) for part in eighths])
+    held_down = hold_down(where_start, upper, swap_cores(upper), own_down)
 
     kept = empty(
         ((micro, tokens, width), LOW),
@@ -916,37 +1062,16 @@
         ((micro, tokens, hidden), WIDE),
     )
 
-    def role_at(at):
-        live = jnp.logical_and(at >= 0, at < micro)
-        role = jnp.where(live, jnp.where(is_mlp, 2, 1), 0)
-        return jnp.stack((role, jnp.clip(at, 0, micro - 1))).astype(jnp.int32)
-
-    steps = micro + 2 * last
+    def sources(first, step, hops, order):
+        arrived = [hops[step - 2, s] for s in order if (step - 2, s) in hops]
+        return ([first[step]] if step < micro else []) + arrived
+
     outs, hops = [], {}
-
-    def arrived(step, by):
-        parts = [
-            (s + by, hops[step - 2, s])
-            for s in range(SEC)
-            if (step - 2, s) in hops
-        ]
-        value = parts[0][1] if parts else None
-        for target, part in parts[1:]:
-            value = jnp.where(section == target, part, value)
-        return value
-
     for step in range(steps):
-        entry = arrived(step, 1)
-        if entry is None:
-            entry = first_in[step]
-        elif step < micro:
-            entry = jnp.where(section == 0, first_in[step], entry)
-        if step == 5:
-            entry = after(entry, all_ids)
         out, *kept = forward_stage(
-            role_at(step - 2 * section),
-            entry,
-            seg_col,
+            3 * step,
+            table,
+            sources(first_in, step, hops, range(SEC)),
             seg_row,
             gain_half,
             held_lead,
@@ -958,6 +1083,11 @@
             if 0 <= step - 2 * s < micro:
                 ready = after(out, hops[step - 1, s]) if (step - 1, s) in hops else out
                 hops[step, s] = link(ready, s, s + 1)
+        if step == 2:
+            readout_own = after(readout_proj.T, out)
+            readout_full = jnp.concatenate(
+                [link(readout_own, s, last) for s in range(last)] + [readout_own]
+            )
     entries, normeds, saved, inner = kept
 
     final_rows = jnp.concatenate(outs[2 * last :]).astype(WIDE)
@@ -966,16 +1096,14 @@
     final_low = (normed_f * gain_f).astype(LOW)
     readout = matmul_nt(final_low, readout_full).astype(LOW)
     sent = [link(readout, last, s) for s in range(last)]
-    for s in range(last):
-        readout = jnp.where(section == s, sent[s], readout)
-    peak, total = head_stats(readout, head_table, 2000)
+    readout, peak, total = head_stats(6 * steps + 1, table, sent + [readout], head_table, 2000)
     stats = jnp.concatenate((peak, total))
-    all_stats = jnp.stack([stats] + [turn(stats, by) for by in TURNS])
+    all_stats = section_exchange(jnp.tile(stats, (SEC, 1))).reshape(SEC, 2, all_tokens)
     peak = jnp.max(all_stats[:, 0], axis=0)
     total = jnp.sum(all_stats[:, 1] * jnp.exp(all_stats[:, 0] - peak), axis=0)
     logsum = (peak + jnp.log(total))[None]
     head_grad, grad_readout = head_grads(
-        (section * vocab_part).reshape(1), readout, head_table, logsum, flat_ids[None]
+        6 * steps, table, readout, head_table, logsum, flat_ids[None]
     )
     grad_low = grad_readout.astype(LOW)
     for s in range(last):
@@ -995,17 +1123,10 @@
     )
     outs, hops = [], {}
     for step in range(steps):
-        grad_next = arrived(step, -1)
-        if grad_next is None:
-            grad_next = last_grads[step]
-        elif step < micro:
-            grad_next = jnp.where(section == last, last_grads[step], grad_next)
-        if step == steps - 1:
-            grad_next = after(grad_next, head_grad)
         out, *totals = backward_stage(
-            role_at(step - 2 * (last - section)),
-            grad_next,
-            seg_col,
+            3 * (steps + step),
+            table,
+            sources(last_grads, step, hops, range(SEC - 1, -1, -1)),
             seg_row,
             gain_half,
             held_lead,
@@ -1020,6 +1141,10 @@
             if 0 <= step - 2 * (last - s) < micro:
                 ready = after(out, hops[step - 1, s]) if (step - 1, s) in hops else out
                 hops[step, s] = link(ready, s, s - 1)
+    section, core, row = lax.optimization_barrier((section, core, row, out))[:3]
+    x_at, y_at = row // NY, row % NY
+    first_at, second_at = jnp.where(core == 0, x_at, y_at), jnp.where(core == 0, y_at, x_at)
+    is_mlp = section % 2 == 1
 
     first_grads = jnp.concatenate(outs[2 * last :])
     noise_grad = matmul_nt(input_full, first_grads).astype(LOW)
@@ -1029,6 +1154,7 @@
     grad_nexts, grads, gain_grads = totals
     gain_grad = jnp.sum(gain_grads[:, 0], axis=0)
     flat = lambda v: v.reshape(all_tokens, v.shape[-1])
+    grads = after(grads, head_grad)
     normed, grad_nexts, grads, saved = flat(normeds), flat(grad_nexts), flat(grads), flat(saved)
     odd = (1, 3)
     role = jnp.where(is_mlp, 2, 1)
@@ -1039,29 +1165,13 @@
         jnp.concatenate((mine, other), axis=1),
         jnp.concatenate((other, mine), axis=1),
     )
-    lead_got = swap_cores(lead_grad(where_other, normed, saved, grads))
-    lead_mine = lead_grad(where_mine, normed, saved, grads)
     down_got = swap_cores(down_grad(where_other, saved, grad_nexts), odd)
     down_mine = down_grad(where_mine, saved, grad_nexts)
+    lead_got = swap_cores(lead_grad(after(where_other, down_mine), normed, saved, grads))
+    packed, noise_wide = noise_pack(6 * steps + 1, table, flat_ids[None], [pieces[0]] + sent)
+    down_first = plane_first(down_mine, down_got, odd)
+    lead_mine = lead_grad(after(where_mine, (packed, down_first[0])), normed, saved, grads)
     lead_first = plane_first(lead_mine, lead_got)
-    down_first = plane_first(down_mine, down_got, odd)
-    noise_grad = pieces[0]
-    for s in range(1, SEC):
-        noise_grad = jnp.where(section == s, sent[s - 1], noise_grad)
-    blocks = gather_own(after(noise_grad, (lead_first[0], down_first[0])))
-    lead_part = plane_second(lead_first, second_at)
-    down_part = plane_second(down_first, second_at, odd)
-    lead_out = both(lead_part, swap_cores(lead_part)).astype(WIDE)
-    blocks = jnp.concatenate([blocks, swap_cores(blocks)])
-    embed_grad = embed_sum((row * (vocab // 16)).reshape(1), all_ids, blocks, vocab // 16).T
-    noise_out = noise_grad.reshape(emb_part, micro, tokens).transpose(1, 2, 0).astype(WIDE)
-
-    down_other = swap_cores(down_part, odd)
-    upper_part = jnp.where(core == 0, down_part, down_other)
-    lower_part = jnp.where(core == 0, down_other, down_part)
-    upper_half = lax.dynamic_slice_in_dim(upper_part, core * (width // 2), width // 2, 1)
-    upper_half = jnp.where(section == 0, link(upper_half, 1, 0), link(upper_half, 3, 2))
-    down_out = jnp.where(is_mlp, lower_part, both(upper_half, swap_cores(upper_half))).astype(WIDE)
 
     input_grad = matmul(embedded, first_grads).reshape(SEC, 16, 4, width)
     input_grad = input_grad.transpose(1, 0, 2, 3).reshape(16, 16, width)
@@ -1082,43 +1192,70 @@
         ),
         axis=1,
     ).astype(LOW)
+    small = after(small, lead_first[0])
     half_of = lambda which: lax.dynamic_slice_in_dim(small, which * (width // 2), width // 2, 2)
     small = half_of(core).astype(WIDE) + swap_cores(half_of(1 - core)).astype(WIDE)
     small = small.astype(LOW).reshape(NX, NY, 32, width // 2)
-    small = jnp.where(core == 0, small, small.swapaxes(0, 1))
-    small = jnp.stack(
-        [lax.dynamic_index_in_dim(small, (first_at + by) % 4, 0, False) for by in range(4)]
-    )
-    small = after(small, (lead_part, down_part)).reshape(4, NY * 32, width // 2)
-    small_part = plane_second(plane_first(small, None), second_at)
-    small = both(small_part, swap_cores(small_part))
+    small = jnp.where(core == 0, small, small.swapaxes(0, 1)).reshape(4, NY * 32, width // 2)
+    deep = emb_part + 16
+
+    def exchange(blocks, packed, first):
+        rows = blocks.shape[1]
+        everywhere = jnp.broadcast_to(packed, (4,) + packed.shape)
+        got = group_exchange(jnp.concatenate((blocks, everywhere), axis=1), first)
+        return jnp.sum(got[:, :rows].astype(WIDE), axis=0).astype(LOW), got[:, rows:]
+
+    small, packed = exchange(small, packed, True)
+    small, packed = exchange(
+        small.reshape(4, 32, width // 2), packed.reshape(4 * deep, all_tokens), False
+    )
+    packed = packed.reshape(16, deep, all_tokens)
+    packed_other = swap_cores(packed)
+    small = both(small, swap_cores(small))
+    down_second = plane_second(after(down_first[0], packed), down_first[1], second_at, odd)
+    lead_second = plane_second(after(lead_first[0], packed), lead_first[1], second_at)
+    embed_grad = embed_sum(
+        (row * (vocab // 16)).reshape(1), packed, packed_other, emb_part, vocab // 16
+    )
+    down_part = plane_sum(after(down_second, embed_grad))
+    lead_part = plane_sum(after(lead_second, embed_grad))
+    noise_out = noise_wide.reshape(emb_part, micro, tokens).transpose(1, 2, 0)
+    lead_out = both(lead_part, swap_cores(lead_part)).astype(WIDE)
+
+    def first_target(s, g, x, y):
+        if s % 2 == 0:
+            return None
+        return (s - 1, 0, x, y) if g == 0 else (s, 0, x, y)
+
+    def second_target(s, g, x, y):
+        return (s - 1, 1, x, y) if s % 2 == 1 and g == 0 else None
+
+    to_core_0 = route(down_part, first_target)
+    to_core_1 = route(down_part, second_target)
+    down_out = jnp.where(
+        core == 0, to_core_0, jnp.where(is_mlp, down_part, to_core_1)
+    ).astype(WIDE)
+
     gain_out = small[16, :64].astype(WIDE)
     input_rows = small[:16].reshape(SEC, 4, width)
     readout_rows = small[:16].reshape(64, SEC, 64)
     final_rows = small[16, 64:128].reshape(SEC, 16)
 
-    def sent_part(by):
-        target = (section + by) % SEC
-        readouts = lax.dynamic_index_in_dim(readout_rows, target, 1, False).reshape(4, width)
-        finals = lax.dynamic_index_in_dim(final_rows, target, 0, False)
-        finals = jnp.pad(finals, (0, width - 16))[None]
-        inputs = lax.dynamic_index_in_dim(input_rows, target, 0, False)
-        return jnp.concatenate((jnp.where(section == 0, inputs, readouts), finals))
-
-    input_out = input_rows[0]
-    readout_out = readout_rows[:, last]
-    final_out = final_rows[last]
-    for by in TURNS:
-        part = turn(sent_part(by), by)
-        input_out = jnp.where(section == by, part[:4], input_out)
-        here = section == (last + by) % SEC
-        readout_out = jnp.where(here, part[:4].reshape(64, 64), readout_out)
-        final_out = jnp.where(here, part[4, :16], final_out)
+    finals = jnp.pad(final_rows, ((0, 0), (0, width - 16)))[:, None]
+    mine = jnp.where(
+        section == 0, input_rows, readout_rows.transpose(1, 0, 2).reshape(SEC, 4, width)
+    )
+    shared = section_exchange(
+        jnp.concatenate((mine, finals, jnp.zeros((SEC, 3, width), LOW)), axis=1)
+    )
+    input_out = shared[0, :4]
+    readout_out = shared[last, :4].reshape(64, 64)
+    final_out = shared[last, 4, :16]
 
     head_out = pair_sum(head_grad, swap_cores(head_grad), vocab_part // (NX * NY))
     return (
         noise_out[:, None],
-        embed_grad,
+        embed_grad.T,
         input_out.astype(WIDE),
         gain_out[None],
         lead_out[None],

time: 575 us -> 569 us (0.990)
  the two profiles are of different devices: /device:TPU:1 before, /device:TPU:19 now
where the time goes in v4:
time: 569 us; the launch traced here: 560 us
  Pallas kernels  206 us (36%)
  starting transfers between devices  133 us (23%)
  waiting for transfers between devices  130 us (23%)
  other arithmetic  31.4 us (6%)
  local copies, waits for them, and re-layouts  25.3 us (4%)
  between operations  16.3 us (3%)
  blocking collectives  13.2 us (2%)
    ppermute x69, waiting for transfers between devices, route(): return lax.ppermute(value, ALL, pairs)  124 us
    ppermute x69, starting transfers between devices, route(): return lax.ppermute(value, ALL, pairs)  104 us
    pallas_call x1, Pallas kernels, upper_half(): pl.pallas_call(upper_kernel, out_shape=pltpu.HBM((4 * rows, width), LOW),...  65.2 us
    pallas_call x10, Pallas kernels, backward_stage(): pl.pallas_call(functools.partial(backward_kernel, spot, count), out_shape...  44.7 us
    pallas_call x10, Pallas kernels, forward_stage(): pl.pallas_call(functools.partial(forward_kernel, spot, down is not None,...  29.8 us
    all_to_all x1, starting transfers between devices, section_exchange(): return lax.all_to_all(values, 'section', 0, 0, tiled=True)  19.2 us
    unnamed x75, local copies, waits for them, and re-layouts  17 us
    pallas_call x2, Pallas kernels, lead_grad(): pl.pallas_call(lead_grad_kernel, out_shape=jax.ShapeDtypeStruct((4, width...  15.1 us
  transfers between devices with their start and end apart: 73, of which 16 were waited for; matrix products, arithmetic and copies ran while one was open for 6% of the time, Pallas kernels for 22%

profile of v4, /device:TPU:19, one launch (start us, length us, event | category | flops | bytes accessed | tf_op | source)
XLA Modules:
  0.0 559.6 jit_solution(5433079368647212755)
XLA Ops:
  18.4 8.7 %lookup.1 = bf16[64,512]{1,0:T(8,128)(2,1)S(1)} custom-call(s32[1,512]{1,0:T(1,128)S(1)} %bitcast.123, bf16[64,32000]{1,0:T(8,128)(2,1)} %bitcast.153, bf16[64,512]{1,0:T(8,128)(2,1)S(1)} %copy_bitcast_fusion.noise_ref), custom_call_target="tpu_custom_call" | custom-call | flops 4194304000 | bytes 4194304 | tf_op jit(solution)/shard_map/lookup/pallas_call | solution.py:608
  45.2 65.2 %upper_half.1.mine_ref = bf16[1024,1024]{1,0:T(8,128)(2,1)} custom-call(s32[2]{0:T(128)S(1)} %pad_add_fusion.where_ref, bf16[256,1024]{1,0:T(8,128)(2,1)} %copy-done.15, bf16[256,1024]{1,0:T(8,128)(2,1)} %copy-done.19, bf16[256,1024]{1,0:T(8,128)(2,1)} %copy-done.20, bf16[256,1024]{1,0:T(8,128)(2,1)} %copy-done.21), custom_call_target="tpu_custom_call" | custom-call | tf_op jit(solution)/shard_map/upper_half/pallas_call | solution.py:753
  110.5 5.0 collective-permute-start.12
  126.4 6.3 %forward_stage.10 = (bf16[128,1024]{1,0:T(8,128)(2,1)S(1)}, bf16[4,128,1024]{2,1,0:T(8,128)(2,1)}, bf16[4,128,1024]{2,1,0:T(8,128)(2,1)}, bf16[4,128,4096]{2,1,0:T(8,128)(2,1)}, f32[4,128,4096]{2,1,0:T(8,128)}) custom-call(s32[62]{0:T(128)S(1)} %fusion.29.refs_0_.plan_ref.table_base_ref, ...), custom_call_target="tpu_custom_call", output_to_operand_aliasing={{1}: (5, {}), {2}: (6, {}), {3}: (7, {}), {4}: (8, {})} | custom-call | flops 2147483648 | bytes 20971520 | tf_op jit(solution)/shard_map/forward_stage/pallas_call | solution.py:243
  134.0 6.4 %forward_stage.11 = (bf16[128,1024]{1,0:T(8,128)(2,1)S(1)}, bf16[4,128,1024]{2,1,0:T(8,128)(2,1)}, bf16[4,128,1024]{2,1,0:T(8,128)(2,1)}, bf16[4,128,4096]{2,1,0:T(8,128)(2,1)}, f32[4,128,4096]{2,1,0:T(8,128)}) custom-call(s32[62]{0:T(128)S(1)} %fusion.29.refs_0_.plan_ref.table_base_ref, ...), custom_call_target="tpu_custom_call", output_to_operand_aliasing={{1}: (5, {}), {2}: (6, {}), {3}: (7, {}), {4}: (8, {})} | custom-call | flops 2147483648 | bytes 20971520 | tf_op jit(solution)/shard_map/forward_stage/pallas_call | solution.py:243
  149.5 6.4 %forward_stage.12 = (bf16[128,1024]{1,0:T(8,128)(2,1)S(1)}, bf16[4,128,1024]{2,1,0:T(8,128)(2,1)}, bf16[4,128,1024]{2,1,0:T(8,128)(2,1)}, bf16[4,128,4096]{2,1,0:T(8,128)(2,1)}, f32[4,128,4096]{2,1,0:T(8,128)}) custom-call(s32[62]{0:T(128)S(1)} %fusion.29.refs_0_.plan_ref.table_base_ref, ...), custom_call_target="tpu_custom_call", output_to_operand_aliasing={{1}: (7, {}), {2}: (8, {}), {3}: (9, {}), {4}: (10, {})} | custom-call | flops 2147483648 | bytes 20971520 | tf_op jit(solution)/shard_map/forward_stage/pallas_call | solution.py:243
  161.2 6.4 %forward_stage.13 = (bf16[128,1024]{1,0:T(8,128)(2,1)S(1)}, bf16[4,128,1024]{2,1,0:T(8,128)(2,1)}, bf16[4,128,1024]{2,1,0:T(8,128)(2,1)}, bf16[4,128,4096]{2,1,0:T(8,128)(2,1)}, f32[4,128,4096]{2,1,0:T(8,128)}) custom-call(s32[62]{0:T(128)S(1)} %fusion.29.refs_0_.plan_ref.table_base_ref, ...), custom_call_target="tpu_custom_call", output_to_operand_aliasing={{1}: (7, {}), {2}: (8, {}), {3}: (9, {}), {4}: (10, {})} | custom-call | flops 2147483648 | bytes 20971520 | tf_op jit(solution)/shard_map/forward_stage/pallas_call | solution.py:243
  185.4 36.6 %collective-permute-done.27.refs_0_ = bf16[512,256]{1,0:T(8,128)(2,1)S(1)} collective-permute-done((bf16[512,256]{1,0:T(8,128)(2,1)S(1)}, bf16[512,256]{1,0:T(8,128)(2,1)S(1)}, u32[]{:S(2)}, u32[]{:S(2)}) %collective-permute-start.27) | collective-permute-done | bytes 262176 | tf_op jit(solution)/shard_map/ppermute | solution.py:913
  222.0 6.7 %head_stats.1 = (bf16[512,256]{1,0:T(8,128)(2,1)S(1)}, f32[1,512]{1,0:T(1,128)S(1)}, f32[1,512]{1,0:T(1,128)S(1)}) custom-call(s32[62]{0:T(128)S(1)} %fusion.29.refs_0_.plan_ref.table_base_ref, bf16[512,256]{1,0:T(8,128)(2,1)S(1)} %collective-permute-done.27.refs_0_, bf16[512,256]{1,0:T(8,128)(2,1)S(1)} %collective-permute-done.28.refs_1_, ...), custom_call_target="tpu_custom_call" | custom-call | flops 2097152000 | bytes 5242880 | tf_op jit(solution)/shard_map/head_stats/pallas_call | solution.py:498
  228.7 13.2 %all_to_all.21 = f32[4,2,512]{2,1,0:T(2,128)S(1)} all-to-all(f32[4,2,512]{2,1,0:T(2,128)S(1)} %tile.2), channel_id=1, replica_groups=mesh['section'=4,'group'=2,'row'=16] {'section'}, dimensions={0} | all-to-all | bytes 32768 | tf_op jit(solution)/shard_map/all_to_all | solution.py:982
  242.0 11.3 %head_grads.1 = (bf16[16,512,256]{2,1,0:T(8,128)(2,1)}, f32[512,256]{1,0:T(8,128)S(1)}) custom-call(s32[62]{0:T(128)S(1)} %fusion.29.refs_0_.plan_ref.table_base_ref, bf16[512,256]{1,0:T(8,128)(2,1)S(1)} %get-tuple-element.219.readout_ref, bf16[8000,256]{1,0:T(8,128)(2,1)} %table_ref.1, f32[1,512]{1,0:T(1,128)S(1)} %bitcast.126, s32[1,512]{1,0:T(1,128)S(1)} %bitcast.124), custom_call_target="tpu_custom_call" | custom-call | flops 6291456000 | bytes 9437184 | tf_op jit(solution)/shard_map/head_grads/pallas_call | solution.py:543
  257.6 4.7 collective-permute-done.30
  274.1 4.5 backward_stage.13
  283.3 39.3 %collective-permute-done.39.refs_2_ = bf16[128,1024]{1,0:T(8,128)(2,1)S(1)} collective-permute-done((bf16[128,1024]{1,0:T(8,128)(2,1)S(1)}, bf16[128,1024]{1,0:T(8,128)(2,1)S(1)}, u32[]{:S(2)}, u32[]{:S(2)}) %collective-permute-start.39) | collective-permute-done | bytes 262176 | tf_op jit(solution)/shard_map/ppermute | solution.py:913
  324.5 9.2 %backward_stage.16 = (bf16[128,1024]{1,0:T(8,128)(2,1)S(1)}, bf16[4,128,1024]{2,1,0:T(8,128)(2,1)}, bf16[4,128,4096]{2,1,0:T(8,128)(2,1)}, f32[4,8,1024]{2,1,0:T(8,128)}) custom-call(s32[62]{0:T(128)S(1)} %fusion.29.refs_0_.plan_ref.table_base_ref, ...), custom_call_target="tpu_custom_call", output_to_operand_aliasing={{1}: (10, {}), {2}: (11, {}), {3}: (12, {})} | custom-call | flops 2147483648 | bytes 20971520 | tf_op jit(solution)/shard_map/backward_stage/pallas_call | solution.py:427
  336.3 9.2 %backward_stage.17 = (bf16[128,1024]{1,0:T(8,128)(2,1)S(1)}, bf16[4,128,1024]{2,1,0:T(8,128)(2,1)}, bf16[4,128,4096]{2,1,0:T(8,128)(2,1)}, f32[4,8,1024]{2,1,0:T(8,128)}) custom-call(s32[62]{0:T(128)S(1)} %fusion.29.refs_0_.plan_ref.table_base_ref, ...), custom_call_target="tpu_custom_call", output_to_operand_aliasing={{1}: (10, {}), {2}: (11, {}), {3}: (12, {})} | custom-call | flops 2147483648 | bytes 20971520 | tf_op jit(solution)/shard_map/backward_stage/pallas_call | solution.py:427
  348.9 9.2 %backward_stage.18 = (bf16[128,1024]{1,0:T(8,128)(2,1)S(1)}, bf16[4,128,1024]{2,1,0:T(8,128)(2,1)}, bf16[4,128,4096]{2,1,0:T(8,128)(2,1)}, f32[4,8,1024]{2,1,0:T(8,128)}) custom-call(s32[62]{0:T(128)S(1)} %fusion.29.refs_0_.plan_ref.table_base_ref, ...), custom_call_target="tpu_custom_call", output_to_operand_aliasing={{1}: (9, {}), {2}: (10, {}), {3}: (11, {})} | custom-call | flops 2147483648 | bytes 20971520 | tf_op jit(solution)/shard_map/backward_stage/pallas_call | solution.py:427
  359.0 9.2 %backward_stage.19 = (bf16[128,1024]{1,0:T(8,128)(2,1)S(1)}, bf16[4,128,1024]{2,1,0:T(8,128)(2,1)}, bf16[4,128,4096]{2,1,0:T(8,128)(2,1)}, f32[4,8,1024]{2,1,0:T(8,128)}) custom-call(s32[62]{0:T(128)S(1)} %fusion.29.refs_0_.plan_ref.table_base_ref, ...), custom_call_target="tpu_custom_call", output_to_operand_aliasing={{1}: (9, {}), {2}: (10, {}), {3}: (11, {})} | custom-call | flops 2147483648 | bytes 20971520 | tf_op jit(solution)/shard_map/backward_stage/pallas_call | solution.py:427
  375.3 8.0 %lead_grad.3 = bf16[4,256,2048]{2,1,0:T(8,128)(2,1)} custom-call(s32[3]{0:T(128)S(1)} %pad_add_fusion.2.where_ref, bf16[512,1024]{1,0:T(8,128)(2,1)} %bitcast.133, bf16[512,4096]{1,0:T(8,128)(2,1)} %bitcast.129, bf16[512,4096]{1,0:T(8,128)(2,1)} %bitcast.131), custom_call_target="tpu_custom_call" | custom-call | flops 2147483648 | bytes 8388608 | tf_op jit(solution)/shard_map/lead_grad/pallas_call | solution.py:660
  383.3 7.9 %collective-permute-start.49 = (bf16[4,256,2048]{2,1,0:T(8,128)(2,1)}, bf16[4,256,2048]{2,1,0:T(8,128)(2,1)}, u32[]{:S(2)}, u32[]{:S(2)}) collective-permute-start(bf16[4,256,2048]{2,1,0:T(8,128)(2,1)} %lead_grad.3), channel_id=1, source_target_pairs={{0,16},{1,17},{2,18},{3,19},{4,20},{5,21},{6,22},{7,23},{8,24},{9,... | collective-permute-start | bytes 12582920 | tf_op jit(solution)/shard_map/ppermute | solution.py:913
  402.8 5.7 %fusion.16 = (bf16[512,1024]{1,0:T(8,128)(2,1)}, bf16[512,1024]{1,0:T(8,128)(2,1)}, bf16[512,1024]{1,0:T(8,128)(2,1)}, bf16[512,1024]{1,0:T(8,128)(2,1)}) fusion(bf16[4,512,1024]{2,1,0:T(8,128)(2,1)} %collective-permute-done.48, bf16[4,512,1024]{2,1,0:T(8,128)(2,1)} %down_grad.2), kind=kLoop, calls=%fused_computation.33 | loop fusion | flops 8388608 | bytes 12582912 | tf_op jit(solution)/shard_map/convert_element_type | solution.py:950
  408.4 7.1 %lead_grad.2 = bf16[4,256,2048]{2,1,0:T(8,128)(2,1)S(1)} custom-call(s32[3]{0:T(128)S(1)} %pad_add_fusion.1.where_ref, bf16[512,1024]{1,0:T(8,128)(2,1)} %bitcast.134, bf16[512,4096]{1,0:T(8,128)(2,1)} %bitcast.130, bf16[512,4096]{1,0:T(8,128)(2,1)} %bitcast.132), custom_call_target="tpu_custom_call" | custom-call | flops 2147483648 | bytes 8388608 | tf_op jit(solution)/shard_map/lead_grad/pallas_call | solution.py:660
  415.6 4.2 fusion.20
  424.3 4.2 all-to-all-start.1
  429.2 5.4 all-to-all-done.1
  436.0 5.0 all-to-all-start.2
  453.2 4.9 collective-permute-start.51
  464.1 12.0 %collective-permute-done.53 = bf16[256,2048]{1,0:T(8,128)(2,1)} collective-permute-done((bf16[256,2048]{1,0:T(8,128)(2,1)}, bf16[256,2048]{1,0:T(8,128)(2,1)}, u32[]{:S(2)}, u32[]{:S(2)}) %collective-permute-start.53) | collective-permute-done | bytes 1048608 | tf_op jit(solution)/shard_map/ppermute | solution.py:913
  482.8 19.2 %all-to-all-start.3 = ((bf16[4,8,1024]{2,1,0:T(8,128)(2,1)}), bf16[4,8,1024]{2,1,0:T(8,128)(2,1)S(1)}, u32[]{:S(2)}, u32[]{:S(2)}) async-start(bf16[4,8,1024]{2,1,0:T(8,128)(2,1)} %maximum_maximum_fusion.1), calls=%async_computation.3 | async-start | bytes 131072 | tf_op jit(solution)/shard_map/all_to_all | solution.py:982
  507.0 11.4 %embed_sum.1 = f32[64,2000]{1,0:T(8,128)} custom-call(s32[1]{0:T(128)} %bitcast.16.base_ref, bf16[16,80,512]{2,1,0:T(8,128)(2,1)S(1)} %bitcast.120, bf16[16,80,512]{2,1,0:T(8,128)(2,1)S(1)} %collective-permute-done.51.other_ref), custom_call_target="tpu_custom_call" | custom-call | flops 4194304000 | bytes 3145728 | tf_op jit(solution)/shard_map/embed_sum/pallas_call | solution.py:871
  520.3 12.0 %collective-permute-start.59 = (bf16[64,2048]{1,0:T(8,128)(2,1)S(1)}, bf16[64,2048]{1,0:T(8,128)(2,1)S(1)}, u32[]{:S(2)}, u32[]{:S(2)}) collective-permute-start(bf16[64,2048]{1,0:T(8,128)(2,1)S(1)} %add_convert_fusion.12), channel_id=1, source_target_pairs={{0,16},{1,17},{2,18},{3,19},{4,20},{5,21},{6,22},{7,23},{8,24},{9,... | collective-permute-start | bytes 786440 | tf_op jit(solution)/shard_map/ppermute | solution.py:913
  537.9 13.6 %collective-permute-done.67 = bf16[128,1024]{1,0:T(8,128)(2,1)S(1)} collective-permute-done((bf16[128,1024]{1,0:T(8,128)(2,1)S(1)}, bf16[128,1024]{1,0:T(8,128)(2,1)S(1)}, u32[]{:S(2)}, u32[]{:S(2)}) %collective-permute-start.67) | collective-permute-done | bytes 262176 | tf_op jit(solution)/shard_map/ppermute | solution.py:913
  (316 shorter events, 165.1 us)
Async XLA Ops:
  7.2 368.1 %reduce-scatter.4.cloned.1.call-start = ((), (), s32[]{:S(2)}) async-start(), calls=%async_computation.5 | async-start | bytes 4456448
  8.5 18.6 %collective-permute-start.7 = (bf16[256,1024]{1,0:T(8,128)(2,1)S(1)}, bf16[256,1024]{1,0:T(8,128)(2,1)S(1)}, u32[]{:S(2)}, u32[]{:S(2)}) collective-permute-start(bf16[256,1024]{1,0:T(8,128)(2,1)S(1)} %dynamic-slice_bitcast_fusion), channel_id=1, source_target_pairs={{0,32},{1,33},{2,34},{3,35},{4,36},{5,37},{6,38},{7,39},{8,40},{9,... | collective-permute-start | bytes 1572872 | tf_op jit(solution)/shard_map/ppermute | solution.py:913
  12.8 15.9 %collective-permute-start = (bf16[64,1024]{1,0:T(8,128)(2,1)}, bf16[64,1024]{1,0:T(8,128)(2,1)S(1)}, u32[]{:S(2)}, u32[]{:S(2)}) collective-permute-start(bf16[64,1024]{1,0:T(8,128)(2,1)} %param.16), channel_id=1, source_target_pairs={{32,0},{33,1},{34,2},{35,3},{36,4},{37,5},{38,6},{39,7},{40,8},{41... | collective-permute-start | bytes 393224 | tf_op jit(solution)/shard_map/ppermute | solution.py:913
  14.1 16.1 %collective-permute-start.1 = (bf16[64,1024]{1,0:T(8,128)(2,1)}, bf16[64,1024]{1,0:T(8,128)(2,1)S(1)}, u32[]{:S(2)}, u32[]{:S(2)}) collective-permute-start(bf16[64,1024]{1,0:T(8,128)(2,1)} %param.16), channel_id=1, source_target_pairs={{64,0},{65,1},{66,2},{67,3},{68,4},{69,5},{70,6},{71,7},{72,8},{73... | collective-permute-start | bytes 393224 | tf_op jit(solution)/shard_map/ppermute | solution.py:913
  15.3 21.4 %collective-permute-start.2 = (bf16[64,1024]{1,0:T(8,128)(2,1)}, bf16[64,1024]{1,0:T(8,128)(2,1)S(1)}, u32[]{:S(2)}, u32[]{:S(2)}) collective-permute-start(bf16[64,1024]{1,0:T(8,128)(2,1)} %param.16), channel_id=1, source_target_pairs={{96,0},{97,1},{98,2},{99,3},{100,4},{101,5},{102,6},{103,7},{104,8... | collective-permute-start | bytes 393224 | tf_op jit(solution)/shard_map/ppermute | solution.py:913
  27.2 16.2 %collective-permute-start.9 = (bf16[256,1024]{1,0:T(8,128)(2,1)S(1)}, bf16[256,1024]{1,0:T(8,128)(2,1)S(1)}, u32[]{:S(2)}, u32[]{:S(2)}) collective-permute-start(bf16[256,1024]{1,0:T(8,128)(2,1)S(1)} %broadcast_select_fusion.refs_0_), channel_id=1, source_target_pairs={{0,4},{1,5},{2,6},{3,7},{4,8},{5,9},{6,10},{7,11},{8,12},{9,13},{1... | collective-permute-start | bytes 1572872 | tf_op jit(solution)/shard_map/ppermute | solution.py:913
  28.3 15.2 %collective-permute-start.10 = (bf16[256,1024]{1,0:T(8,128)(2,1)S(1)}, bf16[256,1024]{1,0:T(8,128)(2,1)S(1)}, u32[]{:S(2)}, u32[]{:S(2)}) collective-permute-start(bf16[256,1024]{1,0:T(8,128)(2,1)S(1)} %broadcast_select_fusion.refs_0_), channel_id=1, source_target_pairs={{0,8},{1,9},{2,10},{3,11},{4,12},{5,13},{6,14},{7,15},{8,0},{9,1},... | collective-permute-start | bytes 1572872 | tf_op jit(solution)/shard_map/ppermute | solution.py:913
  110.5 33.6 %collective-permute-start.12 = (bf16[1024,1024]{1,0:T(8,128)(2,1)}, bf16[1024,1024]{1,0:T(8,128)(2,1)S(1)}, u32[]{:S(2)}, u32[]{:S(2)}) collective-permute-start(bf16[1024,1024]{1,0:T(8,128)(2,1)} %upper_half.1.mine_ref), channel_id=1, source_target_pairs={{0,16},{1,17},{2,18},{3,19},{4,20},{5,21},{6,22},{7,23},{8,24},{9,... | collective-permute-start | bytes 6291464 | tf_op jit(solution)/shard_map/ppermute | solution.py:913
  140.4 16.2 %collective-permute-start.13 = (bf16[128,1024]{1,0:T(8,128)(2,1)S(1)}, bf16[128,1024]{1,0:T(8,128)(2,1)S(1)}, u32[]{:S(2)}, u32[]{:S(2)}) collective-permute-start(bf16[128,1024]{1,0:T(8,128)(2,1)S(1)} %get-tuple-element.174), channel_id=1, source_target_pairs={{0,32},{1,33},{2,34},{3,35},{4,36},{5,37},{6,38},{7,39},{8,40},{9,... | collective-permute-start | bytes 786440 | tf_op jit(solution)/shard_map/ppermute | solution.py:913
  159.9 16.9 %collective-permute-start.25 = (bf16[64,1024]{1,0:T(8,128)(2,1)S(1)}, bf16[64,1024]{1,0:T(8,128)(2,1)S(1)}, u32[]{:S(2)}, u32[]{:S(2)}) collective-permute-start(bf16[64,1024]{1,0:T(8,128)(2,1)S(1)} %bitcast.149), channel_id=1, source_target_pairs={{32,96},{33,97},{34,98},{35,99},{36,100},{37,101},{38,102},{39,103... | collective-permute-start | bytes 393224 | tf_op jit(solution)/shard_map/ppermute | solution.py:913
  160.6 18.2 %collective-permute-start.26 = (bf16[64,1024]{1,0:T(8,128)(2,1)S(1)}, bf16[64,1024]{1,0:T(8,128)(2,1)S(1)}, u32[]{:S(2)}, u32[]{:S(2)}) collective-permute-start(bf16[64,1024]{1,0:T(8,128)(2,1)S(1)} %bitcast.150), channel_id=1, source_target_pairs={{64,96},{65,97},{66,98},{67,99},{68,100},{69,101},{70,102},{71,103... | collective-permute-start | bytes 393224 | tf_op jit(solution)/shard_map/ppermute | solution.py:913
  182.7 39.2 %collective-permute-start.27 = (bf16[512,256]{1,0:T(8,128)(2,1)S(1)}, bf16[512,256]{1,0:T(8,128)(2,1)S(1)}, u32[]{:S(2)}, u32[]{:S(2)}) collective-permute-start(bf16[512,256]{1,0:T(8,128)(2,1)S(1)} %convolution_convert_fusion.2.refs_3_), channel_id=1, source_target_pairs={{96,0},{97,1},{98,2},{99,3},{100,4},{101,5},{102,6},{103,7},{104,8... | collective-permute-start | bytes 786440 | tf_op jit(solution)/shard_map/ppermute | solution.py:913
  184.0 37.9 %collective-permute-start.28 = (bf16[512,256]{1,0:T(8,128)(2,1)S(1)}, bf16[512,256]{1,0:T(8,128)(2,1)S(1)}, u32[]{:S(2)}, u32[]{:S(2)}) collective-permute-start(bf16[512,256]{1,0:T(8,128)(2,1)S(1)} %convolution_convert_fusion.2.refs_3_), channel_id=1, source_target_pairs={{96,32},{97,33},{98,34},{99,35},{100,36},{101,37},{102,38},{103,39... | collective-permute-start | bytes 786440 | tf_op jit(solution)/shard_map/ppermute | solution.py:913
  184.7 37.3 %collective-permute-start.29 = (bf16[512,256]{1,0:T(8,128)(2,1)S(1)}, bf16[512,256]{1,0:T(8,128)(2,1)S(1)}, u32[]{:S(2)}, u32[]{:S(2)}) collective-permute-start(bf16[512,256]{1,0:T(8,128)(2,1)S(1)} %convolution_convert_fusion.2.refs_3_), channel_id=1, source_target_pairs={{96,64},{97,65},{98,66},{99,67},{100,68},{101,69},{102,70},{103,71... | collective-permute-start | bytes 786440 | tf_op jit(solution)/shard_map/ppermute | solution.py:913
  280.6 41.9 %collective-permute-start.39 = (bf16[128,1024]{1,0:T(8,128)(2,1)S(1)}, bf16[128,1024]{1,0:T(8,128)(2,1)S(1)}, u32[]{:S(2)}, u32[]{:S(2)}) collective-permute-start(bf16[128,1024]{1,0:T(8,128)(2,1)S(1)} %get-tuple-element.249), channel_id=1, source_target_pairs={{32,0},{33,1},{34,2},{35,3},{36,4},{37,5},{38,6},{39,7},{40,8},{41... | collective-permute-start | bytes 786440 | tf_op jit(solution)/shard_map/ppermute | solution.py:913
  281.9 41.9 %collective-permute-start.38 = (bf16[128,1024]{1,0:T(8,128)(2,1)S(1)}, bf16[128,1024]{1,0:T(8,128)(2,1)S(1)}, u32[]{:S(2)}, u32[]{:S(2)}) collective-permute-start(bf16[128,1024]{1,0:T(8,128)(2,1)S(1)} %get-tuple-element.249), channel_id=1, source_target_pairs={{64,32},{65,33},{66,34},{67,35},{68,36},{69,37},{70,38},{71,39},{7... | collective-permute-start | bytes 786440 | tf_op jit(solution)/shard_map/ppermute | solution.py:913
  370.3 32.5 %collective-permute-start.48 = (bf16[4,512,1024]{2,1,0:T(8,128)(2,1)}, bf16[4,512,1024]{2,1,0:T(8,128)(2,1)}, u32[]{:S(2)}, u32[]{:S(2)}) collective-permute-start(bf16[4,512,1024]{2,1,0:T(8,128)(2,1)} %down_grad.3), channel_id=1, source_target_pairs={{32,48},{33,49},{34,50},{35,51},{36,52},{37,53},{38,54},{39,55},{4... | collective-permute-start | bytes 12582920 | tf_op jit(solution)/shard_map/ppermute | solution.py:913
  383.3 32.3 %collective-permute-start.49 = (bf16[4,256,2048]{2,1,0:T(8,128)(2,1)}, bf16[4,256,2048]{2,1,0:T(8,128)(2,1)}, u32[]{:S(2)}, u32[]{:S(2)}) collective-permute-start(bf16[4,256,2048]{2,1,0:T(8,128)(2,1)} %lead_grad.3), channel_id=1, source_target_pairs={{0,16},{1,17},{2,18},{3,19},{4,20},{5,21},{6,22},{7,23},{8,24},{9,... | collective-permute-start | bytes 12582920 | tf_op jit(solution)/shard_map/ppermute | solution.py:913
  428.5 19.9 %collective-permute-start.60 = (bf16[512,1024]{1,0:T(8,128)(2,1)}, bf16[512,1024]{1,0:T(8,128)(2,1)S(1)}, u32[]{:S(2)}, u32[]{:S(2)}) collective-permute-start(bf16[512,1024]{1,0:T(8,128)(2,1)} %get-tuple-element.308), channel_id=1, source_target_pairs={{32,36},{33,37},{34,38},{35,39},{36,40},{37,41},{38,42},{39,43},{4... | collective-permute-start | bytes 3145736 | tf_op jit(solution)/shard_map/ppermute | solution.py:913
  436.0 16.1 %all-to-all-start.2 = ((bf16[4,352,512]{2,1,0:T(8,128)(2,1)}), bf16[4,352,512]{2,1,0:T(8,128)(2,1)S(1)}, u32[]{:S(2)}, u32[]{:S(2)}) async-start(bf16[4,352,512]{2,1,0:T(8,128)(2,1)} %pad_maximum_fusion), calls=%async_computation.2 | async-start | bytes 2883584 | tf_op jit(solution)/shard_map/all_to_all | solution.py:978
  442.6 15.6 %collective-permute-start.62 = (bf16[512,1024]{1,0:T(8,128)(2,1)}, bf16[512,1024]{1,0:T(8,128)(2,1)}, u32[]{:S(2)}, u32[]{:S(2)}) collective-permute-start(bf16[512,1024]{1,0:T(8,128)(2,1)} %get-tuple-element.307), channel_id=1, source_target_pairs={{32,40},{33,41},{34,42},{35,43},{36,44},{37,45},{38,46},{39,47},{4... | collective-permute-start | bytes 3145736 | tf_op jit(solution)/shard_map/ppermute | solution.py:913
  447.5 28.7 %collective-permute-start.53 = (bf16[256,2048]{1,0:T(8,128)(2,1)}, bf16[256,2048]{1,0:T(8,128)(2,1)}, u32[]{:S(2)}, u32[]{:S(2)}) collective-permute-start(bf16[256,2048]{1,0:T(8,128)(2,1)} %get-tuple-element.304), channel_id=1, source_target_pairs={{0,4},{1,5},{2,6},{3,7},{4,8},{5,9},{6,10},{7,11},{8,12},{9,13},{1... | collective-permute-start | bytes 3145736 | tf_op jit(solution)/shard_map/ppermute | solution.py:913
  448.4 29.2 %collective-permute-start.54 = (bf16[256,2048]{1,0:T(8,128)(2,1)}, bf16[256,2048]{1,0:T(8,128)(2,1)}, u32[]{:S(2)}, u32[]{:S(2)}) collective-permute-start(bf16[256,2048]{1,0:T(8,128)(2,1)} %get-tuple-element.302), channel_id=1, source_target_pairs={{0,12},{1,13},{2,14},{3,15},{4,0},{5,1},{6,2},{7,3},{8,4},{9,5},{1... | collective-permute-start | bytes 3145736 | tf_op jit(solution)/shard_map/ppermute | solution.py:913
  449.2 28.4 %collective-permute-start.55 = (bf16[256,2048]{1,0:T(8,128)(2,1)}, bf16[256,2048]{1,0:T(8,128)(2,1)}, u32[]{:S(2)}, u32[]{:S(2)}) collective-permute-start(bf16[256,2048]{1,0:T(8,128)(2,1)} %get-tuple-element.303), channel_id=1, source_target_pairs={{0,8},{1,9},{2,10},{3,11},{4,12},{5,13},{6,14},{7,15},{8,0},{9,1},... | collective-permute-start | bytes 3145736 | tf_op jit(solution)/shard_map/ppermute | solution.py:913
  453.2 53.8 %collective-permute-start.51 = (bf16[16,80,512]{2,1,0:T(8,128)(2,1)S(1)}, bf16[16,80,512]{2,1,0:T(8,128)(2,1)S(1)}, u32[]{:S(2)}, u32[]{:S(2)}) collective-permute-start(bf16[16,80,512]{2,1,0:T(8,128)(2,1)S(1)} %bitcast.119), channel_id=1, source_target_pairs={{0,16},{1,17},{2,18},{3,19},{4,20},{5,21},{6,22},{7,23},{8,24},{9,... | collective-permute-start | bytes 3932168 | tf_op jit(solution)/shard_map/ppermute | solution.py:913
  461.9 71.7 %collective-permute-start.63 = (bf16[128,1024]{1,0:T(8,128)(2,1)}, bf16[128,1024]{1,0:T(8,128)(2,1)}, u32[]{:S(2)}, u32[]{:S(2)}) collective-permute-start(bf16[128,1024]{1,0:T(8,128)(2,1)} %get-tuple-element.312), channel_id=1, source_target_pairs={{32,33},{33,34},{34,35},{35,32},{36,37},{37,38},{38,39},{39,36},{4... | collective-permute-start | bytes 786440 | tf_op jit(solution)/shard_map/ppermute | solution.py:913
  476.2 57.4 %collective-permute-start.64 = (bf16[128,1024]{1,0:T(8,128)(2,1)}, bf16[128,1024]{1,0:T(8,128)(2,1)}, u32[]{:S(2)}, u32[]{:S(2)}) collective-permute-start(bf16[128,1024]{1,0:T(8,128)(2,1)} %get-tuple-element.311), channel_id=1, source_target_pairs={{32,35},{33,32},{34,33},{35,34},{36,39},{37,36},{38,37},{39,38},{4... | collective-permute-start | bytes 786440 | tf_op jit(solution)/shard_map/ppermute | solution.py:913
  482.8 23.6 %all-to-all-start.3 = ((bf16[4,8,1024]{2,1,0:T(8,128)(2,1)}), bf16[4,8,1024]{2,1,0:T(8,128)(2,1)S(1)}, u32[]{:S(2)}, u32[]{:S(2)}) async-start(bf16[4,8,1024]{2,1,0:T(8,128)(2,1)} %maximum_maximum_fusion.1), calls=%async_computation.3 | async-start | bytes 131072 | tf_op jit(solution)/shard_map/all_to_all | solution.py:982
  504.0 15.1 %collective-permute-start.57 = (bf16[64,2048]{1,0:T(8,128)(2,1)}, bf16[64,2048]{1,0:T(8,128)(2,1)}, u32[]{:S(2)}, u32[]{:S(2)}) collective-permute-start(bf16[64,2048]{1,0:T(8,128)(2,1)} %get-tuple-element.315), channel_id=1, source_target_pairs={{0,3},{1,0},{2,1},{3,2},{4,7},{5,4},{6,5},{7,6},{8,11},{9,8},{10,9... | collective-permute-start | bytes 786440 | tf_op jit(solution)/shard_map/ppermute | solution.py:913
  518.4 15.1 %collective-permute-start.65 = (bf16[128,1024]{1,0:T(8,128)(2,1)S(1)}, bf16[128,1024]{1,0:T(8,128)(2,1)S(1)}, u32[]{:S(2)}, u32[]{:S(2)}) collective-permute-start(bf16[128,1024]{1,0:T(8,128)(2,1)S(1)} %get-tuple-element.310), channel_id=1, source_target_pairs={{32,34},{33,35},{34,32},{35,33},{36,38},{37,39},{38,36},{39,37},{4... | collective-permute-start | bytes 786440 | tf_op jit(solution)/shard_map/ppermute | solution.py:913
  520.3 16.5 %collective-permute-start.59 = (bf16[64,2048]{1,0:T(8,128)(2,1)S(1)}, bf16[64,2048]{1,0:T(8,128)(2,1)S(1)}, u32[]{:S(2)}, u32[]{:S(2)}) collective-permute-start(bf16[64,2048]{1,0:T(8,128)(2,1)S(1)} %add_convert_fusion.12), channel_id=1, source_target_pairs={{0,16},{1,17},{2,18},{3,19},{4,20},{5,21},{6,22},{7,23},{8,24},{9,... | collective-permute-start | bytes 786440 | tf_op jit(solution)/shard_map/ppermute | solution.py:913
  535.5 16.0 %collective-permute-start.67 = (bf16[128,1024]{1,0:T(8,128)(2,1)S(1)}, bf16[128,1024]{1,0:T(8,128)(2,1)S(1)}, u32[]{:S(2)}, u32[]{:S(2)}) collective-permute-start(bf16[128,1024]{1,0:T(8,128)(2,1)S(1)} %add_convert_fusion.11), channel_id=1, source_target_pairs={{32,16},{33,17},{34,18},{35,19},{36,20},{37,21},{38,22},{39,23},{4... | collective-permute-start | bytes 786440 | tf_op jit(solution)/shard_map/ppermute | solution.py:913
  (74 other events, 567.5 us)
Sparse Core Ops, SparseCore 0:
  253.5 76.4 reduce-scatter.3
